TPU v7x, 32 devices: a whole 2x2x4 slice. The times are simulated.
32 devices in a mesh: dp: 16 (over z, y, x), blk: 2 (over core).
Axes of the slice: x: 2, y: 2, z: 4, core: 2. Of those that a mesh axis runs over, the one named last changes fastest.
Arguments:
- tokens: bfloat16 [16, 512, 1024], P('dp', 'blk'), may hold values from -6 to 6
- doc_lengths: int32 [16, 8], P('dp'), may hold values from 0 to 512, as said below
- cotangent: bfloat16 [16, 512, 1024], P('dp', 'blk'), may hold values from -6 to 6
- w_qkv: bfloat16 [1024, 3072], P('dp'), may hold values from -0.1875 to 0.1875
- qv_bias: bfloat16 [2048], P('dp'), may hold values from -1.25 to 1.25
- w_out: bfloat16 [1024, 1024], P('dp'), may hold values from -0.5 to 0.5
- out_bias: bfloat16 [1024], P('dp'), may hold values from -1.25 to 1.25
- w_up: bfloat16 [1024, 4096], P('dp'), may hold values from -0.1875 to 0.1875
- up_bias: bfloat16 [4096], P('dp'), may hold values from -1.25 to 1.25
- w_down: bfloat16 [4096, 1024], P('dp'), may hold values from -0.09375 to 0.09375
- down_bias: bfloat16 [1024], P('dp'), may hold values from -1.25 to 1.25
- norm_gain: bfloat16 [4, 1024], P(None, 'dp'), may hold values from 0.5 to 1.5
- norm_bias: bfloat16 [4, 1024], P(None, 'dp'), may hold values from -1.25 to 1.25
Outputs:
- layer_out: bfloat16 [16, 512, 1024], P('dp', 'blk')
- grad_tokens: float32 [16, 512, 1024], P('dp', 'blk')
- grad_w_qkv: float32 [1024, 3072], P('dp')
- grad_qv_bias: float32 [2048], P('dp')
- grad_w_out: float32 [1024, 1024], P('dp')
- grad_out_bias: float32 [1024], P('dp')
- grad_w_up: float32 [1024, 4096], P('dp')
- grad_up_bias: float32 [4096], P('dp')
- grad_w_down: float32 [4096, 1024], P('dp')
- grad_down_bias: float32 [1024], P('dp')
- grad_norm_gain: float32 [4, 1024], P(None, 'dp')
- grad_norm_bias: float32 [4, 1024], P(None, 'dp')
Inputs may be any that keep to these rules, and one draw needn't show every extreme that they name: `doc_lengths`: in each row the lengths sum to at most 512; slots past the sum are padding, and unused document slots hold 0. Every row holds one document that starts within its first 256 slots and ends within its last 256.
All inputs are finite; a program needn't handle non-finite values.
Results may differ from a plain program's by a relative error of at most 0.015.
Values may be sent and summed in bfloat16 or wider, within the bound.
A program may use at most 192 MiB of HBM per device.

v0:
```python
import math

import jax
import jax.numpy as jnp
from jax import lax
from jax.sharding import PartitionSpec as P

HEADS = 16
ALPHA = 32


EPSILON = 1e-05
FILLER = -1000000000.0


def normalize(values):
    center = values - jnp.mean(values, axis=-1, keepdims=True)
    inverse = lax.rsqrt(jnp.mean(center * center, axis=-1, keepdims=True) + EPSILON)
    return (center * inverse, inverse)


def norm_back(normed, inverse, gain_row, upstream):
    scaled = upstream * gain_row
    return inverse * (
        scaled
        - jnp.mean(scaled, axis=-1, keepdims=True)
        - normed * jnp.mean(scaled * normed, axis=-1, keepdims=True)
    )


def segment_of(position, doc_ends):
    return jnp.sum((position[:, None] >= doc_ends[None, :]).astype(jnp.int32), axis=1)


def gelu_tanh(values):
    return jax.nn.gelu(values, approximate=True)


def shards(
    tokens,
    doc_lengths,
    cotangent,
    w_qkv,
    qv_bias,
    w_out,
    out_bias,
    w_up,
    up_bias,
    w_down,
    down_bias,
    norm_gain,
    norm_bias,
):
    inputs = tokens[0].astype(jnp.float32)
    length = inputs.shape[0]
    model_width = inputs.shape[1]
    block_count = lax.axis_size("blk")
    seq_len = length * block_count
    offset = lax.axis_index("blk") * length
    doc_ends = jnp.cumsum(doc_lengths[0])
    filled = doc_ends[-1]
    query_pos = offset + jnp.arange(length, dtype=jnp.int32)
    query_seg = segment_of(query_pos, doc_ends)
    valid_rows = (query_pos < filled).astype(jnp.float32)
    key_seg = segment_of(jnp.arange(seq_len, dtype=jnp.int32), doc_ends)
    last_query = offset + length - 1

    def block_meets(first_row, piece_rows):
        first_at = jnp.asarray(first_row, jnp.int32)
        first_seg = lax.dynamic_index_in_dim(key_seg, first_at, keepdims=False)
        last_seg = lax.dynamic_index_in_dim(key_seg, first_at + piece_rows - 1, keepdims=False)
        return (first_at <= last_query) & (first_seg <= query_seg[-1]) & (last_seg >= query_seg[0])

    gathered = (
        lax.all_gather(w_qkv, "dp", axis=0, tiled=True),
        lax.all_gather(qv_bias, "dp", axis=0, tiled=True),
        lax.all_gather(w_out, "dp", axis=0, tiled=True),
        lax.all_gather(out_bias, "dp", axis=0, tiled=True),
        lax.all_gather(w_up, "dp", axis=0, tiled=True),
        lax.all_gather(up_bias, "dp", axis=0, tiled=True),
        lax.all_gather(w_down, "dp", axis=0, tiled=True),
        lax.all_gather(down_bias, "dp", axis=0, tiled=True),
        lax.all_gather(norm_gain, "dp", axis=1, tiled=True),
        lax.all_gather(norm_bias, "dp", axis=1, tiled=True),
    )
    (
        qkv_weight,
        qv_shift,
        out_weight,
        out_shift,
        up_weight,
        up_shift,
        down_weight,
        down_shift,
        gain_all,
        shift_all,
    ) = gathered
    gain_rows = gain_all.astype(jnp.float32)
    shift_rows = shift_all.astype(jnp.float32)
    query_scale = 1.0 / (ALPHA * math.sqrt(model_width // HEADS))
    first_hat, first_inv = normalize(inputs)
    attn_in = (first_hat * gain_rows[0] + shift_rows[0]).astype(jnp.bfloat16)
    projected = jnp.dot(attn_in, qkv_weight, preferred_element_type=jnp.float32)
    qv_float = qv_shift.astype(jnp.float32)
    queries = ((projected[:, :model_width] + qv_float[:model_width]) * query_scale).astype(
        jnp.bfloat16
    )
    keys_own = projected[:, model_width : 2 * model_width].astype(jnp.bfloat16)
    values_own = (projected[:, 2 * model_width :] + qv_float[model_width:]).astype(jnp.bfloat16)
    query_heads = queries.reshape(length, HEADS, -1)

    def scores_of(key_piece, first_row):
        piece_rows = key_piece.shape[0]
        piece_pos = first_row + jnp.arange(piece_rows, dtype=jnp.int32)
        piece_seg = lax.dynamic_slice_in_dim(key_seg, jnp.asarray(first_row, jnp.int32), piece_rows)
        allowed_pairs = (query_seg[:, None] == piece_seg[None, :]) & (
            piece_pos[None, :] <= query_pos[:, None]
        )
        raw_scores = jnp.einsum(
            "qhd,khd->hqk",
            query_heads,
            key_piece.reshape(piece_rows, HEADS, -1),
            preferred_element_type=jnp.float32,
        )
        return (jnp.where(allowed_pairs[None], raw_scores, FILLER), allowed_pairs[None])

    head_dim = model_width // HEADS
    start_state = (
        jnp.full((HEADS, length), FILLER, jnp.float32),
        jnp.zeros((HEADS, length), jnp.float32),
        jnp.zeros((HEADS, length, head_dim), jnp.float32),
    )
    accumulate_first_row = jnp.int32(0)
    accumulate_key_piece = lax.all_gather(keys_own, "blk", axis=0, tiled=True)
    accumulate_value_piece = lax.all_gather(values_own, "blk", axis=0, tiled=True)
    piece_rows = accumulate_value_piece.shape[0]

    def update(state):
        row_top, row_total, summed = state
        masked, allowed_pairs = scores_of(accumulate_key_piece, accumulate_first_row)
        new_top = jnp.maximum(row_top, jnp.max(masked, axis=2))
        factor = jnp.exp(ALPHA * (row_top - new_top))
        weights = jnp.where(allowed_pairs, jnp.exp(ALPHA * (masked - new_top[:, :, None])), 0.0)
        summed = summed * factor[:, :, None] + jnp.einsum(
            "hqk,khd->hqd",
            weights,
            accumulate_value_piece.reshape(piece_rows, HEADS, -1),
            preferred_element_type=jnp.float32,
        )
        return (new_top, row_total * factor + jnp.sum(weights, axis=2), summed)

    def unchanged(state):
        return state

    softmax_state = lax.cond(
        block_meets(accumulate_first_row, piece_rows), update, unchanged, start_state
    )
    row_top, row_total, summed = softmax_state
    attended_heads = summed / row_total[:, :, None]
    attended = jnp.transpose(attended_heads, (1, 0, 2)).reshape(length, model_width)
    attn_low = attended.astype(jnp.bfloat16)
    branch = jnp.dot(attn_low, out_weight, preferred_element_type=jnp.float32) + out_shift.astype(
        jnp.float32
    )
    second_hat, second_inv = normalize(branch)
    middle = inputs + second_hat * gain_rows[1] + shift_rows[1]
    third_hat, third_inv = normalize(middle)
    ffn_in = (third_hat * gain_rows[2] + shift_rows[2]).astype(jnp.bfloat16)
    pre_act = jnp.dot(ffn_in, up_weight, preferred_element_type=jnp.float32) + up_shift.astype(
        jnp.float32
    )
    activated, gelu_pullback = jax.vjp(gelu_tanh, pre_act)
    act_low = activated.astype(jnp.bfloat16)
    ffn_out = jnp.dot(act_low, down_weight, preferred_element_type=jnp.float32) + down_shift.astype(
        jnp.float32
    )
    fourth_hat, fourth_inv = normalize(ffn_out)
    result = middle + fourth_hat * gain_rows[3] + shift_rows[3]
    qkv_again, out_again, up_again, down_again, gain_again = (
        lax.all_gather(w_qkv, "dp", axis=0, tiled=True),
        lax.all_gather(w_out, "dp", axis=0, tiled=True),
        lax.all_gather(w_up, "dp", axis=0, tiled=True),
        lax.all_gather(w_down, "dp", axis=0, tiled=True),
        lax.all_gather(norm_gain, "dp", axis=1, tiled=True),
    )
    back_gains = gain_again.astype(jnp.float32)
    upstream = cotangent[0].astype(jnp.float32) * valid_rows[:, None]
    grad_ffn = norm_back(fourth_hat, fourth_inv, back_gains[3], upstream).astype(jnp.bfloat16)
    grad_down = jnp.einsum("tf,td->fd", act_low, grad_ffn, preferred_element_type=jnp.float32)
    grad_act = jnp.einsum("td,fd->tf", grad_ffn, down_again, preferred_element_type=jnp.float32)
    grad_pre = gelu_pullback(grad_act)[0].astype(jnp.bfloat16)
    grad_up = jnp.einsum("td,tf->df", ffn_in, grad_pre, preferred_element_type=jnp.float32)
    grad_ffn_in = jnp.einsum("tf,df->td", grad_pre, up_again, preferred_element_type=jnp.float32)
    grad_middle = upstream + norm_back(third_hat, third_inv, back_gains[2], grad_ffn_in)
    grad_branch = norm_back(second_hat, second_inv, back_gains[1], grad_middle).astype(jnp.bfloat16)
    grad_out = jnp.einsum("td,te->de", attn_low, grad_branch, preferred_element_type=jnp.float32)
    grad_attn = jnp.einsum(
        "te,de->td", grad_branch, out_again, preferred_element_type=jnp.float32
    ).astype(jnp.bfloat16)
    grad_heads = grad_attn.reshape(length, HEADS, -1)
    row_delta = jnp.einsum(
        "qhd,hqd->hq", grad_heads, attended_heads, preferred_element_type=jnp.float32
    )
    keys_all, values_all = (
        lax.all_gather(keys_own, "blk", axis=0, tiled=True),
        lax.all_gather(values_own, "blk", axis=0, tiled=True),
    )
    grad_query = jnp.zeros((length, HEADS, head_dim), jnp.float32)
    key_terms = []
    for block_index in range(block_count):
        first_row = block_index * length
        key_piece = keys_all[first_row : first_row + length]
        value_piece = values_all[first_row : first_row + length]

        def block_grads(operands):
            key_block, value_block = operands
            value_heads = value_block.reshape(length, HEADS, -1)
            masked, allowed_pairs = scores_of(key_block, first_row)
            probabilities = (
                jnp.where(allowed_pairs, jnp.exp(ALPHA * (masked - row_top[:, :, None])), 0.0)
                / row_total[:, :, None]
            )
            grad_probs = jnp.einsum(
                "qhd,khd->hqk", grad_heads, value_heads, preferred_element_type=jnp.float32
            )
            grad_scores = ALPHA * probabilities * (grad_probs - row_delta[:, :, None])
            query_term = jnp.einsum(
                "hqk,khd->qhd",
                grad_scores,
                key_block.reshape(length, HEADS, -1),
                preferred_element_type=jnp.float32,
            )
            grad_key = jnp.einsum(
                "hqk,qhd->khd", grad_scores, query_heads, preferred_element_type=jnp.float32
            )
            grad_value = jnp.einsum(
                "hqk,qhd->khd", probabilities, grad_heads, preferred_element_type=jnp.float32
            )
            return (
                query_term,
                jnp.concatenate(
                    [
                        grad_key.reshape(length, model_width),
                        grad_value.reshape(length, model_width),
                    ],
                    1,
                ),
            )

        def block_zeros(operands):
            return (
                jnp.zeros((length, HEADS, head_dim), jnp.float32),
                jnp.zeros((length, 2 * model_width), jnp.float32),
            )

        query_term, key_term = lax.cond(
            block_meets(first_row, length), block_grads, block_zeros, (key_piece, value_piece)
        )
        grad_query = grad_query + query_term
        key_terms.append(key_term)
    key_grads = lax.psum_scatter(
        jnp.concatenate(key_terms, 0).astype(jnp.bfloat16), "blk", scatter_dimension=0, tiled=True
    ).astype(jnp.float32)
    grad_keys = key_grads[:, :model_width].astype(jnp.bfloat16)
    grad_values = key_grads[:, model_width:].astype(jnp.bfloat16)
    grad_queries = grad_query.reshape(length, model_width).astype(jnp.bfloat16) * jnp.asarray(
        query_scale, jnp.bfloat16
    )
    grad_projected = jnp.concatenate([grad_queries, grad_keys, grad_values], 1)
    grad_qkv = jnp.einsum("td,te->de", attn_in, grad_projected, preferred_element_type=jnp.float32)
    grad_qv = jnp.concatenate(
        [
            jnp.sum(grad_queries.astype(jnp.float32), axis=0),
            jnp.sum(grad_values.astype(jnp.float32), axis=0),
        ]
    )
    grad_attn_in = jnp.einsum(
        "te,de->td", grad_projected, qkv_again, preferred_element_type=jnp.float32
    )
    grad_inputs = grad_middle + norm_back(first_hat, first_inv, back_gains[0], grad_attn_in)
    grad_gains = jnp.stack(
        [
            jnp.sum(grad_attn_in * first_hat, axis=0),
            jnp.sum(grad_middle * second_hat, axis=0),
            jnp.sum(grad_ffn_in * third_hat, axis=0),
            jnp.sum(upstream * fourth_hat, axis=0),
        ]
    )
    grad_shifts = jnp.stack(
        [
            jnp.sum(grad_attn_in, axis=0),
            jnp.sum(grad_middle, axis=0),
            jnp.sum(grad_ffn_in, axis=0),
            jnp.sum(upstream, axis=0),
        ]
    )
    grad_out_shift = jnp.sum(grad_branch.astype(jnp.float32), axis=0)
    grad_up_shift = jnp.sum(grad_pre.astype(jnp.float32), axis=0)
    grad_down_shift = jnp.sum(grad_ffn.astype(jnp.float32), axis=0)
    shares = (
        lax.psum_scatter(grad_qkv, "dp", scatter_dimension=0, tiled=True),
        lax.psum_scatter(grad_qv, "dp", scatter_dimension=0, tiled=True),
        lax.psum_scatter(grad_out, "dp", scatter_dimension=0, tiled=True),
        lax.psum_scatter(grad_out_shift, "dp", scatter_dimension=0, tiled=True),
        lax.psum_scatter(grad_up, "dp", scatter_dimension=0, tiled=True),
        lax.psum_scatter(grad_up_shift, "dp", scatter_dimension=0, tiled=True),
        lax.psum_scatter(grad_down, "dp", scatter_dimension=0, tiled=True),
        lax.psum_scatter(grad_down_shift, "dp", scatter_dimension=0, tiled=True),
        lax.psum_scatter(grad_gains, "dp", scatter_dimension=1, tiled=True),
        lax.psum_scatter(grad_shifts, "dp", scatter_dimension=1, tiled=True),
    )
    totals = (
        lax.psum(shares[0].astype(jnp.bfloat16), "blk").astype(jnp.float32),
        lax.psum(shares[1].astype(jnp.bfloat16), "blk").astype(jnp.float32),
        lax.psum(shares[2].astype(jnp.bfloat16), "blk").astype(jnp.float32),
        lax.psum(shares[3].astype(jnp.bfloat16), "blk").astype(jnp.float32),
        lax.psum(shares[4].astype(jnp.bfloat16), "blk").astype(jnp.float32),
        lax.psum(shares[5].astype(jnp.bfloat16), "blk").astype(jnp.float32),
        lax.psum(shares[6].astype(jnp.bfloat16), "blk").astype(jnp.float32),
        lax.psum(shares[7].astype(jnp.bfloat16), "blk").astype(jnp.float32),
        lax.psum(shares[8].astype(jnp.bfloat16), "blk").astype(jnp.float32),
        lax.psum(shares[9].astype(jnp.bfloat16), "blk").astype(jnp.float32),
    )
    return (result.astype(jnp.bfloat16)[None], grad_inputs[None]) + tuple(totals)


def solution(mesh):
    placed = (
        P("dp", "blk", None),
        P("dp", None),
        P("dp", "blk", None),
        P("dp", None),
        P("dp"),
        P("dp", None),
        P("dp"),
        P("dp", None),
        P("dp"),
        P("dp", None),
        P("dp"),
        P(None, "dp"),
        P(None, "dp"),
    )
    return jax.shard_map(
        shards,
        mesh=mesh,
        in_specs=placed,
        out_specs=(
            P("dp", "blk", None),
            P("dp", "blk", None),
            P("dp", None),
            P("dp"),
            P("dp", None),
            P("dp"),
            P("dp", None),
            P("dp"),
            P("dp", None),
            P("dp"),
            P(None, "dp"),
            P(None, "dp"),
        ),
        check_vma=False,
    )
```

profile of v0, /device:TPU:1, one launch (start us, length us, event | category | flops | bytes accessed | tf_op | source)
XLA Modules:
  0.0 1713.7 jit_solution(3798090056790817167)
XLA Ops:
  8.0 34.8 %all-gather = bf16[16,64,4]{1,2,0:T(4,128)(2,1)S(1)} all-gather(bf16[1,64,4]{1,2,0:T(4,128)(2,1)} %bitcast.228), channel_id=1, replica_groups=mesh['dp'=16,'blk'=2] {'dp'}, dimensions={0}, use_global_device_ids=true | all-gather | bytes 8704 | tf_op jit(solution)/shard_map/all_gather | solution.py:83
  42.9 29.1 %all-gather.1 = bf16[16,64,4]{1,2,0:T(4,128)(2,1)S(1)} all-gather(bf16[1,64,4]{1,2,0:T(4,128)(2,1)} %bitcast.229), channel_id=1, replica_groups=mesh['dp'=16,'blk'=2] {'dp'}, dimensions={0}, use_global_device_ids=true | all-gather | bytes 8704 | tf_op jit(solution)/shard_map/all_gather | solution.py:84
  72.0 30.5 %all-gather.2 = bf16[16,1,128]{2,1,0:T(2,128)(2,1)S(1)} all-gather(bf16[1,1,128]{2,1,0:T(2,128)(2,1)} %bitcast.230), channel_id=1, replica_groups=mesh['dp'=16,'blk'=2] {'dp'}, dimensions={0}, use_global_device_ids=true | all-gather | bytes 4352 | tf_op jit(solution)/shard_map/all_gather | solution.py:76
  106.4 4.9 fusion.63
  114.1 2.1 slice.132
  120.5 33.2 %all-reduce.7 = (bf16[1024]{0:T(1024)(128)(2,1)S(1)}, bf16[1024]{0:T(1024)(128)(2,1)S(1)}) all-reduce(bf16[1024]{0:T(1024)(128)(2,1)S(1)} %dynamic-update-slice, bf16[1024]{0:T(1024)(128)(2,1)S(1)} %dynamic-update-slice.1), channel_id=1, replica_groups=mesh['dp'=16,'blk'=2] {'dp'}, use_global_device_ids=true, to_apply=%add | all-reduce | flops 2048 | bytes 8192
  159.7 28.6 %all-gather.3 = bf16[16,1,256]{2,1,0:T(2,128)(2,1)S(1)} all-gather(bf16[1,1,256]{2,1,0:T(2,128)(2,1)S(1)} %reshape.359), channel_id=1, replica_groups=mesh['dp'=16,'blk'=2] {'dp'}, dimensions={0}, use_global_device_ids=true | all-gather | bytes 8704 | tf_op jit(solution)/shard_map/all_gather | solution.py:80
  189.9 13.5 conditional.3
  193.1 2.5 select_reduce_fusion
  196.2 2.9 fusion.7
  199.1 3.3 fusion.1
  203.6 12.2 all-gather.17.cloned.1.call-done
  215.7 2.4 fusion.79
  219.1 110.8 %all-gather.19.cloned.1.call-done = bf16[1024,4096]{1,0:T(8,128)(2,1)} async-done(((bf16[64,4096]{1,0:T(8,128)(2,1)}), bf16[1024,4096]{1,0:T(8,128)(2,1)}) %all-gather.19.cloned.1.call-update) | async-done | bytes 8388624 | tf_op jit(solution)/shard_map/all_gather | solution.py:79
  329.9 7.8 convolution_add_fusion
  337.7 105.9 %all-gather.21.cloned.1.call-done = bf16[4096,1024]{1,0:T(8,128)(2,1)} async-done(((bf16[256,1024]{1,0:T(8,128)(2,1)}), bf16[4096,1024]{1,0:T(8,128)(2,1)}) %all-gather.21.cloned.1.call-update) | async-done | bytes 8388624 | tf_op jit(solution)/shard_map/all_gather | solution.py:81
  443.6 7.6 fusion.80
  453.4 5.5 convert_reduce_fusion
  459.0 2.7 multiply_reduce_fusion
  468.2 14.8 conditional.5
  469.8 2.3 copy.74
  473.1 3.5 select_divide_fusion.1
  483.1 13.2 conditional.4
  486.1 3.5 select_divide_fusion
  493.3 1.7 convolution_bitcast_fusion
  496.3 3.1 pad_maximum_fusion
  499.5 2.7 fusion.85
  502.3 1.8 convert_reduce_fusion.5
  504.1 4.1 reduce-scatter.12.cloned.1.call-done
  508.2 7.8 fusion.55
  517.0 10.9 fusion.66
  527.9 9.8 fusion.65
  539.0 5.8 fusion.36
  547.1 58.6 %reduce-scatter.16.cloned.1.call-done = f32[64,1024]{1,0:T(8,128)} async-done(((f32[1024,1024]{1,0:T(8,128)}), f32[64,1024]{1,0:T(8,128)}) %reduce-scatter.16.cloned.1.call-update) | async-done | bytes 262160 | tf_op jit(solution)/shard_map/reduce_scatter | solution.py:303
  607.3 209.3 %reduce-scatter.14.cloned.1.call-done = f32[64,3072]{1,0:T(8,128)} async-done(((f32[1024,3072]{1,0:T(8,128)}), f32[64,3072]{1,0:T(8,128)}) %reduce-scatter.14.cloned.1.call-update) | async-done | bytes 786448 | tf_op jit(solution)/shard_map/reduce_scatter | solution.py:301
  816.6 1.9 convert_element_type.208
  818.6 346.4 %reduce-scatter.20.cloned.1.call-done = f32[256,1024]{1,0:T(8,128)} async-done(((f32[4096,1024]{1,0:T(8,128)}), f32[256,1024]{1,0:T(8,128)}) %reduce-scatter.20.cloned.1.call-update) | async-done | bytes 1048592 | tf_op jit(solution)/shard_map/reduce_scatter | solution.py:307
  1165.0 2.1 convert_element_type.224
  1167.1 352.3 %reduce-scatter.18.cloned.1.call-done = f32[64,4096]{1,0:T(8,128)} async-done(((f32[1024,4096]{1,0:T(8,128)}), f32[64,4096]{1,0:T(8,128)}) %reduce-scatter.18.cloned.1.call-update) | async-done | bytes 1048592 | tf_op jit(solution)/shard_map/reduce_scatter | solution.py:305
  1519.4 2.1 convert_element_type.219
  1523.7 66.1 %all-reduce.6 = (bf16[2048]{0:T(1024)(128)(2,1)S(1)}, bf16[1024]{0:T(1024)(128)(2,1)S(1)}, bf16[4096]{0:T(1024)(128)(2,1)S(1)}, bf16[1024]{0:T(1024)(128)(2,1)S(1)}) all-reduce(f32[2048]{0:T(1024)S(1)} %pad_maximum_fusion.6, f32[1024]{0:T(1024)S(1)} %get-tuple-element.278, ...), channel_id=4, replica_groups=mesh['dp'=16,'blk'=2] {'dp'}, use_global_device_ids=true, to_apply=%region_32.33.clone | all-reduce | flops 8192 | bytes 49152
  1590.1 2.6 fusion.35
  1593.5 74.3 %reduce-scatter.22.cloned.1.call-done = f32[64,4]{1,0:T(8,128)} async-done(((f32[1024,4]{1,0:T(8,128)}), f32[64,4]{1,0:T(8,128)}) %reduce-scatter.22.cloned.1.call-update) | async-done | bytes 1040
  1668.6 14.0 all-reduce.8
  1685.9 13.3 all-reduce.12.cloned.1.call-done
  1700.9 1.9 convert_element_type.209
  1702.8 2.1 convert_element_type.220
  1704.9 2.1 convert_element_type.225
  (187 shorter events, 58.0 us)
Async XLA Ops:
  7.2 99.2 %all-gather.11.cloned.1.call-start = ((), (), s32[]{:S(2)}) async-start(), calls=%async_computation.7 | async-start | bytes 6684672 | tf_op jit(solution)/shard_map/all_gather | solution.py:75
  7.9 182.0 %all-gather.15.cloned.1.call-start = ((), (), s32[]{:S(2)}) async-start(), calls=%async_computation.9 | async-start | bytes 1572864 | tf_op jit(solution)/shard_map/all_gather | solution.py:135
  111.3 1.7 copy-start.10
  111.3 6.7 copy-start.19
  111.3 7.5 copy-start.20
  111.3 7.5 copy-start.17
  111.3 8.7 copy-start.21
  111.3 9.0 copy-start.22
  114.0 75.9 %all-gather.13.cloned.1.call-start = ((), (), s32[]{:S(2)}) async-start(), calls=%async_computation.8 | async-start | bytes 1572864 | tf_op jit(solution)/shard_map/all_gather | solution.py:134
  116.2 99.5 %all-gather.17.cloned.1.call-start = ((), (), s32[]{:S(2)}) async-start(), calls=%async_computation.10 | async-start | bytes 2228224 | tf_op jit(solution)/shard_map/all_gather | solution.py:77
  116.8 213.1 %all-gather.19.cloned.1.call-start = ((), (), s32[]{:S(2)}) async-start(), calls=%async_computation.11 | async-start | bytes 8912896 | tf_op jit(solution)/shard_map/all_gather | solution.py:79
  117.4 326.2 %all-gather.21.cloned.1.call-start = ((), (), s32[]{:S(2)}) async-start(), calls=%async_computation.12 | async-start | bytes 8912896 | tf_op jit(solution)/shard_map/all_gather | solution.py:81
  117.9 390.2 %reduce-scatter.12.cloned.1.call-start = ((), (), s32[]{:S(2)}) async-start(), calls=%async_computation.13 | async-start | bytes 3145728 | tf_op jit(solution)/shard_map/reduce_scatter | solution.py:261
  203.4 15.0 copy-start.4
  203.4 15.0 copy-start
  203.5 15.6 copy-start.5
  337.7 113.8 %copy-start.8 = (bf16[1,256,1024]{2,1,0:T(8,128)(2,1)S(1)}, bf16[1,256,1024]{2,1,0:T(8,128)(2,1)}, u32[]{:S(2)}) copy-start(bf16[1,256,1024]{2,1,0:T(8,128)(2,1)} %param.21) | copy-start | bytes 1572868
  443.6 9.9 copy-start.18
  451.2 2.3 copy-start.7
  452.1 6.9 slice-start.2
  453.4 5.5 copy-start.14
  453.4 5.5 slice-start.3
  458.9 2.7 copy-start.16
  461.7 2.3 copy-start.13
  462.8 1.0 copy-start.1
  463.2 0.8 copy-start.11
  463.2 5.0 copy-start.3
  476.6 1.0 slice-start
  489.6 1.0 slice-start.1
  496.3 3.2 copy-start.6
  496.3 3.2 copy-start.12
  499.5 106.2 %reduce-scatter.16.cloned.1.call-start = ((), (), s32[]{:S(2)}) async-start(), calls=%async_computation.15 | async-start | bytes 4456448 | tf_op jit(solution)/shard_map/reduce_scatter | solution.py:303
  502.3 314.3 %reduce-scatter.14.cloned.1.call-start = ((), (), s32[]{:S(2)}) async-start(), calls=%async_computation.14 | async-start | bytes 13369344 | tf_op jit(solution)/shard_map/reduce_scatter | solution.py:301
  515.9 1.0 copy-start.15
  515.9 649.0 %reduce-scatter.20.cloned.1.call-start = ((), (), s32[]{:S(2)}) async-start(), calls=%async_computation.17 | async-start | bytes 17825792 | tf_op jit(solution)/shard_map/reduce_scatter | solution.py:307
  527.9 991.5 %reduce-scatter.18.cloned.1.call-start = ((), (), s32[]{:S(2)}) async-start(), calls=%async_computation.16 | async-start | bytes 17825792 | tf_op jit(solution)/shard_map/reduce_scatter | solution.py:305
  537.8 1.2 copy-start.9
  537.8 1054.9 %reduce-scatter.24.cloned.1.call-start = ((), (), s32[]{:S(2)}) async-start(), calls=%async_computation.19 | async-start | bytes 557056
  545.8 1044.2 %copy-start.2 = (f32[256,1024]{1,0:T(8,128)S(1)}, f32[256,1024]{1,0:T(8,128)}, u32[]{:S(2)}) copy-start(f32[256,1024]{1,0:T(8,128)} %copy-done.1) | copy-start | bytes 3145732
  545.9 1121.9 %reduce-scatter.22.cloned.1.call-start = ((), (), s32[]{:S(2)}) async-start(), calls=%async_computation.18 | async-start | bytes 557056
  547.0 1152.3 %all-reduce.12.cloned.1.call-start = ((), (), s32[]{:S(2)}) async-start(), calls=%async_computation.20 | async-start | bytes 3145728 | tf_op jit(solution)/shard_map/psum | solution.py:313
Sparse Core Ops, SparseCore 0:
  10.8 95.5 all-gather.10
  114.1 25.4 all-gather.14
  141.8 10.1 all-gather.12
  154.6 61.0 all-gather.16
  218.3 111.5 all-gather.18
  332.5 111.0 all-gather.20
  499.6 8.5 reduce-scatter.11
  510.6 95.0 reduce-scatter.15
  612.3 204.2 reduce-scatter.13
  818.8 346.1 reduce-scatter.19
  1167.3 352.0 reduce-scatter.17
  1521.5 71.1 reduce-scatter.23
  1595.0 72.7 reduce-scatter.21
  1670.8 28.4 all-reduce.11
where the time goes:
time: 1720 us; the launch traced here: 1710 us
  waiting for transfers between devices  1290 us (75%)
  blocking collectives  236 us (14%)
  matrix products  91.6 us (5%)
  other arithmetic  44.5 us (3%)
  local copies, waits for them, and re-layouts  27.1 us (2%)
  between operations  22.5 us (1%)
    reduce_scatter x1, waiting for transfers between devices, shards(): lax.psum_scatter(grad_up, 'dp', scatter_dimension=0, tiled=True)  352 us
    reduce_scatter x1, waiting for transfers between devices, shards(): lax.psum_scatter(grad_down, 'dp', scatter_dimension=0, tiled=True)  346 us
    reduce_scatter x1, waiting for transfers between devices, shards(): lax.psum_scatter(grad_qkv, 'dp', scatter_dimension=0, tiled=True)  209 us
    all_gather x1, waiting for transfers between devices, shards(): lax.all_gather(w_up, 'dp', axis=0, tiled=True)  111 us
    all_gather x1, waiting for transfers between devices, shards(): lax.all_gather(w_down, 'dp', axis=0, tiled=True)  106 us
    unnamed x2, blocking collectives  99.2 us
    unnamed x16, waiting for transfers between devices  76.7 us
    reduce_scatter x1, waiting for transfers between devices, shards(): lax.psum_scatter(grad_out, 'dp', scatter_dimension=0, tiled=True)  58.6 us
  transfers between devices with their start and end apart: 14, of which 11 were waited for; matrix products, arithmetic and copies ran while one was open for 5% of the time, Pallas kernels for 0%

commit v1 on v0

--- a/solution.py
+++ b/solution.py
@@ -1,8 +1,11 @@
+import functools
 import math
 
 import jax
 import jax.numpy as jnp
 from jax import lax
+from jax.experimental import pallas as pl
+from jax.experimental.pallas import tpu as pltpu
 from jax.sharding import PartitionSpec as P
 
 HEADS = 16
@@ -324,6 +327,973 @@
     return (result.astype(jnp.bfloat16)[None], grad_inputs[None]) + tuple(totals)
 
 
+NZ = 4
+NPOS = 512
+LEN = 256
+WIDTH = 1024
+OWN = 512
+HID = 2048
+BF = jnp.bfloat16
+F32 = jnp.float32
+MESH = pl.DeviceIdType.MESH
+MIB = 1 << 20
+ROW_OUT, ROW_DOWN, ROW_GAIN, ROW_SHIFT = 3, 4, 5, 9
+CORE = NZ
+
+
+def dot_nn(a, b):
+    return lax.dot_general(a, b, (((1,), (0,)), ((), ())), preferred_element_type=F32)
+
+
+def dot_nt(a, b):
+    return lax.dot_general(a, b, (((1,), (1,)), ((), ())), preferred_element_type=F32)
+
+
+def dot_tn(a, b):
+    return lax.dot_general(a, b, (((0,), (0,)), ((), ())), preferred_element_type=F32)
+
+
+def loop(count, body):
+    lax.fori_loop(0, count, lambda index, carry: (body(index), carry)[1], 0)
+
+
+def mul(index, size):
+    return pl.multiple_of(index * size, size)
+
+
+class Net:
+    def __init__(self, sems):
+        self.chip = lax.axis_index("dp")
+        self.core = lax.axis_index("blk")
+        self.z = self.chip // 4
+        self.y = (self.chip // 2) % 2
+        self.x = self.chip % 2
+        self.sems = sems
+        self.used = 0
+        self.unsent = []
+
+    def sem(self):
+        self.used += 1
+        return self.sems.at[self.used - 1]
+
+    def chip_at(self, z, y, x):
+        return z * 4 + y * 2 + x
+
+    def peers(self, dim):
+        if dim == "x":
+            return [(1, self.z, self.y, 1 - self.x, self.core)]
+        if dim == "y":
+            return [(1, self.z, 1 - self.y, self.x, self.core)]
+        if dim == "c":
+            return [(1, self.z, self.y, self.x, 1 - self.core)]
+        return [(k, (self.z + k) % NZ, self.y, self.x, self.core) for k in range(1, NZ)]
+
+    def send(self, src, dst, recv, peer):
+        _, z, y, x, core = peer
+        copy = pltpu.make_async_remote_copy(
+            src_ref=src,
+            dst_ref=dst,
+            send_sem=self.sem(),
+            recv_sem=recv,
+            device_id=(self.chip_at(z, y, x), core),
+            device_id_type=MESH,
+        )
+        copy.start()
+        self.unsent.append(copy)
+        return copy
+
+    def drain(self):
+        for copy in self.unsent:
+            copy.wait_send()
+        self.unsent = []
+
+    def sibling(self, src, dst):
+        return self.send(src, dst, self.sem(), self.peers("c")[0])
+
+    def barrier(self):
+        barrier = pltpu.get_barrier_semaphore()
+        count = 0
+        for dim in "xyzc":
+            for _, z, y, x, core in self.peers(dim):
+                pl.semaphore_signal(
+                    barrier, inc=1, device_id=(self.chip_at(z, y, x), core), device_id_type=MESH
+                )
+                count += 1
+        pl.semaphore_wait(barrier, count)
+
+
+def gather_stages(net, ref, rows, lanes, order):
+    def at(z, y, x):
+        return ref.at[z, y, x, rows, lanes]
+
+    def place(**given):
+        where = {"z": net.z, "y": net.y, "x": net.x}
+        where.update(given)
+        return at(where["z"], where["y"], where["x"])
+
+    every = {"z": slice(None), "y": slice(None), "x": slice(None)}
+    first, second, third = order
+    got_first, got_second, got_near, got_far = net.sem(), net.sem(), net.sem(), net.sem()
+
+    def start():
+        for peer in net.peers(first):
+            net.send(place(), place(), got_first, peer)
+
+    def await_bytes(view, sem):
+        pltpu.make_async_copy(view, view, sem).wait()
+
+    def after_first():
+        if first == "z":
+            await_bytes(ref.at[pl.ds(0, NZ - 1), net.y, net.x, rows, lanes], got_first)
+        else:
+            await_bytes(place(), got_first)
+        held = {first: every[first]}
+        for peer in net.peers(second):
+            net.send(place(**held), place(**held), got_second, peer)
+        for peer in net.peers(third):
+            net.send(place(**held), place(**held), got_near, peer)
+
+    def after_second():
+        held = {first: every[first]}
+        other = {"x": {"x": 1 - net.x}, "y": {"y": 1 - net.y}}[second]
+        await_bytes(place(**held, **other), got_second)
+        for peer in net.peers(third):
+            net.send(place(**held, **other), place(**held, **other), got_far, peer)
+
+    def finish():
+        held = {first: every[first]}
+        other = {"x": {"x": 1 - net.x}, "y": {"y": 1 - net.y}}[third]
+        await_bytes(place(**held, **other), got_near)
+        await_bytes(place(**held, **other), got_far)
+
+    return start, after_first, after_second, finish
+
+
+def scatter_stages(net, ref, rows, lanes, order, bufs, done):
+    wide, half, line = bufs
+    first, second = order[0], order[1]
+    got_wide, got_half, got_line = net.sem(), net.sem(), net.sem()
+    dtype = wide.dtype
+    step = min(32, wide.shape[2])
+    steps = wide.shape[2] // step
+
+    def await_bytes(view, sem):
+        pltpu.make_async_copy(view, view, sem).wait()
+
+    def row_slice(part):
+        return pl.ds(rows.start + part * step, step)
+
+    def start():
+        peer = net.peers(first)[0]
+        if first == "x":
+            src = ref.at[:, :, 1 - net.x, rows, lanes]
+        else:
+            src = ref.at[:, 1 - net.y, :, rows, lanes]
+        net.send(src, wide, got_wide, peer)
+
+    def after_first():
+        await_bytes(wide, got_wide)
+
+        def add(a, b):
+            y, x = (b, net.x) if first == "x" else (net.y, b)
+            for part in range(steps):
+                kept = ref[a, y, x, row_slice(part), lanes].astype(F32)
+                come = wide[a, b, pl.ds(part * step, step), :].astype(F32)
+                ref[a, y, x, row_slice(part), lanes] = (kept + come).astype(dtype)
+
+        gone = 1 - net.y if first == "x" else 1 - net.x
+        loop(NZ, lambda a: add(a, gone))
+        if first == "x":
+            src = ref.at[:, 1 - net.y, net.x, rows, lanes]
+        else:
+            src = ref.at[:, net.y, 1 - net.x, rows, lanes]
+        net.send(src, half, got_half, net.peers(second)[0])
+        loop(NZ, lambda a: add(a, 1 - gone))
+
+    def after_second():
+        await_bytes(half, got_half)
+
+        def add(a):
+            for part in range(steps):
+                kept = ref[a, net.y, net.x, row_slice(part), lanes].astype(F32)
+                come = half[a, pl.ds(part * step, step), :].astype(F32)
+                ref[a, net.y, net.x, row_slice(part), lanes] = (kept + come).astype(dtype)
+
+        loop(NZ, add)
+        for peer in net.peers("z"):
+            net.send(
+                ref.at[peer[1], net.y, net.x, rows, lanes], line.at[peer[0] - 1], got_line, peer
+            )
+
+    def finish():
+        await_bytes(line, got_line)
+        for part in range(steps):
+            here = pl.ds(part * step, step)
+            total = ref[net.z, net.y, net.x, row_slice(part), lanes].astype(F32)
+            for k in range(NZ - 1):
+                total = total + line[k, here, :].astype(F32)
+            done(part * step, step, total)
+
+    return start, after_first, after_second, finish
+
+
+def layer_kernel(
+    tok,
+    doc,
+    cot,
+    wq_in,
+    wo_in,
+    wu_in,
+    wd_in,
+    vec_in,
+    res_out,
+    gtok_out,
+    gq_out,
+    go_out,
+    gu_out,
+    gd_out,
+    gvec_out,
+    wq,
+    wo,
+    wu,
+    wd,
+    vbuf,
+    vecs,
+    vq,
+    vu,
+    xin,
+    qb,
+    kb,
+    vb,
+    pb,
+    att,
+    attb,
+    attx,
+    hat1,
+    hat2,
+    inv1,
+    inv2,
+    mid,
+    fin,
+    act,
+    dge,
+    rcv,
+    own,
+    snd,
+    gff,
+    gbr,
+    dob,
+    dsb,
+    gu,
+    gd,
+    swap,
+    acc,
+    acc_qv,
+    acc_up,
+    gvecs,
+    gv,
+    vother,
+    r_q,
+    r_o,
+    r_u,
+    r_d,
+    r_v,
+    st_q,
+    st_o,
+    st_u,
+    st_d,
+    sems,
+    local_sems,
+):
+    (rq_a, rq_b), (ro_a, ro_b), (ru_a, ru_b), (rd_a, rd_b) = r_q, r_o, r_u, r_d
+    net = Net(sems)
+    core = net.core
+    me = (net.z, net.y, net.x)
+
+    locals_ = []
+
+    def fetch(src, dst):
+        copy = pltpu.make_async_copy(src, dst, local_sems.at[len(locals_)])
+        copy.start()
+        locals_.append(copy)
+
+    def lanes_of(start, size):
+        return pl.ds(pl.multiple_of(start, 128), size)
+
+    for part in range(3):
+        fetch(
+            wq_in.at[:, lanes_of(part * WIDTH + core * OWN, OWN)],
+            wq.at[net.z, net.y, net.x, :, pl.ds(part * OWN, OWN)],
+        )
+    fetch(wo_in.at[:, lanes_of(core * OWN, OWN)], wo.at[core, net.z, net.y, net.x])
+    for i in range(NZ * 4):
+        fetch(
+            wu_in.at[:, lanes_of(i * 256 + core * 128, 128)],
+            wu.at[net.z, net.y, net.x, :, pl.ds(i * 128, 128)],
+        )
+    fetch(wd_in.at[pl.ds(mul(core, 128), 128), :], wd.at[net.z, net.y, net.x])
+    vbuf[net.z, net.y, net.x] = vec_in[...]
+    wo_own = wo.at[core]
+
+    full = slice(None)
+    pieces = [gather_stages(net, vbuf, full, full, "zyx")]
+    for ref, size in ((wq, 64), (wo_own, 64), (wu, 64), (wd, 128)):
+        half = size // 2
+        pieces.append(gather_stages(net, ref, pl.ds(0, half), full, "zyx"))
+        pieces.append(gather_stages(net, ref, pl.ds(half, half), full, "zxy"))
+    net.barrier()
+    pieces[0][0]()
+    ready = (0, 0, 0, 3, 3, 4, 4, 20, 20)
+    landed = 0
+    for piece, first in zip(pieces[1:], ready[1:], strict=True):
+        need = {0: 3, 3: 4, 4: 20, 20: 21}[first]
+        while landed < need:
+            locals_[landed].wait()
+            landed += 1
+        piece[0]()
+
+    events = [(0, 1), (0, 2), (0, 3)]
+    for slot in range(1, len(pieces) + 4):
+        for stage in (3, 2, 1):
+            first = slot - 2 * (stage - 1)
+            if first >= 1 and first < len(pieces) and first % 2 == 1:
+                events.append((first, stage))
+                events.append((first + 1, stage))
+    state = {"at": 0}
+
+    def pump(count):
+        for _ in range(count):
+            if state["at"] < len(events):
+                piece, stage = events[state["at"]]
+                pieces[piece][stage]()
+                state["at"] += 1
+
+    def pump_until(piece):
+        last = max(events.index((p, 3)) for p in piece)
+        while state["at"] <= last:
+            pump(1)
+
+    pump(3)
+
+    for z in range(NZ):
+        for y in range(2):
+            both = vbuf[z, y, 0].astype(F32) + vbuf[z, y, 1].astype(F32)
+            vecs[:, pl.ds((z * 2 + y) * 128, 128)] = both
+    for y in range(2):
+        for x in range(2):
+            at = pl.ds((y * 2 + x) * 128, 128)
+            vq[0:8, at] = vbuf[core, y, x].astype(F32)[0:8]
+            vq[8:16, at] = vbuf[core + 2, y, x].astype(F32)[0:8]
+            for z in range(NZ):
+                block = vbuf[z, y, x].astype(F32)
+                vu[0:1, pl.ds((z * 4 + y * 2 + x) * 128, 128)] = jnp.where(
+                    core == 0, block[1:2], block[2:3]
+                )
+
+    def gain(n):
+        return vecs[ROW_GAIN + n : ROW_GAIN + n + 1, :]
+
+    def shift(n):
+        return vecs[ROW_SHIFT + n : ROW_SHIFT + n + 1, :]
+
+    def accumulate(row, value):
+        parts = value.reshape(value.shape[0] // 8, 8, value.shape[1])
+        acc[row] += jnp.sum(parts, axis=0)
+
+    acc[...] = jnp.zeros_like(acc)
+    acc_up[...] = jnp.zeros_like(acc_up)
+
+    chunk = 32
+    chunks = LEN // chunk
+
+    def ln0(i):
+        here = pl.ds(mul(i, chunk), chunk)
+        hat, _ = normalize(tok[here, :].astype(F32))
+        xin[core, here, :] = (hat * gain(0) + shift(0)).astype(BF)
+
+    loop(chunks, ln0)
+    got_x = net.sibling(xin.at[core], xin.at[core])
+    pump(2)
+    got_x.wait_recv()
+
+    ends = []
+    end = jnp.int32(0)
+    for j in range(8):
+        end = end + doc[0, j]
+        ends.append(end)
+
+    def segment(position):
+        total = jnp.zeros(position.shape, jnp.int32)
+        for value in ends:
+            total = total + (position >= value).astype(jnp.int32)
+        return total
+
+    pump_until((1, 2))
+    scale = 1.0 / (ALPHA * 8.0)
+
+    def project(t):
+        n = t // 2
+        m = t % 2
+        tile = pl.ds(mul(n, 256), 256)
+        rows = pl.ds(mul(m, 256), 256)
+
+        def part(index, dst, bias, factor):
+            weight = wq[:, :, :, :, pl.ds(pl.multiple_of(index * OWN + n * 256, 256), 256)]
+            value = dot_nn(xin[m], weight.reshape(WIDTH, 256))
+            if bias is not None:
+                value = value + vq[bias : bias + 1, tile]
+            if factor is not None:
+                value = value * factor
+            dst[rows, tile] = value.astype(BF)
+
+        part(0, qb, 0, scale)
+        part(1, kb, None, None)
+        part(2, vb, 8, None)
+
+    loop(4, project)
+    pump(2)
+
+    lane = lax.broadcasted_iota(jnp.int32, (1, 128), 1)
+    block = 128
+
+    def attend(pair):
+        at = pl.ds(mul(pair, 128), 128)
+        for r in range(NPOS // block):
+            rows = pl.ds(r * block, block)
+            count = (r + 1) * block
+            q_pos = r * block + lax.broadcasted_iota(jnp.int32, (block, 1), 0)
+            k_pos = lax.broadcasted_iota(jnp.int32, (1, count), 1)
+            allowed = (segment(q_pos) == segment(k_pos)) & (k_pos <= q_pos)
+            q = qb[rows, at]
+            k = kb[0:count, at]
+            v = vb[0:count, at]
+            outs = []
+            for head in range(2):
+                mine = (lane < 64) if head == 0 else (lane >= 64)
+                scores = dot_nt(jnp.where(mine, q, jnp.zeros_like(q)), k)
+                scores = jnp.where(allowed, scores, FILLER)
+                top = jnp.max(scores, axis=1, keepdims=True)
+                weights = jnp.exp(ALPHA * (scores - top))
+                probs = weights * (1.0 / jnp.sum(weights, axis=1, keepdims=True))
+                probs = probs.astype(BF)
+                pb[pair * 2 + head, rows, 0:count] = probs
+                outs.append(dot_nn(probs, v))
+            out = jnp.where(lane < 64, outs[0], outs[1])
+            att[rows, at] = out
+            attb[rows, at] = out.astype(BF)
+
+    loop(2, attend)
+    pump(2)
+    loop(2, lambda i: attend(i + 2))
+    other_rows = pl.ds(mul(1 - core, LEN), LEN)
+    own_rows = pl.ds(mul(core, LEN), LEN)
+    got_att = net.sibling(attb.at[other_rows, :], attx)
+    pump_until((3, 4))
+    got_wo = net.sibling(wo_own, wo.at[core])
+    got_att.wait_recv()
+    got_wo.wait_recv()
+
+    def branch_tile(n):
+        lanes = pl.ds(mul(n % 2, 256), 256)
+        mine = wo[n // 2, pl.ds(2 * core, 2), :, :, :, lanes].reshape(OWN, 256)
+        theirs = wo[n // 2, pl.ds(2 * (1 - core), 2), :, :, :, lanes].reshape(OWN, 256)
+        at = pl.ds(mul(n, 256), 256)
+        own[:, at] = dot_nn(attb[own_rows, :], mine) + dot_nn(attx[...], theirs)
+
+    loop(4, branch_tile)
+
+    def ln12(i):
+        here = pl.ds(mul(i, chunk), chunk)
+        first, first_inv = normalize(own[here, :] + vecs[ROW_OUT : ROW_OUT + 1, :])
+        hat1[here, :] = first
+        inv1[here, :] = jnp.broadcast_to(first_inv, (chunk, 128))
+        middle = tok[here, :].astype(F32) + first * gain(1) + shift(1)
+        mid[here, :] = middle
+        second, second_inv = normalize(middle)
+        hat2[here, :] = second
+        inv2[here, :] = jnp.broadcast_to(second_inv, (chunk, 128))
+        fin[core, here, :] = (second * gain(2) + shift(2)).astype(BF)
+
+    loop(chunks, ln12)
+    got_fin = net.sibling(fin.at[core], fin.at[core])
+    pump(2)
+    got_fin.wait_recv()
+    pump_until((5, 6))
+
+    root = math.sqrt(2.0 / math.pi)
+
+    def up_tile(t):
+        n = t // 2
+        m = t % 2
+        at = pl.ds(mul(n, 256), 256)
+        rows = pl.ds(mul(m, 256), 256)
+        weight = wu[:, :, :, :, at].reshape(WIDTH, 256)
+        u = dot_nn(fin[m], weight) + vu[0:1, at]
+        square = u * u
+        inner = jnp.tanh(root * (u + 0.044715 * (square * u)))
+        half = 0.5 * (1.0 + inner)
+        act[rows, at] = (u * half).astype(BF)
+        slope = 0.5 * u * (1.0 - inner * inner) * (root * (1.0 + (3 * 0.044715) * square))
+        dge[rows, at] = (half + slope).astype(BF)
+
+    loop(8, up_tile)
+    pump(2)
+    loop(8, lambda i: up_tile(i + 8))
+    pump(len(events))
+
+    def down_tile(rows, dst):
+        def body(n):
+            at = pl.ds(mul(n, 256), 256)
+            weight = wd[:, :, :, :, at].reshape(HID, 256)
+            dst[:, at] = dot_nn(act[rows, :], weight)
+
+        loop(4, body)
+
+    down_tile(other_rows, snd)
+    got_part = net.sibling(snd, rcv)
+    down_tile(own_rows, own)
+    got_part.wait_recv()
+
+    filled = ends[-1]
+
+    def upstream_of(i):
+        here = pl.ds(mul(i, chunk), chunk)
+        position = core * LEN + i * chunk + lax.broadcasted_iota(jnp.int32, (chunk, 1), 0)
+        return cot[here, :].astype(F32) * (position < filled).astype(F32)
+
+    def top_tile(i):
+        here = pl.ds(mul(i, chunk), chunk)
+        value = own[here, :] + rcv[here, :] + vecs[ROW_DOWN : ROW_DOWN + 1, :]
+        hat, inv = normalize(value)
+        res_out[here, :] = (mid[here, :] + hat * gain(3) + shift(3)).astype(BF)
+        upstream = upstream_of(i)
+        grad = norm_back(hat, inv, gain(3), upstream).astype(BF)
+        gff[core, here, :] = grad
+        accumulate(ROW_GAIN + 3, upstream * hat)
+        accumulate(ROW_SHIFT + 3, upstream)
+        accumulate(ROW_DOWN, grad.astype(F32))
+
+    loop(chunks, top_tile)
+    got_gff = net.sibling(gff.at[core], gff.at[core])
+
+    out_copies = []
+
+    def deliver(stage, out_views):
+        for src, dst in out_views:
+            copy = pltpu.make_async_copy(src, dst, local_sems.at[21 + len(out_copies)])
+            copy.start()
+            out_copies.append((copy, net.sibling(src, dst)))
+
+    def store_to(stage, row0):
+        def done(offset, size, total):
+            stage[row0 + offset : row0 + offset + size, :] = total
+
+        return done
+
+    wgrad = {}
+    for name, ref, lanes, size, bufs, stage in (
+        ("d", gd, full, 128, (rd_a, rd_b), st_d),
+        ("u", gu, full, 64, (ru_a, ru_b), st_u),
+        ("o", wu, pl.ds(3 * OWN, OWN), 64, (ro_a, ro_b), st_o),
+        ("q", wu, pl.ds(0, 3 * OWN), 64, (rq_a, rq_b), st_q),
+    ):
+        half = size // 2
+        wgrad[name] = [
+            scatter_stages(net, ref, pl.ds(0, half), lanes, "xyz", bufs[0], store_to(stage, 0)),
+            scatter_stages(
+                net, ref, pl.ds(half, half), lanes, "yxz", bufs[1], store_to(stage, half)
+            ),
+        ]
+
+    def ship(name, half):
+        def views():
+            if name == "d":
+                rows = pl.ds(pl.multiple_of(core * 128 + half * 64, 64), 64)
+                return [(st_d.at[half * 64 : half * 64 + 64, :], gd_out.at[rows, :])]
+            rows = slice(half * 32, half * 32 + 32)
+            if name == "u":
+                return [
+                    (
+                        st_u.at[rows, pl.ds(i * 128, 128)],
+                        gu_out.at[rows, lanes_of(i * 256 + core * 128, 128)],
+                    )
+                    for i in range(NZ * 4)
+                ]
+            if name == "o":
+                return [(st_o.at[rows, :], go_out.at[rows, lanes_of(core * OWN, OWN)])]
+            return [
+                (
+                    st_q.at[rows, pl.ds(p * OWN, OWN)],
+                    gq_out.at[rows, lanes_of(p * WIDTH + core * OWN, OWN)],
+                )
+                for p in range(3)
+            ]
+
+        deliver(None, views())
+
+    queue = []
+
+    def launch(name):
+        for half in range(2):
+            wgrad[name][half][0]()
+
+    def relay(name, stage):
+        for half in range(2):
+            wgrad[name][half][stage]()
+            if stage == 3:
+                ship(name, half)
+
+    got_gff.wait_recv()
+
+    def gdown_tile(t):
+        k = t // 2
+        z = k // 2
+        y = k % 2
+        at = pl.ds(mul(t % 2, 512), 512)
+        left = act[:, pl.ds(mul(k, 256), 256)]
+        grad = gff[:, :, at].reshape(NPOS, 512)
+        gd[z, y, :, :, at] = dot_tn(left, grad).astype(BF).reshape(2, 128, 512)
+
+    loop(16, gdown_tile)
+    launch("d")
+
+    def gpre_tile(t):
+        k = t // 2
+        m = t % 2
+        at = pl.ds(mul(k, 256), 256)
+        rows = pl.ds(mul(m, 256), 256)
+        weight = wd[k // 2, k % 2].reshape(256, WIDTH)
+        value = dot_nt(gff[m], weight) * dge[rows, at].astype(F32)
+        value = value.astype(BF)
+        dge[rows, at] = value
+        acc_up[:, at] += jnp.sum(value.astype(F32).reshape(32, 8, 256), axis=0)
+
+    loop(16, gpre_tile)
+
+    def gup_tile(t):
+        z = t // 4
+        at = pl.ds(mul(t % 4, 512), 512)
+        left = fin[:, :, pl.ds(mul(z, 256), 256)].reshape(NPOS, 256)
+        gu[z, :, :, :, at] = dot_tn(left, dge[:, at]).astype(BF).reshape(2, 2, 64, 512)
+
+    loop(16, gup_tile)
+    launch("u")
+
+    net.drain()
+
+    def gfi_tile(rows, dst):
+        def body(z):
+            weight = wu[z].reshape(256, HID)
+            dst[:, pl.ds(mul(z, 256), 256)] = dot_nt(dge[rows, :], weight)
+
+        loop(NZ, body)
+
+    gfi_tile(other_rows, snd)
+    got_part = net.sibling(snd, rcv)
+    gfi_tile(own_rows, own)
+    relay("d", 1)
+    got_part.wait_recv()
+
+    def middle_tile(i):
+        here = pl.ds(mul(i, chunk), chunk)
+        grad_in = own[here, :] + rcv[here, :]
+        second = hat2[here, :]
+        accumulate(ROW_GAIN + 2, grad_in * second)
+        accumulate(ROW_SHIFT + 2, grad_in)
+        grad_mid = upstream_of(i) + norm_back(second, inv2[here, 0:1], gain(2), grad_in)
+        mid[here, :] = grad_mid
+        first = hat1[here, :]
+        accumulate(ROW_GAIN + 1, grad_mid * first)
+        accumulate(ROW_SHIFT + 1, grad_mid)
+        grad = norm_back(first, inv1[here, 0:1], gain(1), grad_mid).astype(BF)
+        gbr[core, here, :] = grad
+        accumulate(ROW_OUT, grad.astype(F32))
+
+    loop(chunks, middle_tile)
+    got_gbr = net.sibling(gbr.at[core], gbr.at[core])
+    relay("u", 1)
+    got_gbr.wait_recv()
+
+    go = wu.at[:, :, :, :, pl.ds(3 * OWN, OWN)]
+
+    def gout_tile(k, cols, put):
+        left = attb[:, pl.ds(mul(k, 256), 256)]
+        grad = gbr[:, :, cols].reshape(NPOS, OWN)
+        put(k, dot_tn(left, grad).astype(BF).reshape(2, 2, 64, OWN))
+
+    def put_swap(k, value):
+        swap[k] = value
+
+    def put_own(k, value):
+        wu[2 * core + k, :, :, :, pl.ds(3 * OWN, OWN)] = value
+
+    loop(2, lambda k: gout_tile(k, lanes_of((1 - core) * OWN, OWN), put_swap))
+    got_swap = net.sibling(swap, go.at[pl.ds(2 * core, 2)])
+    loop(2, lambda k: gout_tile(k, lanes_of(core * OWN, OWN), put_own))
+
+    def gatt_tile(t):
+        k = t // 2
+        m = t % 2
+        left = wo[0, 2 * core + k].reshape(256, OWN)
+        right = wo[1, 2 * core + k].reshape(256, OWN)
+        value = dot_nt(gbr[m, :, 0:OWN], left) + dot_nt(gbr[m, :, OWN:WIDTH], right)
+        dob[pl.ds(mul(m, 256), 256), pl.ds(mul(k, 256), 256)] = value.astype(BF)
+
+    loop(4, gatt_tile)
+    got_swap.wait_recv()
+    launch("o")
+
+    def attend_back(pair):
+        at = pl.ds(mul(pair, 128), 128)
+        sums = []
+        for head in range(2):
+            mine = (lane < 64) if head == 0 else (lane >= 64)
+            queries_ = []
+            for r in range(NPOS // block):
+                rows = pl.ds(r * block, block)
+                count = (r + 1) * block
+                grad = dob[rows, at]
+                grad = jnp.where(mine, grad, jnp.zeros_like(grad))
+                delta = jnp.sum(grad.astype(F32) * att[rows, at], axis=1, keepdims=True)
+                probs = pb[pair * 2 + head, rows, 0:count].astype(F32)
+                grad_probs = dot_nt(grad, vb[0:count, at])
+                scores = (ALPHA * probs * (grad_probs - delta)).astype(BF)
+                dsb[rows, 0:count] = scores
+                queries_.append(dot_nn(scores, kb[0:count, at]))
+            keys_, values_ = [], []
+            for r in range(NPOS // block):
+                rows = pl.ds(r * block, NPOS - r * block)
+                cols = pl.ds(r * block, block)
+                keys_.append(dot_tn(dsb[rows, cols], qb[rows, at]))
+                values_.append(dot_tn(pb[pair * 2 + head, rows, cols], dob[rows, at]))
+            sums.append((queries_, keys_, values_))
+        total_q = jnp.zeros((8, 128), F32)
+        total_v = jnp.zeros((8, 128), F32)
+        for r in range(NPOS // block):
+            rows = pl.ds(r * block, block)
+            merged = [
+                jnp.where(lane < 64, sums[0][i][r], sums[1][i][r]).astype(BF) for i in range(3)
+            ]
+            grad_q = merged[0] * jnp.asarray(scale, BF)
+            qb[rows, at] = grad_q
+            kb[rows, at] = merged[1]
+            vb[rows, at] = merged[2]
+            total_q += jnp.sum(grad_q.astype(F32).reshape(block // 8, 8, 128), axis=0)
+            total_v += jnp.sum(merged[2].astype(F32).reshape(block // 8, 8, 128), axis=0)
+        acc_qv[0, :, at] = total_q
+        acc_qv[1, :, at] = total_v
+
+    loop(1, attend_back)
+    relay("d", 2)
+    loop(1, lambda i: attend_back(i + 1))
+    loop(1, lambda i: attend_back(i + 2))
+    relay("u", 2)
+    loop(1, lambda i: attend_back(i + 3))
+    relay("o", 1)
+
+    def gqkv_tile(z):
+        left = xin[:, :, pl.ds(mul(z, 256), 256)].reshape(NPOS, 256)
+        for part, ref in enumerate((qb, kb, vb)):
+            value = dot_tn(left, ref[...]).astype(BF)
+            wu[z, :, :, :, pl.ds(part * OWN, OWN)] = value.reshape(2, 2, 64, OWN)
+
+    loop(NZ, gqkv_tile)
+    launch("q")
+    net.drain()
+
+    def gai_tile(rows, dst):
+        def body(z):
+            value = None
+            for part, ref in enumerate((qb, kb, vb)):
+                weight = wq[z, :, :, :, pl.ds(part * OWN, OWN)].reshape(256, OWN)
+                term = dot_nt(ref[rows, :], weight)
+                value = term if value is None else value + term
+            dst[:, pl.ds(mul(z, 256), 256)] = value
+
+        loop(NZ, body)
+
+    gai_tile(other_rows, snd)
+    got_part = net.sibling(snd, rcv)
+    gai_tile(own_rows, own)
+    relay("d", 3)
+    relay("o", 2)
+    got_part.wait_recv()
+
+    def bottom_tile(i):
+        here = pl.ds(mul(i, chunk), chunk)
+        hat, inv = normalize(tok[here, :].astype(F32))
+        grad_in = own[here, :] + rcv[here, :]
+        accumulate(ROW_GAIN, grad_in * hat)
+        accumulate(ROW_SHIFT, grad_in)
+        gtok_out[here, :] = mid[here, :] + norm_back(hat, inv, gain(0), grad_in)
+
+    loop(chunks, bottom_tile)
+
+    for row in range(16):
+        gvecs[row : row + 1, :] = jnp.sum(acc[row], axis=0, keepdims=True)
+    row_id = lax.broadcasted_iota(jnp.int32, (16, 1), 0)
+    for z in range(NZ):
+        for y in range(2):
+            base = gvecs[:, pl.ds((z * 2 + y) * 128, 128)]
+            for x in range(2):
+                at = pl.ds((y * 2 + x) * 128, 128)
+                kind = 0 if z < 2 else 1
+                qv_row = jnp.sum(acc_qv[kind, :, at], axis=0, keepdims=True)
+                qv_row = jnp.where(core == z % 2, qv_row, 0.0)
+                up_at = pl.ds((z * 4 + y * 2 + x) * 128, 128)
+                up_row = jnp.sum(acc_up[:, up_at], axis=0, keepdims=True)
+                value = base + jnp.where(row_id == 0, qv_row, 0.0)
+                gv[z, y, x] = value + jnp.where(row_id == 1 + core, up_row, 0.0)
+
+    def keep_vec(offset, size, total):
+        gvec_out[offset : offset + size, :] = total
+
+    vec = scatter_stages(net, gv, pl.ds(0, 16), full, "xyz", r_v, keep_vec)
+    vec[0]()
+    relay("q", 1)
+    vec[1]()
+    relay("u", 3)
+    vec[2]()
+    relay("o", 3)
+    vec[3]()
+    got_vec = net.sibling(gvec_out, vother)
+    relay("q", 2)
+    got_vec.wait()
+    net.unsent = [copy for copy in net.unsent if copy is not got_vec]
+    gvec_out[...] = gvec_out[...] + vother[...]
+    relay("q", 3)
+    for copy, remote in out_copies:
+        copy.wait()
+        remote.wait_recv()
+    net.drain()
+
+
+def scatter_bufs(rows, cols, dtype):
+    return [
+        pltpu.VMEM((NZ, 2, rows, cols), dtype),
+        pltpu.VMEM((NZ, rows, cols), dtype),
+        pltpu.VMEM((NZ - 1, rows, cols), dtype),
+    ]
+
+
+def fused(
+    tokens,
+    doc_lengths,
+    cotangent,
+    w_qkv,
+    qv_bias,
+    w_out,
+    out_bias,
+    w_up,
+    up_bias,
+    w_down,
+    down_bias,
+    norm_gain,
+    norm_bias,
+):
+    right = lax.axis_index("dp") % 2 == 1
+    narrow = jnp.concatenate([out_bias[None], down_bias[None], norm_gain, norm_bias], 0)
+    blank = jnp.zeros_like(narrow)
+    wide = jnp.where(
+        right, jnp.concatenate([blank, narrow], 1), jnp.concatenate([narrow, blank], 1)
+    )
+    packed = jnp.concatenate(
+        [qv_bias[None], up_bias.reshape(2, 128), wide, jnp.zeros((3, 128), BF)], 0
+    )
+    vmem = pl.BlockSpec(memory_space=pltpu.VMEM)
+    anywhere = pl.BlockSpec(memory_space=pl.ANY)
+    scratch = [
+        pltpu.VMEM((NZ, 2, 2, 64, 3 * OWN), BF),
+        pltpu.VMEM((2, NZ, 2, 2, 64, OWN), BF),
+        pltpu.VMEM((NZ, 2, 2, 64, HID), BF),
+        pltpu.VMEM((NZ, 2, 2, 128, WIDTH), BF),
+        pltpu.VMEM((NZ, 2, 2, 16, 128), BF),
+        pltpu.VMEM((16, WIDTH), F32),
+        pltpu.VMEM((16, OWN), F32),
+        pltpu.VMEM((8, HID), F32),
+        pltpu.VMEM((2, LEN, WIDTH), BF),
+        pltpu.VMEM((NPOS, OWN), BF),
+        pltpu.VMEM((NPOS, OWN), BF),
+        pltpu.VMEM((NPOS, OWN), BF),
+        pltpu.VMEM((8, NPOS, NPOS), BF),
+        pltpu.VMEM((NPOS, OWN), F32),
+        pltpu.VMEM((NPOS, OWN), BF),
+        pltpu.VMEM((LEN, OWN), BF),
+        pltpu.VMEM((LEN, WIDTH), F32),
+        pltpu.VMEM((LEN, WIDTH), F32),
+        pltpu.VMEM((LEN, 128), F32),
+        pltpu.VMEM((LEN, 128), F32),
+        pltpu.VMEM((LEN, WIDTH), F32),
+        pltpu.VMEM((2, LEN, WIDTH), BF),
+        pltpu.VMEM((NPOS, HID), BF),
+        pltpu.VMEM((NPOS, HID), BF),
+        pltpu.VMEM((LEN, WIDTH), F32),
+        pltpu.VMEM((LEN, WIDTH), F32),
+        pltpu.VMEM((LEN, WIDTH), F32),
+        pltpu.VMEM((2, LEN, WIDTH), BF),
+        pltpu.VMEM((2, LEN, WIDTH), BF),
+        pltpu.VMEM((NPOS, OWN), BF),
+        pltpu.VMEM((NPOS, NPOS), BF),
+        pltpu.VMEM((NZ, 2, 2, 64, HID), BF),
+        pltpu.VMEM((NZ, 2, 2, 128, WIDTH), BF),
+        pltpu.VMEM((2, 2, 2, 64, OWN), BF),
+        pltpu.VMEM((16, 8, WIDTH), F32),
+        pltpu.VMEM((2, 8, OWN), F32),
+        pltpu.VMEM((8, HID), F32),
+        pltpu.VMEM((16, WIDTH), F32),
+        pltpu.VMEM((NZ, 2, 2, 16, 128), F32),
+        pltpu.VMEM((16, 128), F32),
+        [scatter_bufs(32, 3 * OWN, BF)] * 2,
+        [scatter_bufs(32, OWN, BF)] * 2,
+        [scatter_bufs(32, HID, BF)] * 2,
+        [scatter_bufs(64, WIDTH, BF)] * 2,
+        scatter_bufs(16, 128, F32),
+        pltpu.VMEM((64, 3 * OWN), F32),
+        pltpu.VMEM((64, OWN), F32),
+        pltpu.VMEM((64, HID), F32),
+        pltpu.VMEM((128, WIDTH), F32),
+        pltpu.SemaphoreType.DMA((300,)),
+        pltpu.SemaphoreType.DMA((70,)),
+    ]
+    outs = pl.pallas_call(
+        layer_kernel,
+        out_shape=[
+            jax.ShapeDtypeStruct((LEN, WIDTH), BF),
+            jax.ShapeDtypeStruct((LEN, WIDTH), F32),
+            jax.ShapeDtypeStruct((64, 3 * WIDTH), F32),
+            jax.ShapeDtypeStruct((64, WIDTH), F32),
+            jax.ShapeDtypeStruct((64, 2 * HID), F32),
+            jax.ShapeDtypeStruct((256, WIDTH), F32),
+            jax.ShapeDtypeStruct((16, 128), F32),
+        ],
+        in_specs=[vmem, pl.BlockSpec(memory_space=pltpu.SMEM), vmem]
+        + [anywhere] * 4
+        + [vmem],
+        out_specs=[vmem, vmem] + [anywhere] * 4 + [vmem],
+        scratch_shapes=scratch,
+        compiler_params=pltpu.CompilerParams(
+            collective_id=0, has_side_effects=True, vmem_limit_bytes=63 * MIB
+        ),
+        name="layer",
+    )(tokens[0], doc_lengths, cotangent[0], w_qkv, w_out, w_up, w_down, packed)
+    result, grad_inputs, grad_qkv, grad_out, grad_up, grad_down, vec = outs
+    part = jnp.where(right, vec[3:13, 64:], vec[3:13, :64])
+    return (
+        result[None],
+        grad_inputs[None],
+        grad_qkv,
+        vec[0],
+        grad_out,
+        part[0],
+        grad_up,
+        vec[1:3].reshape(256),
+        grad_down,
+        part[1],
+        part[2:6],
+        part[6:10],
+    )
+
+
 def solution(mesh):
     placed = (
         P("dp", "blk", None),
@@ -340,8 +1310,9 @@
         P(None, "dp"),
         P(None, "dp"),
     )
+    sizes = (mesh.shape["dp"], mesh.shape["blk"])
     return jax.shard_map(
-        shards,
+        fused if sizes == (NZ * 4, 2) else shards,
         mesh=mesh,
         in_specs=placed,
         out_specs=(

time: 1720 us -> 309 us (0.18)
  waiting for transfers between devices: 1290 us -> 0 us
  Pallas kernels: 0 us -> 293 us
  blocking collectives: 236 us -> 0 us
  matrix products: 91.6 us -> 0 us
  other arithmetic: 44.5 us -> 1.6 us
  between operations: 22.5 us -> 0.75 us
    reduce_scatter x5 -> x0, waiting for transfers between devices: 971 us -> none  [the longest x1 352 us: shards(): lax.psum_scatter(grad_up, 'dp', scatter_dimension=0, tiled=True)]
    pallas_call x0 -> x1, Pallas kernels: none -> 293 us  [fused(): pl.pallas_call(layer_kernel, out_shape=[jax.ShapeDtypeStruct((LEN, WIDTH)...]
    all_gather x6 -> x0, waiting for transfers between devices: 230 us -> none  [the longest x1 111 us: shards(): lax.all_gather(w_up, 'dp', axis=0, tiled=True)]
    all_gather x4 -> x0, blocking collectives: 123 us -> none  [the longest x1 34.8 us: shards(): lax.all_gather(norm_gain, 'dp', axis=1, tiled=True)]
    unnamed x2 -> x0, blocking collectives: 99.2 us -> none
    dot_general x24 -> x0, matrix products: 91.6 us -> none  [the longest x1 10.9 us: shards(): jnp.einsum('tf,td->fd', act_low, grad_ffn, preferred_element_type=jnp.flo...]
    unnamed x16 -> x0, waiting for transfers between devices: 76.7 us -> none
    convert_element_type x22 -> x0, other arithmetic: 20.6 us -> none  [the longest x1 2.13 us: shards(): lax.psum(shares[6].astype(jnp.bfloat16), 'blk').astype(jnp.float32)]
  transfers between devices with their start and end apart: 14 -> 0, of which waited for: 11 -> 0; matrix products, arithmetic and copies ran while one was open for 5% -> 0% of each run, Pallas kernels for 0% -> 0%
where the time goes in v1:
time: 309 us; the launch traced here: 308 us
  Pallas kernels  293 us (95%)
  local copies, waits for them, and re-layouts  12.6 us (4%)
    pallas_call x1, Pallas kernels, fused(): pl.pallas_call(layer_kernel, out_shape=[jax.ShapeDtypeStruct((LEN, WIDTH)...  293 us
    unnamed x28, local copies, waits for them, and re-layouts  8.92 us

profile of v1, /device:TPU:1, one launch (start us, length us, event | category | flops | bytes accessed | tf_op | source)
XLA Modules:
  0.0 308.1 jit_solution(13154481201173217205)
XLA Ops:
  0.7 0.0 copy-start.6
  0.7 0.0 copy-start.8
  0.7 0.0 copy-start.5
  0.7 0.0 copy-start.7
  0.7 0.1 pad.5.clone
  0.8 0.5 copy-done.6
  1.3 0.0 copy-done.8
  1.3 0.0 copy-done.5
  1.4 0.0 copy-done.7
  1.4 0.0 copy-start.9
  1.4 0.0 copy-start.10
  1.4 0.1 pad_select_fusion
  1.5 0.6 copy-done.9
  2.0 0.0 copy-done.10
  2.1 0.7 maximum_maximum_fusion.vec_in
  2.7 293.2 %layer.1 = (bf16[256,1024]{1,0:T(8,128)(2,1)}, f32[256,1024]{1,0:T(8,128)}, f32[64,3072]{1,0:T(8,128)}, f32[64,1024]{1,0:T(8,128)}, f32[64,4096]{1,0:T(8,128)}, /*index=5*/f32[256,1024]{1,0:T(8,128)}, f32[16,128]{1,0:T(8,128)}) custom-call(bf16[256,1024]{1,0:T(8,128)(2,1)} %bitcast.18, s32[1,8]{1,0:T(1,128)} %doc.1, bf16[256,1024]{1,0:T(8,128)(2,1)} %bitcast.19, ...), custom_call_target="tpu_custom_call" | custom-call | tf_op jit(solution)/shard_map/layer/pallas_call | solution.py:1258
  295.9 0.0 copy-start.2
  295.9 1.3 slice_bitcast_fusion.3
  297.2 1.2 slice_bitcast_fusion
  298.4 0.8 slice_select_fusion
  299.2 0.5 slice_bitcast_fusion.1
  299.8 0.6 fusion
  300.3 1.9 copy.31
  302.2 0.0 copy-done.2
  302.2 0.0 copy-start.3
  302.2 1.0 copy.32
  303.2 0.5 copy-done.3
  303.7 0.0 copy-start.4
  303.7 0.0 copy-start.1
  303.7 0.9 copy.33
  304.6 0.2 copy-done.4
  304.8 0.7 copy.34
  305.5 0.0 copy-done.1
  305.5 0.0 copy-start
  305.5 1.0 copy.35
  306.5 0.6 copy-done
  307.1 1.0 copy.36
  (2 shorter events, 0.0 us)
Async XLA Ops:
  0.7 0.7 copy-start.6
  0.7 0.7 copy-start.8
  0.7 0.7 copy-start.5
  0.7 0.7 copy-start.7
  1.4 0.7 copy-start.9
  1.4 0.7 copy-start.10
  295.9 6.3 %copy-start.2 = (f32[256,1024]{1,0:T(8,128)S(1)}, f32[256,1024]{1,0:T(8,128)}, u32[]{:S(2)}) copy-start(f32[256,1024]{1,0:T(8,128)} %get-tuple-element.20) | copy-start | bytes 3145732
  302.2 1.5 copy-start.3
  303.7 1.1 copy-start.4
  303.7 1.8 copy-start.1
  305.5 1.6 copy-start

commit v2 on v1

--- a/solution.py
+++ b/solution.py
@@ -338,7 +338,57 @@
 MESH = pl.DeviceIdType.MESH
 MIB = 1 << 20
 ROW_OUT, ROW_DOWN, ROW_GAIN, ROW_SHIFT = 3, 4, 5, 9
-CORE = NZ
+GATHER = (
+    ("v", 0, "zyx"), ("o", 0, "zyx"), ("q", 0, "zyx"), ("q", 1, "xzy"),
+    ("o", 1, "zyx"), ("q", 2, "zyx"), ("q", 3, "zxy"), ("u", 0, "yzx"),
+    ("u", 1, "xzy"), ("u", 2, "zyx"), ("u", 3, "zxy"), ("d", 0, "zyx"),
+    ("u", 4, "yzx"), ("u", 5, "zxy"), ("d", 1, "yzx"), ("d", 2, "zxy"),
+    ("u", 6, "zxy"), ("d", 3, "xzy"), ("u", 7, "zxy"), ("d", 4, "yzx"),
+    ("d", 5, "zyx"), ("d", 6, "yzx"), ("d", 7, "xzy"),
+)
+GATHER_STEPS = (
+    (0, 0), (1, 0), (2, 0), (0, 1), (3, 0), (0, 2), (3, 1), (6, 0),
+    (1, 1), (0, 3), (4, 0), (-1, 0), (2, 1), (5, 0), (-1, 1), (1, 2),
+    (2, 2), (4, 1), (7, 0), (1, 3), (6, 1), (9, 0), (7, 1), (10, 0),
+    (4, 2), (5, 1), (8, 0), (2, 3), (5, 2), (8, 1), (11, 0), (3, 2),
+    (9, 1), (12, 0), (10, 1), (13, 0), (4, 3), (12, 1), (15, 0), (6, 2),
+    (7, 2), (9, 2), (11, 1), (14, 0), (13, 1), (16, 0), (10, 2), (14, 1),
+    (17, 0), (15, 1), (18, 0), (5, 3), (8, 2), (3, 3), (6, 3), (-1, 2),
+    (-1, 3), (17, 1), (20, 0), (11, 2), (9, 3), (16, 1), (12, 2), (19, 0),
+    (-1, 4), (10, 3), (13, 2), (18, 1), (21, 0), (-1, 5), (7, 3), (15, 2),
+    (19, 1), (22, 0), (-1, 6), (14, 2), (20, 1), (21, 1), (8, 3), (-1, 7),
+    (11, 3), (16, 2), (17, 2), (22, 1), (-1, 8), (13, 3), (18, 2), (15, 3),
+    (19, 2), (-1, 9), (12, 3), (-1, 10), (-1, 11), (-1, 12), (-1, 13), (20, 2),
+    (-1, 14), (21, 2), (-1, 15), (22, 2), (14, 3), (16, 3), (-1, 16), (18, 3),
+    (-1, 17), (-1, 18), (17, 3), (-1, 19), (19, 3), (20, 3), (-1, 20), (22, 3),
+    (21, 3), (-1, 21),
+)
+SCATTER = (
+    ("d", 0, "yzx"), ("d", 1, "xzy"), ("d", 2, "yzx"), ("d", 3, "xzy"),
+    ("d", 4, "xzy"), ("d", 5, "xzy"), ("u", 0, "yxz"), ("u", 1, "yxz"),
+    ("u", 2, "yzx"), ("d", 6, "yxz"), ("d", 7, "yxz"), ("u", 3, "xzy"),
+    ("o", 0, "yxz"), ("u", 4, "xyz"), ("q", 0, "xzy"), ("u", 5, "xyz"),
+    ("o", 1, "yxz"), ("q", 1, "xyz"), ("u", 6, "yxz"), ("u", 7, "yxz"),
+    ("q", 2, "xyz"), ("q", 3, "xyz"), ("q", 4, "yxz"), ("q", 5, "yxz"),
+    ("v", 0, "xyz"),
+)
+SCATTER_STEPS = (
+    (-1, 0), (0, 0), (1, 0), (2, 0), (3, 0), (-1, 1), (4, 0), (5, 0),
+    (-1, 2), (-1, 3), (-1, 4), (6, 0), (7, 0), (-1, 5), (0, 1), (2, 1),
+    (8, 0), (10, 0), (-1, 6), (-1, 7), (-1, 8), (1, 1), (3, 1), (9, 0),
+    (11, 0), (4, 1), (5, 1), (13, 0), (-1, 9), (0, 2), (-1, 10), (2, 2),
+    (0, 3), (6, 1), (7, 1), (11, 1), (12, 0), (15, 0), (19, 0), (-1, 11),
+    (2, 3), (8, 1), (10, 1), (13, 1), (16, 0), (18, 0), (-1, 12), (9, 1),
+    (-1, 13), (6, 2), (7, 2), (-1, 14), (1, 2), (-1, 15), (3, 2), (14, 0),
+    (10, 2), (17, 0), (-1, 16), (4, 2), (9, 2), (5, 2), (15, 1), (21, 0),
+    (-1, 17), (1, 3), (23, 0), (-1, 18), (3, 3), (13, 2), (-1, 19), (4, 3),
+    (5, 3), (6, 3), (7, 3), (12, 1), (14, 1), (17, 1), (10, 3), (11, 2),
+    (19, 1), (8, 2), (9, 3), (15, 2), (12, 2), (13, 3), (16, 1), (11, 3),
+    (18, 1), (8, 3), (20, 0), (21, 1), (19, 2), (22, 0), (24, 0), (17, 2),
+    (23, 1), (14, 2), (21, 2), (15, 3), (16, 2), (12, 3), (24, 1), (14, 3),
+    (18, 2), (22, 1), (19, 3), (24, 2), (17, 3), (23, 2), (20, 1), (22, 2),
+    (24, 3), (21, 3), (16, 3), (20, 2), (18, 3), (23, 3), (22, 3), (20, 3),
+)
 
 
 def dot_nn(a, b):
@@ -402,10 +452,10 @@
         self.unsent.append(copy)
         return copy
 
-    def drain(self):
+    def drain(self, waited):
         for copy in self.unsent:
-            copy.wait_send()
-        self.unsent = []
+            if not any(copy is other for other in waited):
+                copy.wait_send()
 
     def sibling(self, src, dst):
         return self.send(src, dst, self.sem(), self.peers("c")[0])
@@ -422,119 +472,135 @@
         pl.semaphore_wait(barrier, count)
 
 
-def gather_stages(net, ref, rows, lanes, order):
-    def at(z, y, x):
-        return ref.at[z, y, x, rows, lanes]
-
-    def place(**given):
-        where = {"z": net.z, "y": net.y, "x": net.x}
+def await_bytes(view, sem):
+    pltpu.make_async_copy(view, view, sem).wait()
+
+
+def view_of(net, ref, lanes, **given):
+    where = {"z": net.z, "y": net.y, "x": net.x}
+    where.update(given)
+    return ref.at[where["z"], where["y"], where["x"], :, lanes]
+
+
+ALL = slice(None)
+
+
+def gather_stages(net, ref, lanes, order):
+    first, second, third = order
+    others = {"z": pl.ds(0, NZ - 1), "y": 1 - net.y, "x": 1 - net.x}
+    got_first, got_second, got_near, got_far = net.sem(), net.sem(), net.sem(), net.sem()
+
+    def pass_on(dim, sem, **held):
+        blocks = view_of(net, ref, lanes, **held)
+        for peer in net.peers(dim):
+            net.send(blocks, blocks, sem, peer)
+
+    def start():
+        pass_on(first, got_first)
+
+    def after_first():
+        await_bytes(view_of(net, ref, lanes, **{first: others[first]}), got_first)
+        pass_on(second, got_second, **{first: ALL})
+        pass_on(third, got_near, **{first: ALL})
+
+    def after_second():
+        held = {first: ALL, second: others[second]}
+        await_bytes(view_of(net, ref, lanes, **held), got_second)
+        if second == "z":
+            for peer in net.peers("z"):
+                pass_on(third, got_far, **{first: ALL, "z": peer[1]})
+        else:
+            pass_on(third, got_far, **held)
+
+    def finish():
+        held = {first: ALL, third: others[third]}
+        await_bytes(view_of(net, ref, lanes, **held), got_near)
+        held[second] = others[second]
+        await_bytes(view_of(net, ref, lanes, **held), got_far)
+
+    return start, after_first, after_second, finish
+
+
+def scatter_stages(net, ref, lanes, order, bufs, done):
+    first, second, third = order
+    wide, half, line = bufs
+    got_wide, got_half, got_line = net.sem(), net.sem(), net.sem()
+    dtype = wide.dtype
+    rows, cols = wide.shape[-2:]
+    step = min(rows, max(16, 32768 // cols))
+    size = {"z": NZ, "y": 2, "x": 2}
+    place = {"z": 0, "y": 1, "x": 2}
+    mine = {"z": net.z, "y": net.y, "x": net.x}
+
+    def coordinate(dim, peer):
+        return peer[1 + place[dim]]
+
+    def block_add(target, sources):
+        for part in range(rows // step):
+            here = pl.ds(part * step, step)
+            total = ref[(*target, here, lanes)].astype(F32)
+            for buf, at in sources:
+                total = total + buf[(*at, here)].astype(F32)
+            ref[(*target, here, lanes)] = total.astype(dtype)
+
+    def target_of(**given):
+        where = dict(mine)
         where.update(given)
-        return at(where["z"], where["y"], where["x"])
-
-    every = {"z": slice(None), "y": slice(None), "x": slice(None)}
-    first, second, third = order
-    got_first, got_second, got_near, got_far = net.sem(), net.sem(), net.sem(), net.sem()
+        return (where["z"], where["y"], where["x"])
 
     def start():
         for peer in net.peers(first):
-            net.send(place(), place(), got_first, peer)
-
-    def await_bytes(view, sem):
-        pltpu.make_async_copy(view, view, sem).wait()
-
-    def after_first():
-        if first == "z":
-            await_bytes(ref.at[pl.ds(0, NZ - 1), net.y, net.x, rows, lanes], got_first)
-        else:
-            await_bytes(place(), got_first)
-        held = {first: every[first]}
-        for peer in net.peers(second):
-            net.send(place(**held), place(**held), got_second, peer)
-        for peer in net.peers(third):
-            net.send(place(**held), place(**held), got_near, peer)
-
-    def after_second():
-        held = {first: every[first]}
-        other = {"x": {"x": 1 - net.x}, "y": {"y": 1 - net.y}}[second]
-        await_bytes(place(**held, **other), got_second)
-        for peer in net.peers(third):
-            net.send(place(**held, **other), place(**held, **other), got_far, peer)
-
-    def finish():
-        held = {first: every[first]}
-        other = {"x": {"x": 1 - net.x}, "y": {"y": 1 - net.y}}[third]
-        await_bytes(place(**held, **other), got_near)
-        await_bytes(place(**held, **other), got_far)
-
-    return start, after_first, after_second, finish
-
-
-def scatter_stages(net, ref, rows, lanes, order, bufs, done):
-    wide, half, line = bufs
-    first, second = order[0], order[1]
-    got_wide, got_half, got_line = net.sem(), net.sem(), net.sem()
-    dtype = wide.dtype
-    step = min(32, wide.shape[2])
-    steps = wide.shape[2] // step
-
-    def await_bytes(view, sem):
-        pltpu.make_async_copy(view, view, sem).wait()
-
-    def row_slice(part):
-        return pl.ds(rows.start + part * step, step)
-
-    def start():
-        peer = net.peers(first)[0]
-        if first == "x":
-            src = ref.at[:, :, 1 - net.x, rows, lanes]
-        else:
-            src = ref.at[:, 1 - net.y, :, rows, lanes]
-        net.send(src, wide, got_wide, peer)
+            there = {"z": ALL, "y": ALL, "x": ALL, first: coordinate(first, peer)}
+            net.send(view_of(net, ref, lanes, **there), wide.at[peer[0] - 1], got_wide, peer)
 
     def after_first():
         await_bytes(wide, got_wide)
-
-        def add(a, b):
-            y, x = (b, net.x) if first == "x" else (net.y, b)
-            for part in range(steps):
-                kept = ref[a, y, x, row_slice(part), lanes].astype(F32)
-                come = wide[a, b, pl.ds(part * step, step), :].astype(F32)
-                ref[a, y, x, row_slice(part), lanes] = (kept + come).astype(dtype)
-
-        gone = 1 - net.y if first == "x" else 1 - net.x
-        loop(NZ, lambda a: add(a, gone))
-        if first == "x":
-            src = ref.at[:, 1 - net.y, net.x, rows, lanes]
-        else:
-            src = ref.at[:, net.y, 1 - net.x, rows, lanes]
-        net.send(src, half, got_half, net.peers(second)[0])
-        loop(NZ, lambda a: add(a, 1 - gone))
+        left = [dim for dim in "zyx" if dim != first]
+
+        def add(second_at, third_at):
+            at = {second: second_at, third: third_at}
+            place_in = (0, at[left[0]], at[left[1]])
+            block_add(target_of(**at), [(wide, place_in)])
+
+        for peer in net.peers(second):
+            gone = coordinate(second, peer)
+            loop(size[third], lambda other: add(gone, other))
+            blocks = view_of(net, ref, lanes, **{second: gone, third: ALL})
+            net.send(blocks, half.at[peer[0] - 1], got_half, peer)
+        loop(size[third], lambda other: add(mine[second], other))
 
     def after_second():
         await_bytes(half, got_half)
-
-        def add(a):
-            for part in range(steps):
-                kept = ref[a, net.y, net.x, row_slice(part), lanes].astype(F32)
-                come = half[a, pl.ds(part * step, step), :].astype(F32)
-                ref[a, net.y, net.x, row_slice(part), lanes] = (kept + come).astype(dtype)
-
-        loop(NZ, add)
-        for peer in net.peers("z"):
-            net.send(
-                ref.at[peer[1], net.y, net.x, rows, lanes], line.at[peer[0] - 1], got_line, peer
+        for peer in net.peers(third):
+            gone = coordinate(third, peer)
+            block_add(
+                target_of(**{third: gone}), [(half, (k, gone)) for k in range(size[second] - 1)]
             )
+            blocks = view_of(net, ref, lanes, **{third: gone})
+            net.send(blocks, line.at[peer[0] - 1], got_line, peer)
 
     def finish():
         await_bytes(line, got_line)
-        for part in range(steps):
+        for part in range(rows // step):
             here = pl.ds(part * step, step)
-            total = ref[net.z, net.y, net.x, row_slice(part), lanes].astype(F32)
-            for k in range(NZ - 1):
-                total = total + line[k, here, :].astype(F32)
+            total = ref[(*target_of(), here, lanes)].astype(F32)
+            for k in range(size[second] - 1):
+                total = total + half[k, mine[third], here].astype(F32)
+            for k in range(size[third] - 1):
+                total = total + line[k, here].astype(F32)
             done(part * step, step, total)
 
     return start, after_first, after_second, finish
+
+
+def pieces_of(plan, widths):
+    counts = {}
+    for group, _, _ in plan:
+        counts[group] = counts.get(group, 0) + 1
+    return [
+        (group, index * (widths[group] // counts[group]), widths[group] // counts[group], order)
+        for group, index, order in plan
+    ]
 
 
 def layer_kernel(
@@ -545,7 +611,12 @@
     wo_in,
     wu_in,
     wd_in,
-    vec_in,
+    qv_in,
+    up_in,
+    out_in,
+    down_in,
+    gain_in,
+    shift_in,
     res_out,
     gtok_out,
     gq_out,
@@ -558,6 +629,7 @@
     wu,
     wd,
     vbuf,
+    pack,
     vecs,
     vq,
     vu,
@@ -593,11 +665,7 @@
     gvecs,
     gv,
     vother,
-    r_q,
-    r_o,
-    r_u,
-    r_d,
-    r_v,
+    piece_bufs,
     st_q,
     st_o,
     st_u,
@@ -605,7 +673,6 @@
     sems,
     local_sems,
 ):
-    (rq_a, rq_b), (ro_a, ro_b), (ru_a, ru_b), (rd_a, rd_b) = r_q, r_o, r_u, r_d
     net = Net(sems)
     core = net.core
     me = (net.z, net.y, net.x)
@@ -632,63 +699,55 @@
             wu.at[net.z, net.y, net.x, :, pl.ds(i * 128, 128)],
         )
     fetch(wd_in.at[pl.ds(mul(core, 128), 128), :], wd.at[net.z, net.y, net.x])
-    vbuf[net.z, net.y, net.x] = vec_in[...]
+    pack[...] = jnp.zeros_like(pack)
+    pack[0:1, :] = qv_in[...].astype(F32)
+    pack[1:3, :] = up_in[...].astype(F32)
+    for row, ref in (
+        (ROW_OUT, out_in),
+        (ROW_DOWN, down_in),
+        (ROW_GAIN, gain_in),
+        (ROW_SHIFT, shift_in),
+    ):
+        value = ref[...].astype(F32)
+        rows = slice(row, row + value.shape[0])
+        pack[rows, 0:64] = jnp.where(net.x == 0, value, 0.0)
+        pack[rows, 64:128] = jnp.where(net.x == 1, value, 0.0)
+    vbuf[net.z, net.y, net.x] = pack[...].astype(BF)
     wo_own = wo.at[core]
-
-    full = slice(None)
-    pieces = [gather_stages(net, vbuf, full, full, "zyx")]
-    for ref, size in ((wq, 64), (wo_own, 64), (wu, 64), (wd, 128)):
-        half = size // 2
-        pieces.append(gather_stages(net, ref, pl.ds(0, half), full, "zyx"))
-        pieces.append(gather_stages(net, ref, pl.ds(half, half), full, "zxy"))
+    plan = pieces_of(GATHER, {"v": 128, "q": 3 * OWN, "o": OWN, "u": HID, "d": WIDTH})
+    sources = {"v": vbuf, "q": wq, "o": wo_own, "u": wu, "d": wd}
+    gathers = [
+        gather_stages(net, sources[group], pl.ds(lane0, count), order)
+        for group, lane0, count, order in plan
+    ]
     net.barrier()
-    pieces[0][0]()
-    ready = (0, 0, 0, 3, 3, 4, 4, 20, 20)
-    landed = 0
-    for piece, first in zip(pieces[1:], ready[1:], strict=True):
-        need = {0: 3, 3: 4, 4: 20, 20: 21}[first]
-        while landed < need:
-            locals_[landed].wait()
-            landed += 1
-        piece[0]()
-
-    events = [(0, 1), (0, 2), (0, 3)]
-    for slot in range(1, len(pieces) + 4):
-        for stage in (3, 2, 1):
-            first = slot - 2 * (stage - 1)
-            if first >= 1 and first < len(pieces) and first % 2 == 1:
-                events.append((first, stage))
-                events.append((first + 1, stage))
-    state = {"at": 0}
-
-    def pump(count):
-        for _ in range(count):
-            if state["at"] < len(events):
-                piece, stage = events[state["at"]]
-                pieces[piece][stage]()
-                state["at"] += 1
-
-    def pump_until(piece):
-        last = max(events.index((p, 3)) for p in piece)
-        while state["at"] <= last:
-            pump(1)
-
-    pump(3)
-
-    for z in range(NZ):
+    ready = {"v": 0, "q": 3, "o": 4, "u": 20, "d": 21}
+    state = {"landed": 0}
+
+    def gather(piece, stage):
+        if stage == 0:
+            while state["landed"] < ready[plan[piece][0]]:
+                locals_[state["landed"]].wait()
+                state["landed"] += 1
+        gathers[piece][stage]()
+
+    def spread_vectors():
+        for z in range(NZ):
+            for y in range(2):
+                both = vbuf[z, y, 0].astype(F32) + vbuf[z, y, 1].astype(F32)
+                vecs[:, pl.ds((z * 2 + y) * 128, 128)] = both
         for y in range(2):
-            both = vbuf[z, y, 0].astype(F32) + vbuf[z, y, 1].astype(F32)
-            vecs[:, pl.ds((z * 2 + y) * 128, 128)] = both
-    for y in range(2):
-        for x in range(2):
-            at = pl.ds((y * 2 + x) * 128, 128)
-            vq[0:8, at] = vbuf[core, y, x].astype(F32)[0:8]
-            vq[8:16, at] = vbuf[core + 2, y, x].astype(F32)[0:8]
-            for z in range(NZ):
-                block = vbuf[z, y, x].astype(F32)
-                vu[0:1, pl.ds((z * 4 + y * 2 + x) * 128, 128)] = jnp.where(
-                    core == 0, block[1:2], block[2:3]
-                )
+            for x in range(2):
+                at = pl.ds((y * 2 + x) * 128, 128)
+                vq[0:8, at] = vbuf[core, y, x].astype(F32)[0:8]
+                vq[8:16, at] = vbuf[core + 2, y, x].astype(F32)[0:8]
+                for z in range(NZ):
+                    block = vbuf[z, y, x].astype(F32)
+                    vu[0:1, pl.ds((z * 4 + y * 2 + x) * 128, 128)] = jnp.where(
+                        core == 0, block[1:2], block[2:3]
+                    )
+        acc[...] = jnp.zeros_like(acc)
+        acc_up[...] = jnp.zeros_like(acc_up)
 
     def gain(n):
         return vecs[ROW_GAIN + n : ROW_GAIN + n + 1, :]
@@ -700,8 +759,7 @@
         parts = value.reshape(value.shape[0] // 8, 8, value.shape[1])
         acc[row] += jnp.sum(parts, axis=0)
 
-    acc[...] = jnp.zeros_like(acc)
-    acc_up[...] = jnp.zeros_like(acc_up)
+    got = {}
 
     chunk = 32
     chunks = LEN // chunk
@@ -711,10 +769,9 @@
         hat, _ = normalize(tok[here, :].astype(F32))
         xin[core, here, :] = (hat * gain(0) + shift(0)).astype(BF)
 
-    loop(chunks, ln0)
-    got_x = net.sibling(xin.at[core], xin.at[core])
-    pump(2)
-    got_x.wait_recv()
+    def attention_input():
+        loop(chunks, ln0)
+        got["x"] = net.sibling(xin.at[core], xin.at[core])
 
     ends = []
     end = jnp.int32(0)
@@ -728,7 +785,6 @@
             total = total + (position >= value).astype(jnp.int32)
         return total
 
-    pump_until((1, 2))
     scale = 1.0 / (ALPHA * 8.0)
 
     def project(t):
@@ -750,8 +806,9 @@
         part(1, kb, None, None)
         part(2, vb, 8, None)
 
-    loop(4, project)
-    pump(2)
+    def projections():
+        got["x"].wait_recv()
+        loop(4, project)
 
     lane = lax.broadcasted_iota(jnp.int32, (1, 128), 1)
     block = 128
@@ -782,16 +839,12 @@
             att[rows, at] = out
             attb[rows, at] = out.astype(BF)
 
-    loop(2, attend)
-    pump(2)
-    loop(2, lambda i: attend(i + 2))
     other_rows = pl.ds(mul(1 - core, LEN), LEN)
     own_rows = pl.ds(mul(core, LEN), LEN)
-    got_att = net.sibling(attb.at[other_rows, :], attx)
-    pump_until((3, 4))
-    got_wo = net.sibling(wo_own, wo.at[core])
-    got_att.wait_recv()
-    got_wo.wait_recv()
+
+    def attend_last():
+        attend(3)
+        got["att"] = net.sibling(attb.at[other_rows, :], attx)
 
     def branch_tile(n):
         lanes = pl.ds(mul(n % 2, 256), 256)
@@ -800,7 +853,12 @@
         at = pl.ds(mul(n, 256), 256)
         own[:, at] = dot_nn(attb[own_rows, :], mine) + dot_nn(attx[...], theirs)
 
-    loop(4, branch_tile)
+    def branch_all():
+        got["wo"] = net.sibling(wo_own, wo.at[core])
+        got["att"].wait_recv()
+        loop(2, lambda i: branch_tile(core * 2 + i))
+        got["wo"].wait_recv()
+        loop(2, lambda i: branch_tile((1 - core) * 2 + i))
 
     def ln12(i):
         here = pl.ds(mul(i, chunk), chunk)
@@ -814,11 +872,9 @@
         inv2[here, :] = jnp.broadcast_to(second_inv, (chunk, 128))
         fin[core, here, :] = (second * gain(2) + shift(2)).astype(BF)
 
-    loop(chunks, ln12)
-    got_fin = net.sibling(fin.at[core], fin.at[core])
-    pump(2)
-    got_fin.wait_recv()
-    pump_until((5, 6))
+    def norms_12():
+        loop(chunks, ln12)
+        got["fin"] = net.sibling(fin.at[core], fin.at[core])
 
     root = math.sqrt(2.0 / math.pi)
 
@@ -836,23 +892,42 @@
         slope = 0.5 * u * (1.0 - inner * inner) * (root * (1.0 + (3 * 0.044715) * square))
         dge[rows, at] = (half + slope).astype(BF)
 
-    loop(8, up_tile)
-    pump(2)
-    loop(8, lambda i: up_tile(i + 8))
-    pump(len(events))
-
-    def down_tile(rows, dst):
-        def body(n):
-            at = pl.ds(mul(n, 256), 256)
-            weight = wd[:, :, :, :, at].reshape(HID, 256)
-            dst[:, at] = dot_nn(act[rows, :], weight)
-
-        loop(4, body)
-
-    down_tile(other_rows, snd)
-    got_part = net.sibling(snd, rcv)
-    down_tile(own_rows, own)
-    got_part.wait_recv()
+    def up_piece(lane0, count):
+        tiles = 2 * count // 256
+        loop(tiles, lambda i: up_tile(i + 2 * lane0 // 256))
+
+    got_parts = []
+
+    def down_piece(lane0, count):
+        at = pl.ds(lane0, count)
+        weight = wd[:, :, :, :, at].reshape(HID, count)
+        snd[:, at] = dot_nn(act[other_rows, :], weight)
+        got_parts.append(net.sibling(snd.at[:, at], rcv.at[:, at]))
+        own[:, at] = dot_nn(act[own_rows, :], weight)
+
+    def tiles_of(width, count, body):
+        return [functools.partial(body, lane0, count) for lane0 in range(0, width, count)]
+
+    steps = [
+        spread_vectors,
+        attention_input,
+        projections,
+        lambda: loop(1, attend),
+        lambda: loop(1, lambda i: attend(i + 1)),
+        lambda: loop(1, lambda i: attend(i + 2)),
+        attend_last,
+        branch_all,
+        norms_12,
+        lambda: got["fin"].wait_recv(),
+    ]
+    steps += tiles_of(HID, 256, up_piece) + tiles_of(WIDTH, 256, down_piece)
+    for piece, stage in GATHER_STEPS:
+        if piece < 0:
+            steps[stage]()
+        else:
+            gather(piece, stage)
+    for part in got_parts:
+        part.wait_recv()
 
     filled = ends[-1]
 
@@ -873,89 +948,81 @@
         accumulate(ROW_SHIFT + 3, upstream)
         accumulate(ROW_DOWN, grad.astype(F32))
 
-    loop(chunks, top_tile)
-    got_gff = net.sibling(gff.at[core], gff.at[core])
+    parts = 2
+    got_gff = []
+    for part in range(parts):
+        loop(chunks // parts, lambda i: top_tile(i + part * (chunks // parts)))
+        rows = pl.ds(part * (LEN // parts), LEN // parts)
+        got_gff.append(net.sibling(gff.at[core, rows], gff.at[core, rows]))
 
     out_copies = []
 
-    def deliver(stage, out_views):
-        for src, dst in out_views:
-            copy = pltpu.make_async_copy(src, dst, local_sems.at[21 + len(out_copies)])
-            copy.start()
-            out_copies.append((copy, net.sibling(src, dst)))
-
-    def store_to(stage, row0):
-        def done(offset, size, total):
-            stage[row0 + offset : row0 + offset + size, :] = total
+    def deliver(src, dst):
+        copy = pltpu.make_async_copy(src, dst, local_sems.at[21 + len(out_copies)])
+        copy.start()
+        out_copies.append((copy, net.sibling(src, dst)))
+
+    def ship(group, lane0, count):
+        if group == "d":
+            at = pl.ds(lane0, count)
+            deliver(st_d.at[:, at], gd_out.at[pl.ds(mul(core, 128), 128), at])
+        if group == "u":
+            for i in range(lane0 // 128, (lane0 + count) // 128):
+                deliver(
+                    st_u.at[:, pl.ds(i * 128, 128)],
+                    gu_out.at[:, lanes_of(i * 256 + core * 128, 128)],
+                )
+        if group == "o":
+            deliver(
+                st_o.at[:, pl.ds(lane0, count)], go_out.at[:, lanes_of(core * OWN + lane0, count)]
+            )
+        if group == "q":
+            start = (lane0 // OWN) * WIDTH + lane0 % OWN
+            deliver(
+                st_q.at[:, pl.ds(lane0, count)], gq_out.at[:, lanes_of(core * OWN + start, count)]
+            )
+
+    plan = pieces_of(SCATTER, {"d": WIDTH, "u": HID, "o": OWN, "q": 3 * OWN, "v": 128})
+    sums = {"d": gd, "u": gu, "o": wu, "q": wu, "v": gv}
+    stage_of = {"d": st_d, "u": st_u, "o": st_o, "q": st_q, "v": gvec_out}
+
+    def store_to(stage, lane0, count):
+        def done(row0, size, total):
+            stage[row0 : row0 + size, lane0 : lane0 + count] = total
 
         return done
 
-    wgrad = {}
-    for name, ref, lanes, size, bufs, stage in (
-        ("d", gd, full, 128, (rd_a, rd_b), st_d),
-        ("u", gu, full, 64, (ru_a, ru_b), st_u),
-        ("o", wu, pl.ds(3 * OWN, OWN), 64, (ro_a, ro_b), st_o),
-        ("q", wu, pl.ds(0, 3 * OWN), 64, (rq_a, rq_b), st_q),
-    ):
-        half = size // 2
-        wgrad[name] = [
-            scatter_stages(net, ref, pl.ds(0, half), lanes, "xyz", bufs[0], store_to(stage, 0)),
+    scatters = []
+    for (group, lane0, count, order), bufs in zip(plan, piece_bufs, strict=True):
+        base = 3 * OWN if group == "o" else 0
+        scatters.append(
             scatter_stages(
-                net, ref, pl.ds(half, half), lanes, "yxz", bufs[1], store_to(stage, half)
-            ),
-        ]
-
-    def ship(name, half):
-        def views():
-            if name == "d":
-                rows = pl.ds(pl.multiple_of(core * 128 + half * 64, 64), 64)
-                return [(st_d.at[half * 64 : half * 64 + 64, :], gd_out.at[rows, :])]
-            rows = slice(half * 32, half * 32 + 32)
-            if name == "u":
-                return [
-                    (
-                        st_u.at[rows, pl.ds(i * 128, 128)],
-                        gu_out.at[rows, lanes_of(i * 256 + core * 128, 128)],
-                    )
-                    for i in range(NZ * 4)
-                ]
-            if name == "o":
-                return [(st_o.at[rows, :], go_out.at[rows, lanes_of(core * OWN, OWN)])]
-            return [
-                (
-                    st_q.at[rows, pl.ds(p * OWN, OWN)],
-                    gq_out.at[rows, lanes_of(p * WIDTH + core * OWN, OWN)],
-                )
-                for p in range(3)
-            ]
-
-        deliver(None, views())
-
-    queue = []
-
-    def launch(name):
-        for half in range(2):
-            wgrad[name][half][0]()
-
-    def relay(name, stage):
-        for half in range(2):
-            wgrad[name][half][stage]()
-            if stage == 3:
-                ship(name, half)
-
-    got_gff.wait_recv()
-
-    def gdown_tile(t):
-        k = t // 2
-        z = k // 2
-        y = k % 2
-        at = pl.ds(mul(t % 2, 512), 512)
-        left = act[:, pl.ds(mul(k, 256), 256)]
-        grad = gff[:, :, at].reshape(NPOS, 512)
-        gd[z, y, :, :, at] = dot_tn(left, grad).astype(BF).reshape(2, 128, 512)
-
-    loop(16, gdown_tile)
-    launch("d")
+                net,
+                sums[group],
+                pl.ds(base + lane0, count),
+                order,
+                bufs,
+                store_to(stage_of[group], lane0, count),
+            )
+        )
+
+    def scatter(piece, stage):
+        scatters[piece][stage]()
+        if stage == 3:
+            ship(*plan[piece][:3])
+
+    for part in got_gff:
+        part.wait_recv()
+
+    def gdown_piece(lane0, count):
+        at = pl.ds(lane0, count)
+
+        def tile(k):
+            left = act[:, pl.ds(mul(k, 256), 256)]
+            grad = gff[:, :, at].reshape(NPOS, count)
+            gd[k // 2, k % 2, :, :, at] = dot_tn(left, grad).astype(BF).reshape(2, 128, count)
+
+        loop(8, tile)
 
     def gpre_tile(t):
         k = t // 2
@@ -968,18 +1035,14 @@
         dge[rows, at] = value
         acc_up[:, at] += jnp.sum(value.astype(F32).reshape(32, 8, 256), axis=0)
 
-    loop(16, gpre_tile)
-
-    def gup_tile(t):
-        z = t // 4
-        at = pl.ds(mul(t % 4, 512), 512)
-        left = fin[:, :, pl.ds(mul(z, 256), 256)].reshape(NPOS, 256)
-        gu[z, :, :, :, at] = dot_tn(left, dge[:, at]).astype(BF).reshape(2, 2, 64, 512)
-
-    loop(16, gup_tile)
-    launch("u")
-
-    net.drain()
+    def gup_piece(lane0, count):
+        at = pl.ds(lane0, count)
+
+        def tile(z):
+            left = fin[:, :, pl.ds(mul(z, 256), 256)].reshape(NPOS, 256)
+            gu[z, :, :, :, at] = dot_tn(left, dge[:, at]).astype(BF).reshape(2, 2, 64, count)
+
+        loop(NZ, tile)
 
     def gfi_tile(rows, dst):
         def body(z):
@@ -988,11 +1051,12 @@
 
         loop(NZ, body)
 
-    gfi_tile(other_rows, snd)
-    got_part = net.sibling(snd, rcv)
-    gfi_tile(own_rows, own)
-    relay("d", 1)
-    got_part.wait_recv()
+    def grad_ffn_in():
+        for part in got_parts:
+            part.wait_send()
+        gfi_tile(other_rows, snd)
+        got["gfi"] = net.sibling(snd, rcv)
+        gfi_tile(own_rows, own)
 
     def middle_tile(i):
         here = pl.ds(mul(i, chunk), chunk)
@@ -1009,10 +1073,12 @@
         gbr[core, here, :] = grad
         accumulate(ROW_OUT, grad.astype(F32))
 
-    loop(chunks, middle_tile)
-    got_gbr = net.sibling(gbr.at[core], gbr.at[core])
-    relay("u", 1)
-    got_gbr.wait_recv()
+    def grad_middle():
+        got["gfi"].wait_recv()
+        loop(chunks, middle_tile)
+        for copy in forward_sends:
+            copy.wait_send()
+        got["gbr"] = net.sibling(gbr.at[core], gbr.at[core])
 
     go = wu.at[:, :, :, :, pl.ds(3 * OWN, OWN)]
 
@@ -1027,9 +1093,6 @@
     def put_own(k, value):
         wu[2 * core + k, :, :, :, pl.ds(3 * OWN, OWN)] = value
 
-    loop(2, lambda k: gout_tile(k, lanes_of((1 - core) * OWN, OWN), put_swap))
-    got_swap = net.sibling(swap, go.at[pl.ds(2 * core, 2)])
-    loop(2, lambda k: gout_tile(k, lanes_of(core * OWN, OWN), put_own))
 
     def gatt_tile(t):
         k = t // 2
@@ -1039,9 +1102,13 @@
         value = dot_nt(gbr[m, :, 0:OWN], left) + dot_nt(gbr[m, :, OWN:WIDTH], right)
         dob[pl.ds(mul(m, 256), 256), pl.ds(mul(k, 256), 256)] = value.astype(BF)
 
-    loop(4, gatt_tile)
-    got_swap.wait_recv()
-    launch("o")
+    def grad_out():
+        got["gbr"].wait_recv()
+        loop(2, lambda k: gout_tile(k, lanes_of((1 - core) * OWN, OWN), put_swap))
+        got_swap = net.sibling(swap, go.at[pl.ds(2 * core, 2)])
+        loop(2, lambda k: gout_tile(k, lanes_of(core * OWN, OWN), put_own))
+        loop(4, gatt_tile)
+        got_swap.wait_recv()
 
     def attend_back(pair):
         at = pl.ds(mul(pair, 128), 128)
@@ -1083,23 +1150,15 @@
         acc_qv[0, :, at] = total_q
         acc_qv[1, :, at] = total_v
 
-    loop(1, attend_back)
-    relay("d", 2)
-    loop(1, lambda i: attend_back(i + 1))
-    loop(1, lambda i: attend_back(i + 2))
-    relay("u", 2)
-    loop(1, lambda i: attend_back(i + 3))
-    relay("o", 1)
-
-    def gqkv_tile(z):
-        left = xin[:, :, pl.ds(mul(z, 256), 256)].reshape(NPOS, 256)
-        for part, ref in enumerate((qb, kb, vb)):
-            value = dot_tn(left, ref[...]).astype(BF)
-            wu[z, :, :, :, pl.ds(part * OWN, OWN)] = value.reshape(2, 2, 64, OWN)
-
-    loop(NZ, gqkv_tile)
-    launch("q")
-    net.drain()
+    def gqkv_piece(lane0, count):
+        ref = (qb, kb, vb)[lane0 // OWN]
+
+        def tile(z):
+            left = xin[:, :, pl.ds(mul(z, 256), 256)].reshape(NPOS, 256)
+            value = dot_tn(left, ref[:, lane0 % OWN : lane0 % OWN + count]).astype(BF)
+            wu[z, :, :, :, pl.ds(lane0, count)] = value.reshape(2, 2, 64, count)
+
+        loop(NZ, tile)
 
     def gai_tile(rows, dst):
         def body(z):
@@ -1112,12 +1171,11 @@
 
         loop(NZ, body)
 
-    gai_tile(other_rows, snd)
-    got_part = net.sibling(snd, rcv)
-    gai_tile(own_rows, own)
-    relay("d", 3)
-    relay("o", 2)
-    got_part.wait_recv()
+    def grad_attn_in():
+        got["gfi"].wait_send()
+        gai_tile(other_rows, snd)
+        got["gai"] = net.sibling(snd, rcv)
+        gai_tile(own_rows, own)
 
     def bottom_tile(i):
         here = pl.ds(mul(i, chunk), chunk)
@@ -1127,53 +1185,94 @@
         accumulate(ROW_SHIFT, grad_in)
         gtok_out[here, :] = mid[here, :] + norm_back(hat, inv, gain(0), grad_in)
 
-    loop(chunks, bottom_tile)
-
-    for row in range(16):
-        gvecs[row : row + 1, :] = jnp.sum(acc[row], axis=0, keepdims=True)
-    row_id = lax.broadcasted_iota(jnp.int32, (16, 1), 0)
-    for z in range(NZ):
-        for y in range(2):
-            base = gvecs[:, pl.ds((z * 2 + y) * 128, 128)]
-            for x in range(2):
-                at = pl.ds((y * 2 + x) * 128, 128)
-                kind = 0 if z < 2 else 1
-                qv_row = jnp.sum(acc_qv[kind, :, at], axis=0, keepdims=True)
-                qv_row = jnp.where(core == z % 2, qv_row, 0.0)
-                up_at = pl.ds((z * 4 + y * 2 + x) * 128, 128)
-                up_row = jnp.sum(acc_up[:, up_at], axis=0, keepdims=True)
-                value = base + jnp.where(row_id == 0, qv_row, 0.0)
-                gv[z, y, x] = value + jnp.where(row_id == 1 + core, up_row, 0.0)
-
-    def keep_vec(offset, size, total):
-        gvec_out[offset : offset + size, :] = total
-
-    vec = scatter_stages(net, gv, pl.ds(0, 16), full, "xyz", r_v, keep_vec)
-    vec[0]()
-    relay("q", 1)
-    vec[1]()
-    relay("u", 3)
-    vec[2]()
-    relay("o", 3)
-    vec[3]()
+    def bottom():
+        got["gai"].wait_recv()
+        loop(chunks, bottom_tile)
+        for row in range(16):
+            gvecs[row : row + 1, :] = jnp.sum(acc[row], axis=0, keepdims=True)
+        row_id = lax.broadcasted_iota(jnp.int32, (16, 1), 0)
+        for z in range(NZ):
+            for y in range(2):
+                base = gvecs[:, pl.ds((z * 2 + y) * 128, 128)]
+                for x in range(2):
+                    at = pl.ds((y * 2 + x) * 128, 128)
+                    kind = 0 if z < 2 else 1
+                    qv_row = jnp.sum(acc_qv[kind, :, at], axis=0, keepdims=True)
+                    qv_row = jnp.where(core == z % 2, qv_row, 0.0)
+                    up_at = pl.ds((z * 4 + y * 2 + x) * 128, 128)
+                    up_row = jnp.sum(acc_up[:, up_at], axis=0, keepdims=True)
+                    value = base + jnp.where(row_id == 0, qv_row, 0.0)
+                    gv[z, y, x] = value + jnp.where(row_id == 1 + core, up_row, 0.0)
+
+    steps = tiles_of(WIDTH, 512, gdown_piece)
+    steps += [
+        lambda: loop(8, gpre_tile),
+        lambda: loop(8, lambda i: gpre_tile(i + 8)),
+    ]
+    steps += tiles_of(HID, 512, gup_piece)
+    steps += [grad_ffn_in, grad_middle, grad_out]
+    steps += [functools.partial(loop, 1, lambda i, pair=p: attend_back(i + pair)) for p in range(4)]
+    steps += tiles_of(3 * OWN, 512, gqkv_piece)
+    steps += [grad_attn_in, bottom]
+    forward_sends = [
+        copy for copy in net.unsent if not any(copy is part for part in got_parts)
+    ]
+    net.unsent = []
+    for piece, stage in SCATTER_STEPS:
+        if piece < 0:
+            steps[stage]()
+        else:
+            scatter(piece, stage)
     got_vec = net.sibling(gvec_out, vother)
-    relay("q", 2)
-    got_vec.wait()
-    net.unsent = [copy for copy in net.unsent if copy is not got_vec]
+    got_vec.wait_send()
+    got_vec.wait_recv()
     gvec_out[...] = gvec_out[...] + vother[...]
-    relay("q", 3)
     for copy, remote in out_copies:
         copy.wait()
         remote.wait_recv()
-    net.drain()
-
-
-def scatter_bufs(rows, cols, dtype):
+    net.drain((got["gfi"], got_vec))
+
+
+def scatter_bufs(group, count, order):
+    rows, dtype = {"d": (128, BF), "v": (16, F32)}.get(group, (64, BF))
+    size = {"z": NZ, "y": 2, "x": 2}
+    left = [size[dim] for dim in "zyx" if dim != order[0]]
     return [
-        pltpu.VMEM((NZ, 2, rows, cols), dtype),
-        pltpu.VMEM((NZ, rows, cols), dtype),
-        pltpu.VMEM((NZ - 1, rows, cols), dtype),
+        pltpu.VMEM((size[order[0]] - 1, *left, rows, count), dtype),
+        pltpu.VMEM((size[order[1]] - 1, size[order[2]], rows, count), dtype),
+        pltpu.VMEM((size[order[2]] - 1, rows, count), dtype),
     ]
+
+
+SPLIT = 4
+
+
+def hand_out_kernel(*refs):
+    large, vec = refs[:6], refs[6]
+    outs, small, held, sems = refs[7:13], refs[13:19], refs[19:25], refs[25]
+    arrivals, copies = [], []
+    for src, mid, dst in zip(large, held, outs, strict=True):
+        rows = src.shape[0] // SPLIT
+        for part in range(SPLIT):
+            here = pl.ds(part * rows, rows)
+            at = len(arrivals)
+            arrivals.append(pltpu.make_async_copy(src.at[here], mid.at[here], sems.at[0, at]))
+            copies.append(pltpu.make_async_copy(mid.at[here], dst.at[here], sems.at[1, at]))
+            arrivals[-1].start()
+    right = lax.axis_index("dp") % 2 == 1
+    values = vec[...]
+    half = jnp.where(right, values[:, 64:], values[:, :64])
+    small[0][...] = values[0:1]
+    small[1][...] = half[ROW_OUT : ROW_OUT + 1]
+    small[2][...] = values[1:3]
+    small[3][...] = half[ROW_DOWN : ROW_DOWN + 1]
+    small[4][...] = half[ROW_GAIN : ROW_GAIN + 4]
+    small[5][...] = half[ROW_SHIFT : ROW_SHIFT + 4]
+    for arrival, copy in zip(arrivals, copies, strict=True):
+        arrival.wait()
+        copy.start()
+    for copy in copies:
+        copy.wait()
 
 
 def fused(
@@ -1191,15 +1290,6 @@
     norm_gain,
     norm_bias,
 ):
-    right = lax.axis_index("dp") % 2 == 1
-    narrow = jnp.concatenate([out_bias[None], down_bias[None], norm_gain, norm_bias], 0)
-    blank = jnp.zeros_like(narrow)
-    wide = jnp.where(
-        right, jnp.concatenate([blank, narrow], 1), jnp.concatenate([narrow, blank], 1)
-    )
-    packed = jnp.concatenate(
-        [qv_bias[None], up_bias.reshape(2, 128), wide, jnp.zeros((3, 128), BF)], 0
-    )
     vmem = pl.BlockSpec(memory_space=pltpu.VMEM)
     anywhere = pl.BlockSpec(memory_space=pl.ANY)
     scratch = [
@@ -1208,6 +1298,7 @@
         pltpu.VMEM((NZ, 2, 2, 64, HID), BF),
         pltpu.VMEM((NZ, 2, 2, 128, WIDTH), BF),
         pltpu.VMEM((NZ, 2, 2, 16, 128), BF),
+        pltpu.VMEM((16, 128), F32),
         pltpu.VMEM((16, WIDTH), F32),
         pltpu.VMEM((16, OWN), F32),
         pltpu.VMEM((8, HID), F32),
@@ -1243,17 +1334,18 @@
         pltpu.VMEM((16, WIDTH), F32),
         pltpu.VMEM((NZ, 2, 2, 16, 128), F32),
         pltpu.VMEM((16, 128), F32),
-        [scatter_bufs(32, 3 * OWN, BF)] * 2,
-        [scatter_bufs(32, OWN, BF)] * 2,
-        [scatter_bufs(32, HID, BF)] * 2,
-        [scatter_bufs(64, WIDTH, BF)] * 2,
-        scatter_bufs(16, 128, F32),
+        [
+            scatter_bufs(group, count, order)
+            for group, _, count, order in pieces_of(
+                SCATTER, {"d": WIDTH, "u": HID, "o": OWN, "q": 3 * OWN, "v": 128}
+            )
+        ],
         pltpu.VMEM((64, 3 * OWN), F32),
         pltpu.VMEM((64, OWN), F32),
         pltpu.VMEM((64, HID), F32),
         pltpu.VMEM((128, WIDTH), F32),
-        pltpu.SemaphoreType.DMA((300,)),
-        pltpu.SemaphoreType.DMA((70,)),
+        pltpu.SemaphoreType.DMA((700,)),
+        pltpu.SemaphoreType.DMA((80,)),
     ]
     outs = pl.pallas_call(
         layer_kernel,
@@ -1268,29 +1360,61 @@
         ],
         in_specs=[vmem, pl.BlockSpec(memory_space=pltpu.SMEM), vmem]
         + [anywhere] * 4
-        + [vmem],
+        + [vmem] * 6,
         out_specs=[vmem, vmem] + [anywhere] * 4 + [vmem],
         scratch_shapes=scratch,
         compiler_params=pltpu.CompilerParams(
             collective_id=0, has_side_effects=True, vmem_limit_bytes=63 * MIB
         ),
         name="layer",
-    )(tokens[0], doc_lengths, cotangent[0], w_qkv, w_out, w_up, w_down, packed)
-    result, grad_inputs, grad_qkv, grad_out, grad_up, grad_down, vec = outs
-    part = jnp.where(right, vec[3:13, 64:], vec[3:13, :64])
+    )(
+        tokens[0],
+        doc_lengths,
+        cotangent[0],
+        w_qkv,
+        w_out,
+        w_up,
+        w_down,
+        qv_bias.reshape(1, 128),
+        up_bias.reshape(2, 128),
+        out_bias.reshape(1, 64),
+        down_bias.reshape(1, 64),
+        norm_gain,
+        norm_bias,
+    )
+    *large, vec = outs
+    done = pl.pallas_call(
+        hand_out_kernel,
+        out_shape=[jax.ShapeDtypeStruct(array.shape, array.dtype) for array in large]
+        + [
+            jax.ShapeDtypeStruct((1, 128), F32),
+            jax.ShapeDtypeStruct((1, 64), F32),
+            jax.ShapeDtypeStruct((2, 128), F32),
+            jax.ShapeDtypeStruct((1, 64), F32),
+            jax.ShapeDtypeStruct((4, 64), F32),
+            jax.ShapeDtypeStruct((4, 64), F32),
+        ],
+        in_specs=[anywhere] * 6 + [vmem],
+        out_specs=[anywhere] * 6 + [vmem] * 6,
+        scratch_shapes=[pltpu.VMEM(array.shape, array.dtype) for array in large]
+        + [pltpu.SemaphoreType.DMA((2, 6 * SPLIT))],
+        name="hand_out",
+    )(*large, vec)
+    result, grad_inputs, grad_qkv, grad_out, grad_up, grad_down = done[:6]
+    grad_qv, grad_out_shift, grad_up_shift, grad_down_shift, grad_gain, grad_shift = done[6:]
     return (
         result[None],
         grad_inputs[None],
         grad_qkv,
-        vec[0],
+        grad_qv.reshape(128),
         grad_out,
-        part[0],
+        grad_out_shift.reshape(64),
         grad_up,
-        vec[1:3].reshape(256),
+        grad_up_shift.reshape(256),
         grad_down,
-        part[1],
-        part[2:6],
-        part[6:10],
+        grad_down_shift.reshape(64),
+        grad_gain,
+        grad_shift,
     )
 
 

time: 309 us -> 254 us (0.82)
  Pallas kernels: 293 us -> 253 us
  local copies, waits for them, and re-layouts: 12.6 us -> 0 us
    pallas_call x1, Pallas kernels: 293 us -> 247 us  [fused(): pl.pallas_call(layer_kernel, out_shape=[jax.ShapeDtypeStruct((LEN, WIDTH)...]
    unnamed x28 -> x0, local copies, waits for them, and re-layouts: 8.92 us -> none
    pallas_call x0 -> x1, Pallas kernels: none -> 6.15 us  [fused(): pl.pallas_call(hand_out_kernel, out_shape=[jax.ShapeDtypeStruct(array.sha...]
where the time goes in v2:
time: 254 us
  Pallas kernels  253 us (100%)
    pallas_call x1, Pallas kernels, fused(): pl.pallas_call(layer_kernel, out_shape=[jax.ShapeDtypeStruct((LEN, WIDTH)...  247 us
    pallas_call x1, Pallas kernels, fused(): pl.pallas_call(hand_out_kernel, out_shape=[jax.ShapeDtypeStruct(array.sha...  6.15 us

profile of v2, /device:TPU:1, one launch (start us, length us, event | category | flops | bytes accessed | tf_op | source)
XLA Modules:
  0.0 253.8 jit_solution(10183351228965217396)
XLA Ops:
  0.6 246.8 %layer.1 = (bf16[256,1024]{1,0:T(8,128)(2,1)}, f32[256,1024]{1,0:T(8,128)}, f32[64,3072]{1,0:T(8,128)}, f32[64,1024]{1,0:T(8,128)}, f32[64,4096]{1,0:T(8,128)}, /*index=5*/f32[256,1024]{1,0:T(8,128)}, f32[16,128]{1,0:T(8,128)}) custom-call(bf16[256,1024]{1,0:T(8,128)(2,1)} %bitcast.12, s32[1,8]{1,0:T(1,128)} %doc.1, bf16[256,1024]{1,0:T(8,128)(2,1)} %bitcast.13, ...), custom_call_target="tpu_custom_call" | custom-call | tf_op jit(solution)/shard_map/layer/pallas_call | solution.py:1350
  247.5 6.2 %hand_out.1 = (bf16[256,1024]{1,0:T(8,128)(2,1)}, f32[256,1024]{1,0:T(8,128)}, f32[64,3072]{1,0:T(8,128)}, f32[64,1024]{1,0:T(8,128)}, f32[64,4096]{1,0:T(8,128)...) custom-call(bf16[256,1024]{1,0:T(8,128)(2,1)} %get-tuple-element.31., ...), custom_call_target="tpu_custom_call" | custom-call | tf_op jit(solution)/shard_map/hand_out/pallas_call | solution.py:1386

commit v3 on v2

--- a/solution.py
+++ b/solution.py
@@ -332,63 +332,50 @@
 LEN = 256
 WIDTH = 1024
 OWN = 512
-HID = 2048
+FF4 = 1024
 BF = jnp.bfloat16
 F32 = jnp.float32
 MESH = pl.DeviceIdType.MESH
 MIB = 1 << 20
 ROW_OUT, ROW_DOWN, ROW_GAIN, ROW_SHIFT = 3, 4, 5, 9
 GATHER = (
-    ("v", 0, "zyx"), ("o", 0, "zyx"), ("q", 0, "zyx"), ("q", 1, "xzy"),
-    ("o", 1, "zyx"), ("q", 2, "zyx"), ("q", 3, "zxy"), ("u", 0, "yzx"),
-    ("u", 1, "xzy"), ("u", 2, "zyx"), ("u", 3, "zxy"), ("d", 0, "zyx"),
-    ("u", 4, "yzx"), ("u", 5, "zxy"), ("d", 1, "yzx"), ("d", 2, "zxy"),
-    ("u", 6, "zxy"), ("d", 3, "xzy"), ("u", 7, "zxy"), ("d", 4, "yzx"),
-    ("d", 5, "zyx"), ("d", 6, "yzx"), ("d", 7, "xzy"),
+    ("v", 0, "zyx"), ("q", 0, "zxy"), ("q", 1, "zyx"), ("q", 2, "zyx"),
+    ("q", 3, "zyx"), ("u", 0, "zy"), ("o", 0, "zyx"), ("d", 0, "zy"),
+    ("u", 1, "zy"), ("d", 1, "zy"), ("u", 2, "zy"), ("d", 2, "yz"),
+    ("u", 3, "yz"), ("d", 3, "zy"),
 )
 GATHER_STEPS = (
-    (0, 0), (1, 0), (2, 0), (0, 1), (3, 0), (0, 2), (3, 1), (6, 0),
-    (1, 1), (0, 3), (4, 0), (-1, 0), (2, 1), (5, 0), (-1, 1), (1, 2),
-    (2, 2), (4, 1), (7, 0), (1, 3), (6, 1), (9, 0), (7, 1), (10, 0),
-    (4, 2), (5, 1), (8, 0), (2, 3), (5, 2), (8, 1), (11, 0), (3, 2),
-    (9, 1), (12, 0), (10, 1), (13, 0), (4, 3), (12, 1), (15, 0), (6, 2),
-    (7, 2), (9, 2), (11, 1), (14, 0), (13, 1), (16, 0), (10, 2), (14, 1),
-    (17, 0), (15, 1), (18, 0), (5, 3), (8, 2), (3, 3), (6, 3), (-1, 2),
-    (-1, 3), (17, 1), (20, 0), (11, 2), (9, 3), (16, 1), (12, 2), (19, 0),
-    (-1, 4), (10, 3), (13, 2), (18, 1), (21, 0), (-1, 5), (7, 3), (15, 2),
-    (19, 1), (22, 0), (-1, 6), (14, 2), (20, 1), (21, 1), (8, 3), (-1, 7),
-    (11, 3), (16, 2), (17, 2), (22, 1), (-1, 8), (13, 3), (18, 2), (15, 3),
-    (19, 2), (-1, 9), (12, 3), (-1, 10), (-1, 11), (-1, 12), (-1, 13), (20, 2),
-    (-1, 14), (21, 2), (-1, 15), (22, 2), (14, 3), (16, 3), (-1, 16), (18, 3),
-    (-1, 17), (-1, 18), (17, 3), (-1, 19), (19, 3), (20, 3), (-1, 20), (22, 3),
-    (21, 3), (-1, 21),
+    (0, 0), (1, 0), (0, 1), (2, 0), (0, 2), (1, 1), (3, 0), (0, 3),
+    (-1, 0), (-1, 1), (2, 1), (4, 0), (1, 2), (3, 1), (5, 0), (7, 0),
+    (4, 1), (6, 0), (2, 2), (5, 1), (10, 0), (10, 1), (12, 0), (1, 3),
+    (3, 2), (4, 2), (7, 1), (8, 0), (9, 0), (12, 1), (2, 3), (8, 1),
+    (12, 2), (6, 1), (7, 2), (3, 3), (4, 3), (-1, 2), (5, 2), (-1, 3),
+    (-1, 4), (6, 2), (10, 2), (-1, 5), (5, 3), (-1, 6), (9, 1), (11, 0),
+    (8, 2), (6, 3), (10, 3), (-1, 7), (-1, 8), (11, 1), (12, 3), (13, 0),
+    (9, 2), (8, 3), (-1, 11), (-1, 12), (-1, 9), (-1, 10), (-1, 13), (13, 1),
+    (-1, 14), (-1, 15), (-1, 16), (11, 2), (-1, 17), (-1, 18), (-1, 19), (13, 2),
+    (-1, 20), (-1, 21), (-1, 22), (-1, 23),
 )
 SCATTER = (
-    ("d", 0, "yzx"), ("d", 1, "xzy"), ("d", 2, "yzx"), ("d", 3, "xzy"),
-    ("d", 4, "xzy"), ("d", 5, "xzy"), ("u", 0, "yxz"), ("u", 1, "yxz"),
-    ("u", 2, "yzx"), ("d", 6, "yxz"), ("d", 7, "yxz"), ("u", 3, "xzy"),
-    ("o", 0, "yxz"), ("u", 4, "xyz"), ("q", 0, "xzy"), ("u", 5, "xyz"),
-    ("o", 1, "yxz"), ("q", 1, "xyz"), ("u", 6, "yxz"), ("u", 7, "yxz"),
-    ("q", 2, "xyz"), ("q", 3, "xyz"), ("q", 4, "yxz"), ("q", 5, "yxz"),
-    ("v", 0, "xyz"),
+    ("d", 0, "zy"), ("d", 1, "yz"), ("o", 0, "xyz"), ("u", 0, "zy"),
+    ("u", 1, "yz"), ("d", 2, "yz"), ("q", 0, "yxz"), ("q", 1, "xyz"),
+    ("q", 2, "xyz"), ("u", 2, "yz"), ("q", 3, "xyz"), ("q", 4, "xyz"),
+    ("q", 5, "yxz"), ("d", 3, "yz"), ("u", 3, "yz"), ("v", 0, "xyz"),
 )
 SCATTER_STEPS = (
-    (-1, 0), (0, 0), (1, 0), (2, 0), (3, 0), (-1, 1), (4, 0), (5, 0),
-    (-1, 2), (-1, 3), (-1, 4), (6, 0), (7, 0), (-1, 5), (0, 1), (2, 1),
-    (8, 0), (10, 0), (-1, 6), (-1, 7), (-1, 8), (1, 1), (3, 1), (9, 0),
-    (11, 0), (4, 1), (5, 1), (13, 0), (-1, 9), (0, 2), (-1, 10), (2, 2),
-    (0, 3), (6, 1), (7, 1), (11, 1), (12, 0), (15, 0), (19, 0), (-1, 11),
-    (2, 3), (8, 1), (10, 1), (13, 1), (16, 0), (18, 0), (-1, 12), (9, 1),
-    (-1, 13), (6, 2), (7, 2), (-1, 14), (1, 2), (-1, 15), (3, 2), (14, 0),
-    (10, 2), (17, 0), (-1, 16), (4, 2), (9, 2), (5, 2), (15, 1), (21, 0),
-    (-1, 17), (1, 3), (23, 0), (-1, 18), (3, 3), (13, 2), (-1, 19), (4, 3),
-    (5, 3), (6, 3), (7, 3), (12, 1), (14, 1), (17, 1), (10, 3), (11, 2),
-    (19, 1), (8, 2), (9, 3), (15, 2), (12, 2), (13, 3), (16, 1), (11, 3),
-    (18, 1), (8, 3), (20, 0), (21, 1), (19, 2), (22, 0), (24, 0), (17, 2),
-    (23, 1), (14, 2), (21, 2), (15, 3), (16, 2), (12, 3), (24, 1), (14, 3),
-    (18, 2), (22, 1), (19, 3), (24, 2), (17, 3), (23, 2), (20, 1), (22, 2),
-    (24, 3), (21, 3), (16, 3), (20, 2), (18, 3), (23, 3), (22, 3), (20, 3),
+    (-1, 0), (-1, 1), (-1, 2), (-1, 3), (-1, 4), (-1, 7), (-1, 8), (-1, 11),
+    (-1, 5), (0, 0), (1, 0), (-1, 12), (-1, 6), (5, 0), (-1, 9), (4, 0),
+    (-1, 10), (1, 1), (3, 0), (0, 1), (-1, 13), (5, 1), (13, 0), (-1, 14),
+    (0, 2), (4, 1), (9, 0), (14, 0), (-1, 15), (2, 0), (-1, 16), (-1, 17),
+    (1, 2), (-1, 18), (-1, 19), (-1, 20), (6, 0), (7, 0), (13, 1), (-1, 21),
+    (8, 0), (-1, 22), (-1, 23), (2, 1), (5, 2), (9, 1), (11, 0), (14, 1),
+    (-1, 24), (4, 2), (3, 1), (6, 1), (12, 0), (7, 1), (3, 2), (15, 0),
+    (4, 3), (2, 2), (13, 2), (8, 1), (10, 0), (3, 3), (9, 2), (6, 2),
+    (14, 2), (15, 1), (7, 2), (11, 1), (8, 2), (12, 1), (9, 3), (14, 3),
+    (15, 2), (2, 3), (10, 1), (11, 2), (12, 2), (6, 3), (7, 3), (10, 2),
+    (15, 3), (8, 3), (11, 3), (12, 3), (10, 3),
 )
+WIDTHS = {"v": 128, "q": 3 * OWN, "o": OWN, "u": FF4, "d": WIDTH}
 
 
 def dot_nn(a, b):
@@ -452,15 +439,16 @@
         self.unsent.append(copy)
         return copy
 
-    def drain(self, waited):
-        for copy in self.unsent:
+    @staticmethod
+    def drain(sends, waited):
+        for copy in sends:
             if not any(copy is other for other in waited):
                 copy.wait_send()
 
     def sibling(self, src, dst):
         return self.send(src, dst, self.sem(), self.peers("c")[0])
 
-    def barrier(self):
+    def greet(self):
         barrier = pltpu.get_barrier_semaphore()
         count = 0
         for dim in "xyzc":
@@ -469,7 +457,7 @@
                     barrier, inc=1, device_id=(self.chip_at(z, y, x), core), device_id_type=MESH
                 )
                 count += 1
-        pl.semaphore_wait(barrier, count)
+        return lambda: pl.semaphore_wait(barrier, count)
 
 
 def await_bytes(view, sem):
@@ -593,6 +581,85 @@
     return start, after_first, after_second, finish
 
 
+def plane_gather_stages(net, ref, lanes, order):
+    first, second = order
+    others = {"z": pl.ds(0, NZ - 1), "y": 1 - net.y}
+    got_first, got_second = net.sem(), net.sem()
+
+    def place(**given):
+        where = {"z": net.z, "y": net.y}
+        where.update(given)
+        return ref.at[where["z"], where["y"], :, lanes]
+
+    def pass_on(dim, sem, **held):
+        for peer in net.peers(dim):
+            net.send(place(**held), place(**held), sem, peer)
+
+    def start():
+        pass_on(first, got_first)
+
+    def after_first():
+        await_bytes(place(**{first: others[first]}), got_first)
+        pass_on(second, got_second, **{first: ALL})
+
+    def finish():
+        await_bytes(place(**{first: ALL, second: others[second]}), got_second)
+
+    return [start, after_first, finish]
+
+
+def plane_scatter_stages(net, ref, lanes, order, bufs, emit):
+    first, second = order
+    wide, line = bufs[:2]
+    got_wide, got_line = net.sem(), net.sem()
+    rows, cols = wide.shape[-2:]
+    step = min(rows, max(16, 32768 // cols))
+    size = {"z": NZ, "y": 2}
+    place = {"z": 1, "y": 2}
+    mine = {"z": net.z, "y": net.y}
+
+    def at(**given):
+        where = dict(mine)
+        where.update(given)
+        return (where["z"], where["y"])
+
+    def start():
+        for peer in net.peers(first):
+            there = at(**{first: peer[place[first]], second: ALL})
+            net.send(ref.at[(*there, ALL, lanes)], wide.at[peer[0] - 1], got_wide, peer)
+
+    def total(where, slot, here):
+        value = ref[(*where, here, lanes)].astype(F32)
+        for k in range(size[first] - 1):
+            value = value + wide[k, slot, here].astype(F32)
+        return value
+
+    def after_first():
+        await_bytes(wide, got_wide)
+        for peer in net.peers(second):
+            gone = peer[place[second]]
+            there = at(**{second: gone})
+
+            def add(part):
+                here = pl.ds(mul(part, step), step)
+                ref[(*there, here, lanes)] = total(there, gone, here).astype(BF)
+
+            loop(rows // step, add)
+            net.send(ref.at[(*there, ALL, lanes)], line.at[peer[0] - 1], got_line, peer)
+
+    def final(here):
+        value = total(at(), mine[second], here)
+        for k in range(size[second] - 1):
+            value = value + line[k, here].astype(F32)
+        return value
+
+    def finish():
+        await_bytes(line, got_line)
+        emit(final)
+
+    return [start, after_first, finish]
+
+
 def pieces_of(plan, widths):
     counts = {}
     for group, _, _ in plan:
@@ -604,9 +671,9 @@
 
 
 def layer_kernel(
-    tok,
+    tok_in,
     doc,
-    cot,
+    cot_in,
     wq_in,
     wo_in,
     wu_in,
@@ -627,8 +694,11 @@
     wq,
     wo,
     wu,
+    wux,
     wd,
     vbuf,
+    tok,
+    cot,
     pack,
     vecs,
     vq,
@@ -652,10 +722,16 @@
     rcv,
     own,
     snd,
+    own_x,
+    snd_s,
+    rcv_s,
+    snd_x,
+    rcv_x,
     gff,
     gbr,
     dob,
     dsb,
+    gqo,
     gu,
     gd,
     swap,
@@ -669,13 +745,15 @@
     st_q,
     st_o,
     st_u,
+    st_ux,
+    r_ux,
     st_d,
     sems,
     local_sems,
 ):
     net = Net(sems)
     core = net.core
-    me = (net.z, net.y, net.x)
+    greeted = net.greet()
 
     locals_ = []
 
@@ -693,12 +771,20 @@
             wq.at[net.z, net.y, net.x, :, pl.ds(part * OWN, OWN)],
         )
     fetch(wo_in.at[:, lanes_of(core * OWN, OWN)], wo.at[core, net.z, net.y, net.x])
-    for i in range(NZ * 4):
+    for zy in range(8):
         fetch(
-            wu_in.at[:, lanes_of(i * 256 + core * 128, 128)],
-            wu.at[net.z, net.y, net.x, :, pl.ds(i * 128, 128)],
+            wu_in.at[:, lanes_of((zy * 2 + 1 - net.x) * 256 + core * 128, 128)],
+            wux.at[:, pl.ds(zy * 128, 128)],
         )
-    fetch(wd_in.at[pl.ds(mul(core, 128), 128), :], wd.at[net.z, net.y, net.x])
+    own_half = pl.ds(mul(net.x, 64), 64)
+    for zy in range(8):
+        fetch(
+            wu_in.at[:, lanes_of((zy * 2 + net.x) * 256 + core * 128, 128)],
+            wu.at[net.z, net.y, own_half, pl.ds(zy * 128, 128)],
+        )
+    fetch(wd_in.at[pl.ds(mul(core, 128), 128), :], wd.at[net.z, net.y])
+    fetch(tok_in, tok)
+    fetch(cot_in, cot)
     pack[...] = jnp.zeros_like(pack)
     pack[0:1, :] = qv_in[...].astype(F32)
     pack[1:3, :] = up_in[...].astype(F32)
@@ -714,22 +800,48 @@
         pack[rows, 64:128] = jnp.where(net.x == 1, value, 0.0)
     vbuf[net.z, net.y, net.x] = pack[...].astype(BF)
     wo_own = wo.at[core]
-    plan = pieces_of(GATHER, {"v": 128, "q": 3 * OWN, "o": OWN, "u": HID, "d": WIDTH})
-    sources = {"v": vbuf, "q": wq, "o": wo_own, "u": wu, "d": wd}
+    plan = pieces_of(GATHER, WIDTHS)
+    sources = {"v": vbuf, "q": wq, "o": wo_own}
+
+    def stages_of(group, lanes, order):
+        if group == "d":
+            return plane_gather_stages(net, wd, lanes, order)
+        if group == "u":
+            passing = plane_gather_stages(net, wu, lanes, order)
+            got_x = net.sem()
+
+            def cross():
+                net.send(
+                    wux.at[:, lanes],
+                    wu.at[net.z, net.y, own_half, lanes],
+                    got_x,
+                    net.peers("x")[0],
+                )
+
+            def crossed():
+                await_bytes(wux.at[:, lanes], got_x)
+                passing[0]()
+
+            return [cross, crossed, *passing[1:]]
+        return gather_stages(net, sources[group], lanes, order)
+
     gathers = [
-        gather_stages(net, sources[group], pl.ds(lane0, count), order)
-        for group, lane0, count, order in plan
+        stages_of(group, pl.ds(lane0, count), order) for group, lane0, count, order in plan
     ]
-    net.barrier()
-    ready = {"v": 0, "q": 3, "o": 4, "u": 20, "d": 21}
+    greeted()
+    ready = {("q", 0): 3, ("o", 0): 4, ("u", 0): 12, ("u", 1): 20, ("d", 0): 21}
     state = {"landed": 0}
+    got_wo = []
 
     def gather(piece, stage):
-        if stage == 0:
-            while state["landed"] < ready[plan[piece][0]]:
-                locals_[state["landed"]].wait()
-                state["landed"] += 1
+        while state["landed"] < ready.get((plan[piece][0], stage), 0):
+            locals_[state["landed"]].wait()
+            state["landed"] += 1
         gathers[piece][stage]()
+        group, lane0, count, _ = plan[piece]
+        if group == "o" and stage == 3:
+            half = wo_own.at[:, :, :, :, pl.ds(lane0, count)]
+            got_wo.append(net.sibling(half, half))
 
     def spread_vectors():
         for z in range(NZ):
@@ -741,11 +853,12 @@
                 at = pl.ds((y * 2 + x) * 128, 128)
                 vq[0:8, at] = vbuf[core, y, x].astype(F32)[0:8]
                 vq[8:16, at] = vbuf[core + 2, y, x].astype(F32)[0:8]
-                for z in range(NZ):
-                    block = vbuf[z, y, x].astype(F32)
-                    vu[0:1, pl.ds((z * 4 + y * 2 + x) * 128, 128)] = jnp.where(
-                        core == 0, block[1:2], block[2:3]
-                    )
+        for z in range(NZ):
+            for y in range(2):
+                block = vbuf[z, y, net.x].astype(F32)
+                vu[0:1, pl.ds((z * 2 + y) * 128, 128)] = jnp.where(
+                    core == 0, block[1:2], block[2:3]
+                )
         acc[...] = jnp.zeros_like(acc)
         acc_up[...] = jnp.zeros_like(acc_up)
 
@@ -770,6 +883,7 @@
         xin[core, here, :] = (hat * gain(0) + shift(0)).astype(BF)
 
     def attention_input():
+        locals_[21].wait()
         loop(chunks, ln0)
         got["x"] = net.sibling(xin.at[core], xin.at[core])
 
@@ -846,6 +960,9 @@
         attend(3)
         got["att"] = net.sibling(attb.at[other_rows, :], attx)
 
+    own_group = net.x * 2 + core
+    across_group = (1 - net.x) * 2 + core
+
     def branch_tile(n):
         lanes = pl.ds(mul(n % 2, 256), 256)
         mine = wo[n // 2, pl.ds(2 * core, 2), :, :, :, lanes].reshape(OWN, 256)
@@ -854,10 +971,10 @@
         own[:, at] = dot_nn(attb[own_rows, :], mine) + dot_nn(attx[...], theirs)
 
     def branch_all():
-        got["wo"] = net.sibling(wo_own, wo.at[core])
         got["att"].wait_recv()
         loop(2, lambda i: branch_tile(core * 2 + i))
-        got["wo"].wait_recv()
+        for part in got_wo:
+            part.wait_recv()
         loop(2, lambda i: branch_tile((1 - core) * 2 + i))
 
     def ln12(i):
@@ -870,21 +987,81 @@
         second, second_inv = normalize(middle)
         hat2[here, :] = second
         inv2[here, :] = jnp.broadcast_to(second_inv, (chunk, 128))
-        fin[core, here, :] = (second * gain(2) + shift(2)).astype(BF)
+        fin[own_group, here, :] = (second * gain(2) + shift(2)).astype(BF)
+
+    class Share:
+        def __init__(self, ref):
+            self.ref = ref
+            self.beside, self.across, self.passed = [], [], []
+
+        def send(self, half):
+            rows = pl.ds(half * 128, 128)
+            view = self.ref.at[own_group, rows]
+            self.beside.append(net.sibling(view, view))
+            self.across.append(net.send(view, view, net.sem(), net.peers("x")[0]))
+
+        def pass_on(self, half):
+            self.across[half].wait_recv()
+            view = self.ref.at[across_group, pl.ds(half * 128, 128)]
+            self.passed.append(net.sibling(view, view))
+
+        def wait(self, copies):
+            for copy in copies:
+                copy.wait_recv()
+
+    class Reduce:
+        def __init__(self, product):
+            self.product = product
+            self.beside, self.across = [], []
+
+        def group_rows(self, group):
+            return pl.ds(mul(group, LEN), LEN)
+
+        def multiply(self, n):
+            at = pl.ds(n * 256, 256)
+            for xg in range(2):
+                value = self.product(self.group_rows(xg * 2 + 1 - core), n)
+                snd_s[xg, :, at] = value.astype(BF)
+            self.beside.append(net.sibling(snd_s.at[:, :, at], rcv_s.at[:, :, at]))
+            own_x[:, at] = self.product(self.group_rows(across_group), n)
+            own[:, at] = self.product(self.group_rows(own_group), n)
+
+        def cross(self, n):
+            at = pl.ds(n * 256, 256)
+            self.beside[n].wait_recv()
+
+            def add(i):
+                here = pl.ds(mul(i, 64), 64)
+                over = own_x[here, at] + rcv_s[1 - net.x, here, at].astype(F32)
+                snd_x[here, at] = over.astype(BF)
+                own[here, at] += rcv_s[net.x, here, at].astype(F32)
+
+            loop(4, add)
+            self.across.append(
+                net.send(snd_x.at[:, at], rcv_x.at[:, at], net.sem(), net.peers("x")[0])
+            )
+
+        def wait(self):
+            for copy in self.across:
+                copy.wait_recv()
+
+        def free(self):
+            for copy in self.beside + self.across:
+                copy.wait_send()
+
+    share_fin, share_gff = Share(fin), Share(gff)
 
     def norms_12():
-        loop(chunks, ln12)
-        got["fin"] = net.sibling(fin.at[core], fin.at[core])
+        for half in range(2):
+            loop(chunks // 2, lambda i: ln12(i + half * (chunks // 2)))
+            share_fin.send(half)
 
     root = math.sqrt(2.0 / math.pi)
 
-    def up_tile(t):
-        n = t // 2
-        m = t % 2
+    def up_tile(n, group):
         at = pl.ds(mul(n, 256), 256)
-        rows = pl.ds(mul(m, 256), 256)
-        weight = wu[:, :, :, :, at].reshape(WIDTH, 256)
-        u = dot_nn(fin[m], weight) + vu[0:1, at]
+        rows = pl.ds(mul(group, LEN), LEN)
+        u = dot_nn(fin[group], wu[:, :, :, at].reshape(WIDTH, 256)) + vu[0:1, at]
         square = u * u
         inner = jnp.tanh(root * (u + 0.044715 * (square * u)))
         half = 0.5 * (1.0 + inner)
@@ -892,18 +1069,21 @@
         slope = 0.5 * u * (1.0 - inner * inner) * (root * (1.0 + (3 * 0.044715) * square))
         dge[rows, at] = (half + slope).astype(BF)
 
-    def up_piece(lane0, count):
-        tiles = 2 * count // 256
-        loop(tiles, lambda i: up_tile(i + 2 * lane0 // 256))
-
-    got_parts = []
-
-    def down_piece(lane0, count):
-        at = pl.ds(lane0, count)
-        weight = wd[:, :, :, :, at].reshape(HID, count)
-        snd[:, at] = dot_nn(act[other_rows, :], weight)
-        got_parts.append(net.sibling(snd.at[:, at], rcv.at[:, at]))
-        own[:, at] = dot_nn(act[own_rows, :], weight)
+    def up_group(group):
+        loop(4, lambda n: up_tile(n, group))
+
+    def up_beside():
+        share_fin.wait(share_fin.beside)
+        up_group(net.x * 2 + 1 - core)
+
+    def up_last():
+        share_fin.wait(share_fin.passed)
+        up_group((1 - net.x) * 2 + 1 - core)
+
+    def down_product(rows, n):
+        return dot_nn(act[rows, :], wd[:, :, :, pl.ds(n * 256, 256)].reshape(FF4, 256))
+
+    down = Reduce(down_product)
 
     def tiles_of(width, count, body):
         return [functools.partial(body, lane0, count) for lane0 in range(0, width, count)]
@@ -918,47 +1098,61 @@
         attend_last,
         branch_all,
         norms_12,
-        lambda: got["fin"].wait_recv(),
+        lambda: share_fin.pass_on(0),
+        lambda: share_fin.pass_on(1),
     ]
-    steps += tiles_of(HID, 256, up_piece) + tiles_of(WIDTH, 256, down_piece)
+    steps += [
+        lambda: up_group(own_group),
+        up_beside,
+        lambda: up_group(across_group),
+        up_last,
+        functools.partial(down.multiply, 0),
+        functools.partial(down.multiply, 1),
+        functools.partial(down.cross, 0),
+        functools.partial(down.multiply, 2),
+        functools.partial(down.cross, 1),
+        functools.partial(down.multiply, 3),
+        functools.partial(down.cross, 2),
+        functools.partial(down.cross, 3),
+    ]
+    filled = ends[-1]
+
+    def upstream_of(i):
+        here = pl.ds(mul(i, chunk), chunk)
+        position = core * LEN + i * chunk + lax.broadcasted_iota(jnp.int32, (chunk, 1), 0)
+        return cot[here, :].astype(F32) * (position < filled).astype(F32)
+
+    def top_tile(i):
+        here = pl.ds(mul(i, chunk), chunk)
+        value = own[here, :] + rcv_x[here, :].astype(F32) + vecs[ROW_DOWN : ROW_DOWN + 1, :]
+        hat, inv = normalize(value)
+        res_out[here, :] = (mid[here, :] + hat * gain(3) + shift(3)).astype(BF)
+        upstream = upstream_of(i)
+        grad = norm_back(hat, inv, gain(3), upstream).astype(BF)
+        gff[own_group, here, :] = grad
+        accumulate(ROW_GAIN + 3, upstream * hat)
+        accumulate(ROW_SHIFT + 3, upstream)
+        accumulate(ROW_DOWN, grad.astype(F32))
+
+    def top():
+        locals_[22].wait()
+        down.wait()
+        for half in range(2):
+            loop(chunks // 2, lambda i: top_tile(i + half * (chunks // 2)))
+            share_gff.send(half)
+
+    steps.append(top)
     for piece, stage in GATHER_STEPS:
         if piece < 0:
             steps[stage]()
         else:
             gather(piece, stage)
-    for part in got_parts:
-        part.wait_recv()
-
-    filled = ends[-1]
-
-    def upstream_of(i):
-        here = pl.ds(mul(i, chunk), chunk)
-        position = core * LEN + i * chunk + lax.broadcasted_iota(jnp.int32, (chunk, 1), 0)
-        return cot[here, :].astype(F32) * (position < filled).astype(F32)
-
-    def top_tile(i):
-        here = pl.ds(mul(i, chunk), chunk)
-        value = own[here, :] + rcv[here, :] + vecs[ROW_DOWN : ROW_DOWN + 1, :]
-        hat, inv = normalize(value)
-        res_out[here, :] = (mid[here, :] + hat * gain(3) + shift(3)).astype(BF)
-        upstream = upstream_of(i)
-        grad = norm_back(hat, inv, gain(3), upstream).astype(BF)
-        gff[core, here, :] = grad
-        accumulate(ROW_GAIN + 3, upstream * hat)
-        accumulate(ROW_SHIFT + 3, upstream)
-        accumulate(ROW_DOWN, grad.astype(F32))
-
-    parts = 2
-    got_gff = []
-    for part in range(parts):
-        loop(chunks // parts, lambda i: top_tile(i + part * (chunks // parts)))
-        rows = pl.ds(part * (LEN // parts), LEN // parts)
-        got_gff.append(net.sibling(gff.at[core, rows], gff.at[core, rows]))
+
 
     out_copies = []
 
     def deliver(src, dst):
-        copy = pltpu.make_async_copy(src, dst, local_sems.at[21 + len(out_copies)])
+        copy = pltpu.make_async_copy(src, dst, local_sems.at[23 + len(out_copies)])
         copy.start()
         out_copies.append((copy, net.sibling(src, dst)))
 
@@ -967,11 +1161,12 @@
             at = pl.ds(lane0, count)
             deliver(st_d.at[:, at], gd_out.at[pl.ds(mul(core, 128), 128), at])
         if group == "u":
-            for i in range(lane0 // 128, (lane0 + count) // 128):
-                deliver(
-                    st_u.at[:, pl.ds(i * 128, 128)],
-                    gu_out.at[:, lanes_of(i * 256 + core * 128, 128)],
-                )
+            for part in range(2):
+                for zy in range(lane0 // 128, (lane0 + count) // 128):
+                    deliver(
+                        st_u.at[part, :, pl.ds(zy * 128, 128)],
+                        gu_out.at[:, lanes_of((zy * 2 + part) * 256 + core * 128, 128)],
+                    )
         if group == "o":
             deliver(
                 st_o.at[:, pl.ds(lane0, count)], go_out.at[:, lanes_of(core * OWN + lane0, count)]
@@ -982,9 +1177,9 @@
                 st_q.at[:, pl.ds(lane0, count)], gq_out.at[:, lanes_of(core * OWN + start, count)]
             )
 
-    plan = pieces_of(SCATTER, {"d": WIDTH, "u": HID, "o": OWN, "q": 3 * OWN, "v": 128})
-    sums = {"d": gd, "u": gu, "o": wu, "q": wu, "v": gv}
-    stage_of = {"d": st_d, "u": st_u, "o": st_o, "q": st_q, "v": gvec_out}
+    plan = pieces_of(SCATTER, WIDTHS)
+    sums = {"o": gqo, "q": gqo, "v": gv}
+    stage_of = {"o": st_o, "q": st_q, "v": gvec_out}
 
     def store_to(stage, lane0, count):
         def done(row0, size, total):
@@ -992,75 +1187,110 @@
 
         return done
 
-    scatters = []
-    for (group, lane0, count, order), bufs in zip(plan, piece_bufs, strict=True):
+    def sums_of(group, lane0, count, order, bufs):
+        lanes = pl.ds(lane0, count)
+        if group == "d":
+
+            def keep(total):
+                for part in range(4):
+                    here = pl.ds(part * 32, 32)
+                    st_d[here, lanes] = total(here)
+
+            return plane_scatter_stages(net, gd, lanes, order, bufs, keep)
+        if group == "u":
+            got_x = net.sem()
+
+            def cross(total):
+                for part in range(2):
+                    here = pl.ds(part * 32, 32)
+                    theirs = pl.multiple_of((1 - net.x) * 64 + part * 32, 32)
+                    st_ux[here, lanes] = total(pl.ds(theirs, 32)).astype(BF)
+                net.send(st_ux.at[:, lanes], r_ux.at[:, lanes], got_x, net.peers("x")[0])
+                for part in range(2):
+                    here = pl.ds(part * 32, 32)
+                    mine = pl.multiple_of(net.x * 64 + part * 32, 32)
+                    st_u[net.x, here, lanes] = total(pl.ds(mine, 32))
+
+            def crossed():
+                await_bytes(r_ux.at[:, lanes], got_x)
+                st_u[1 - net.x, :, lanes] = r_ux[:, lanes].astype(F32)
+
+            return [*plane_scatter_stages(net, gu, lanes, order, bufs, cross), crossed]
         base = 3 * OWN if group == "o" else 0
-        scatters.append(
-            scatter_stages(
-                net,
-                sums[group],
-                pl.ds(base + lane0, count),
-                order,
-                bufs,
-                store_to(stage_of[group], lane0, count),
-            )
+        return scatter_stages(
+            net,
+            sums[group],
+            pl.ds(base + lane0, count),
+            order,
+            bufs,
+            store_to(stage_of[group], lane0, count),
         )
+
+    scatters = [
+        sums_of(*piece, bufs) for piece, bufs in zip(plan, piece_bufs, strict=True)
+    ]
 
     def scatter(piece, stage):
         scatters[piece][stage]()
-        if stage == 3:
+        if stage == len(scatters[piece]) - 1:
             ship(*plan[piece][:3])
-
-    for part in got_gff:
-        part.wait_recv()
 
     def gdown_piece(lane0, count):
         at = pl.ds(lane0, count)
 
-        def tile(k):
-            left = act[:, pl.ds(mul(k, 256), 256)]
-            grad = gff[:, :, at].reshape(NPOS, count)
-            gd[k // 2, k % 2, :, :, at] = dot_tn(left, grad).astype(BF).reshape(2, 128, count)
-
-        loop(8, tile)
-
-    def gpre_tile(t):
-        k = t // 2
-        m = t % 2
-        at = pl.ds(mul(k, 256), 256)
-        rows = pl.ds(mul(m, 256), 256)
-        weight = wd[k // 2, k % 2].reshape(256, WIDTH)
-        value = dot_nt(gff[m], weight) * dge[rows, at].astype(F32)
+        def tile(z):
+            left = act[:, pl.ds(mul(z, 256), 256)]
+            grad = gff[:, :, at].reshape(4 * LEN, count)
+            gd[z, :, :, at] = dot_tn(left, grad).astype(BF).reshape(2, 128, count)
+
+        loop(NZ, tile)
+
+    def gpre_tile(group, z):
+        at = pl.ds(mul(z, 256), 256)
+        rows = pl.ds(mul(group, LEN), LEN)
+        weight = wd[z].reshape(256, WIDTH)
+        value = dot_nt(gff[group], weight) * dge[rows, at].astype(F32)
         value = value.astype(BF)
         dge[rows, at] = value
         acc_up[:, at] += jnp.sum(value.astype(F32).reshape(32, 8, 256), axis=0)
 
+    def gpre_group(group):
+        loop(NZ, functools.partial(gpre_tile, group))
+
+    def gpre_beside():
+        share_gff.wait(share_gff.beside)
+        gpre_group(net.x * 2 + 1 - core)
+
+    def gpre_last():
+        share_gff.wait(share_gff.passed)
+        gpre_group((1 - net.x) * 2 + 1 - core)
+
     def gup_piece(lane0, count):
         at = pl.ds(lane0, count)
 
         def tile(z):
-            left = fin[:, :, pl.ds(mul(z, 256), 256)].reshape(NPOS, 256)
-            gu[z, :, :, :, at] = dot_tn(left, dge[:, at]).astype(BF).reshape(2, 2, 64, count)
+            left = fin[:, :, pl.ds(mul(z, 256), 256)].reshape(4 * LEN, 256)
+            gu[z, :, :, at] = dot_tn(left, dge[:, at]).astype(BF).reshape(2, 128, count)
 
         loop(NZ, tile)
 
-    def gfi_tile(rows, dst):
-        def body(z):
-            weight = wu[z].reshape(256, HID)
-            dst[:, pl.ds(mul(z, 256), 256)] = dot_nt(dge[rows, :], weight)
-
-        loop(NZ, body)
+    def grad_ffn_in_product(rows, n):
+        return dot_nt(dge[rows, :], wu[n].reshape(256, FF4))
+
+    gfi = Reduce(grad_ffn_in_product)
 
     def grad_ffn_in():
-        for part in got_parts:
-            part.wait_send()
-        gfi_tile(other_rows, snd)
-        got["gfi"] = net.sibling(snd, rcv)
-        gfi_tile(own_rows, own)
+        down.free()
+        for n in range(4):
+            gfi.multiply(n)
+
+    def grad_ffn_in_cross():
+        for n in range(4):
+            gfi.cross(n)
 
     def middle_tile(i):
         here = pl.ds(mul(i, chunk), chunk)
-        grad_in = own[here, :] + rcv[here, :]
+        grad_in = own[here, :] + rcv_x[here, :].astype(F32)
         second = hat2[here, :]
         accumulate(ROW_GAIN + 2, grad_in * second)
         accumulate(ROW_SHIFT + 2, grad_in)
@@ -1074,13 +1304,11 @@
         accumulate(ROW_OUT, grad.astype(F32))
 
     def grad_middle():
-        got["gfi"].wait_recv()
+        gfi.wait()
         loop(chunks, middle_tile)
-        for copy in forward_sends:
-            copy.wait_send()
         got["gbr"] = net.sibling(gbr.at[core], gbr.at[core])
 
-    go = wu.at[:, :, :, :, pl.ds(3 * OWN, OWN)]
+    go = gqo.at[:, :, :, :, pl.ds(3 * OWN, OWN)]
 
     def gout_tile(k, cols, put):
         left = attb[:, pl.ds(mul(k, 256), 256)]
@@ -1091,7 +1319,7 @@
         swap[k] = value
 
     def put_own(k, value):
-        wu[2 * core + k, :, :, :, pl.ds(3 * OWN, OWN)] = value
+        gqo[2 * core + k, :, :, :, pl.ds(3 * OWN, OWN)] = value
 
 
     def gatt_tile(t):
@@ -1105,10 +1333,9 @@
     def grad_out():
         got["gbr"].wait_recv()
         loop(2, lambda k: gout_tile(k, lanes_of((1 - core) * OWN, OWN), put_swap))
-        got_swap = net.sibling(swap, go.at[pl.ds(2 * core, 2)])
+        got["swap"] = net.sibling(swap, go.at[pl.ds(2 * core, 2)])
         loop(2, lambda k: gout_tile(k, lanes_of(core * OWN, OWN), put_own))
         loop(4, gatt_tile)
-        got_swap.wait_recv()
 
     def attend_back(pair):
         at = pl.ds(mul(pair, 128), 128)
@@ -1156,7 +1383,7 @@
         def tile(z):
             left = xin[:, :, pl.ds(mul(z, 256), 256)].reshape(NPOS, 256)
             value = dot_tn(left, ref[:, lane0 % OWN : lane0 % OWN + count]).astype(BF)
-            wu[z, :, :, :, pl.ds(lane0, count)] = value.reshape(2, 2, 64, count)
+            gqo[z, :, :, :, pl.ds(lane0, count)] = value.reshape(2, 2, 64, count)
 
         loop(NZ, tile)
 
@@ -1172,7 +1399,6 @@
         loop(NZ, body)
 
     def grad_attn_in():
-        got["gfi"].wait_send()
         gai_tile(other_rows, snd)
         got["gai"] = net.sibling(snd, rcv)
         gai_tile(own_rows, own)
@@ -1199,25 +1425,31 @@
                     kind = 0 if z < 2 else 1
                     qv_row = jnp.sum(acc_qv[kind, :, at], axis=0, keepdims=True)
                     qv_row = jnp.where(core == z % 2, qv_row, 0.0)
-                    up_at = pl.ds((z * 4 + y * 2 + x) * 128, 128)
+                    up_at = pl.ds((z * 2 + y) * 128, 128)
                     up_row = jnp.sum(acc_up[:, up_at], axis=0, keepdims=True)
+                    up_row = jnp.where(net.x == x, up_row, 0.0)
                     value = base + jnp.where(row_id == 0, qv_row, 0.0)
                     gv[z, y, x] = value + jnp.where(row_id == 1 + core, up_row, 0.0)
 
-    steps = tiles_of(WIDTH, 512, gdown_piece)
-    steps += [
-        lambda: loop(8, gpre_tile),
-        lambda: loop(8, lambda i: gpre_tile(i + 8)),
+    steps = [
+        lambda: None,
+        lambda: gpre_group(own_group),
+        gpre_beside,
+        lambda: share_gff.pass_on(0),
+        lambda: share_gff.pass_on(1),
+        *tiles_of(WIDTH, 512, gdown_piece),
+        lambda: gpre_group(across_group),
+        gpre_last,
+        *tiles_of(FF4, 512, gup_piece),
+        grad_ffn_in,
+        grad_ffn_in_cross,
+        grad_middle,
+        grad_out,
+        lambda: got["swap"].wait_recv(),
     ]
-    steps += tiles_of(HID, 512, gup_piece)
-    steps += [grad_ffn_in, grad_middle, grad_out]
     steps += [functools.partial(loop, 1, lambda i, pair=p: attend_back(i + pair)) for p in range(4)]
     steps += tiles_of(3 * OWN, 512, gqkv_piece)
     steps += [grad_attn_in, bottom]
-    forward_sends = [
-        copy for copy in net.unsent if not any(copy is part for part in got_parts)
-    ]
-    net.unsent = []
     for piece, stage in SCATTER_STEPS:
         if piece < 0:
             steps[stage]()
@@ -1230,17 +1462,24 @@
     for copy, remote in out_copies:
         copy.wait()
         remote.wait_recv()
-    net.drain((got["gfi"], got_vec))
+    net.drain(net.unsent, (*down.beside, *down.across, got_vec))
 
 
 def scatter_bufs(group, count, order):
-    rows, dtype = {"d": (128, BF), "v": (16, F32)}.get(group, (64, BF))
+    rows, dtype = {"v": (16, F32)}.get(group, (64, BF))
     size = {"z": NZ, "y": 2, "x": 2}
-    left = [size[dim] for dim in "zyx" if dim != order[0]]
+    if group in "du":
+        first, second = order
+        return [
+            pltpu.VMEM((size[first] - 1, size[second], 128, count), BF),
+            pltpu.VMEM((size[second] - 1, 128, count), BF),
+        ]
+    first, second, third = order
+    left = [size[dim] for dim in "zyx" if dim != first]
     return [
-        pltpu.VMEM((size[order[0]] - 1, *left, rows, count), dtype),
-        pltpu.VMEM((size[order[1]] - 1, size[order[2]], rows, count), dtype),
-        pltpu.VMEM((size[order[2]] - 1, rows, count), dtype),
+        pltpu.VMEM((size[first] - 1, *left, rows, count), dtype),
+        pltpu.VMEM((size[second] - 1, size[third], rows, count), dtype),
+        pltpu.VMEM((size[third] - 1, rows, count), dtype),
     ]
 
 
@@ -1295,13 +1534,16 @@
     scratch = [
         pltpu.VMEM((NZ, 2, 2, 64, 3 * OWN), BF),
         pltpu.VMEM((2, NZ, 2, 2, 64, OWN), BF),
-        pltpu.VMEM((NZ, 2, 2, 64, HID), BF),
-        pltpu.VMEM((NZ, 2, 2, 128, WIDTH), BF),
+        pltpu.VMEM((NZ, 2, 128, FF4), BF),
+        pltpu.VMEM((64, FF4), BF),
+        pltpu.VMEM((NZ, 2, 128, WIDTH), BF),
         pltpu.VMEM((NZ, 2, 2, 16, 128), BF),
+        pltpu.VMEM((LEN, WIDTH), BF),
+        pltpu.VMEM((LEN, WIDTH), BF),
         pltpu.VMEM((16, 128), F32),
         pltpu.VMEM((16, WIDTH), F32),
         pltpu.VMEM((16, OWN), F32),
-        pltpu.VMEM((8, HID), F32),
+        pltpu.VMEM((8, FF4), F32),
         pltpu.VMEM((2, LEN, WIDTH), BF),
         pltpu.VMEM((NPOS, OWN), BF),
         pltpu.VMEM((NPOS, OWN), BF),
@@ -1315,37 +1557,43 @@
         pltpu.VMEM((LEN, 128), F32),
         pltpu.VMEM((LEN, 128), F32),
         pltpu.VMEM((LEN, WIDTH), F32),
-        pltpu.VMEM((2, LEN, WIDTH), BF),
-        pltpu.VMEM((NPOS, HID), BF),
-        pltpu.VMEM((NPOS, HID), BF),
+        pltpu.VMEM((4, LEN, WIDTH), BF),
+        pltpu.VMEM((4 * LEN, FF4), BF),
+        pltpu.VMEM((4 * LEN, FF4), BF),
+        pltpu.VMEM((LEN, WIDTH), F32),
         pltpu.VMEM((LEN, WIDTH), F32),
         pltpu.VMEM((LEN, WIDTH), F32),
         pltpu.VMEM((LEN, WIDTH), F32),
         pltpu.VMEM((2, LEN, WIDTH), BF),
         pltpu.VMEM((2, LEN, WIDTH), BF),
+        pltpu.VMEM((LEN, WIDTH), BF),
+        pltpu.VMEM((LEN, WIDTH), BF),
+        pltpu.VMEM((4, LEN, WIDTH), BF),
+        pltpu.VMEM((2, LEN, WIDTH), BF),
         pltpu.VMEM((NPOS, OWN), BF),
         pltpu.VMEM((NPOS, NPOS), BF),
-        pltpu.VMEM((NZ, 2, 2, 64, HID), BF),
-        pltpu.VMEM((NZ, 2, 2, 128, WIDTH), BF),
+        pltpu.VMEM((NZ, 2, 2, 64, 4 * OWN), BF),
+        pltpu.VMEM((NZ, 2, 128, FF4), BF),
+        pltpu.VMEM((NZ, 2, 128, WIDTH), BF),
         pltpu.VMEM((2, 2, 2, 64, OWN), BF),
         pltpu.VMEM((16, 8, WIDTH), F32),
         pltpu.VMEM((2, 8, OWN), F32),
-        pltpu.VMEM((8, HID), F32),
+        pltpu.VMEM((8, FF4), F32),
         pltpu.VMEM((16, WIDTH), F32),
         pltpu.VMEM((NZ, 2, 2, 16, 128), F32),
         pltpu.VMEM((16, 128), F32),
         [
             scatter_bufs(group, count, order)
-            for group, _, count, order in pieces_of(
-                SCATTER, {"d": WIDTH, "u": HID, "o": OWN, "q": 3 * OWN, "v": 128}
-            )
+            for group, _, count, order in pieces_of(SCATTER, WIDTHS)
         ],
         pltpu.VMEM((64, 3 * OWN), F32),
         pltpu.VMEM((64, OWN), F32),
-        pltpu.VMEM((64, HID), F32),
+        pltpu.VMEM((2, 64, FF4), F32),
+        pltpu.VMEM((64, FF4), BF),
+        pltpu.VMEM((64, FF4), BF),
         pltpu.VMEM((128, WIDTH), F32),
-        pltpu.SemaphoreType.DMA((700,)),
-        pltpu.SemaphoreType.DMA((80,)),
+        pltpu.SemaphoreType.DMA((800,)),
+        pltpu.SemaphoreType.DMA((90,)),
     ]
     outs = pl.pallas_call(
         layer_kernel,
@@ -1354,11 +1602,11 @@
             jax.ShapeDtypeStruct((LEN, WIDTH), F32),
             jax.ShapeDtypeStruct((64, 3 * WIDTH), F32),
             jax.ShapeDtypeStruct((64, WIDTH), F32),
-            jax.ShapeDtypeStruct((64, 2 * HID), F32),
+            jax.ShapeDtypeStruct((64, 4 * FF4), F32),
             jax.ShapeDtypeStruct((256, WIDTH), F32),
             jax.ShapeDtypeStruct((16, 128), F32),
         ],
-        in_specs=[vmem, pl.BlockSpec(memory_space=pltpu.SMEM), vmem]
+        in_specs=[anywhere, pl.BlockSpec(memory_space=pltpu.SMEM), anywhere]
         + [anywhere] * 4
         + [vmem] * 6,
         out_specs=[vmem, vmem] + [anywhere] * 4 + [vmem],

time: 254 us -> 228 us (0.90)
  Pallas kernels: 253 us -> 227 us
    pallas_call x1, Pallas kernels: 247 us -> 221 us  [fused(): pl.pallas_call(layer_kernel, out_shape=[jax.ShapeDtypeStruct((LEN, WIDTH)...]
where the time goes in v3:
time: 228 us
  Pallas kernels  227 us (100%)
    pallas_call x1, Pallas kernels, fused(): pl.pallas_call(layer_kernel, out_shape=[jax.ShapeDtypeStruct((LEN, WIDTH)...  221 us
    pallas_call x1, Pallas kernels, fused(): pl.pallas_call(hand_out_kernel, out_shape=[jax.ShapeDtypeStruct(array.sha...  6.15 us

profile of v3, /device:TPU:1, one launch (start us, length us, event | category | flops | bytes accessed | tf_op | source)
XLA Modules:
  0.0 227.5 jit_solution(14069258576119256232)
XLA Ops:
  0.6 220.5 %layer.1 = (bf16[256,1024]{1,0:T(8,128)(2,1)}, f32[256,1024]{1,0:T(8,128)}, f32[64,3072]{1,0:T(8,128)}, f32[64,1024]{1,0:T(8,128)}, f32[64,4096]{1,0:T(8,128)}, /*index=5*/f32[256,1024]{1,0:T(8,128)}, f32[16,128]{1,0:T(8,128)}) custom-call(bf16[256,1024]{1,0:T(8,128)(2,1)} %bitcast.12, s32[1,8]{1,0:T(1,128)} %doc.1, bf16[256,1024]{1,0:T(8,128)(2,1)} %bitcast.13, ...), custom_call_target="tpu_custom_call" | custom-call | tf_op jit(solution)/shard_map/layer/pallas_call | solution.py:1598
  221.2 6.2 %hand_out.1 = (bf16[256,1024]{1,0:T(8,128)(2,1)}, f32[256,1024]{1,0:T(8,128)}, f32[64,3072]{1,0:T(8,128)}, f32[64,1024]{1,0:T(8,128)}, f32[64,4096]{1,0:T(8,128)...) custom-call(bf16[256,1024]{1,0:T(8,128)(2,1)} %get-tuple-element.31., ...), custom_call_target="tpu_custom_call" | custom-call | tf_op jit(solution)/shard_map/hand_out/pallas_call | solution.py:1634

commit v4 on v3

--- a/solution.py
+++ b/solution.py
@@ -339,41 +339,41 @@
 MIB = 1 << 20
 ROW_OUT, ROW_DOWN, ROW_GAIN, ROW_SHIFT = 3, 4, 5, 9
 GATHER = (
-    ("v", 0, "zyx"), ("q", 0, "zxy"), ("q", 1, "zyx"), ("q", 2, "zyx"),
-    ("q", 3, "zyx"), ("u", 0, "zy"), ("o", 0, "zyx"), ("d", 0, "zy"),
-    ("u", 1, "zy"), ("d", 1, "zy"), ("u", 2, "zy"), ("d", 2, "yz"),
-    ("u", 3, "yz"), ("d", 3, "zy"),
+    ("v", 0, "zyx"), ("q", 0, "zxy"), ("q", 1, "zyx"), ("q", 2, "zxy"),
+    ("q", 3, "zyx"), ("o", 0, "zyx"), ("u", 0, "zy"), ("u", 1, "zy"),
+    ("d", 0, "zy"), ("u", 2, "yz"), ("d", 1, "zy"), ("d", 2, "zy"),
+    ("u", 3, "zy"), ("d", 3, "zy"),
 )
 GATHER_STEPS = (
     (0, 0), (1, 0), (0, 1), (2, 0), (0, 2), (1, 1), (3, 0), (0, 3),
     (-1, 0), (-1, 1), (2, 1), (4, 0), (1, 2), (3, 1), (5, 0), (7, 0),
-    (4, 1), (6, 0), (2, 2), (5, 1), (10, 0), (10, 1), (12, 0), (1, 3),
-    (3, 2), (4, 2), (7, 1), (8, 0), (9, 0), (12, 1), (2, 3), (8, 1),
-    (12, 2), (6, 1), (7, 2), (3, 3), (4, 3), (-1, 2), (5, 2), (-1, 3),
-    (-1, 4), (6, 2), (10, 2), (-1, 5), (5, 3), (-1, 6), (9, 1), (11, 0),
-    (8, 2), (6, 3), (10, 3), (-1, 7), (-1, 8), (11, 1), (12, 3), (13, 0),
-    (9, 2), (8, 3), (-1, 11), (-1, 12), (-1, 9), (-1, 10), (-1, 13), (13, 1),
-    (-1, 14), (-1, 15), (-1, 16), (11, 2), (-1, 17), (-1, 18), (-1, 19), (13, 2),
+    (4, 1), (6, 0), (2, 2), (7, 1), (8, 0), (6, 1), (5, 1), (9, 0),
+    (3, 2), (1, 3), (9, 1), (12, 0), (4, 2), (2, 3), (12, 1), (9, 2),
+    (7, 2), (8, 1), (10, 0), (11, 0), (3, 3), (5, 2), (6, 2), (4, 3),
+    (-1, 2), (-1, 3), (-1, 4), (5, 3), (-1, 5), (-1, 7), (-1, 6), (6, 3),
+    (7, 3), (8, 2), (12, 2), (-1, 8), (10, 1), (13, 0), (11, 1), (-1, 9),
+    (12, 3), (9, 3), (-1, 10), (-1, 11), (-1, 12), (13, 1), (-1, 13), (-1, 14),
+    (-1, 15), (10, 2), (-1, 16), (11, 2), (-1, 17), (-1, 18), (-1, 19), (13, 2),
     (-1, 20), (-1, 21), (-1, 22), (-1, 23),
 )
 SCATTER = (
-    ("d", 0, "zy"), ("d", 1, "yz"), ("o", 0, "xyz"), ("u", 0, "zy"),
-    ("u", 1, "yz"), ("d", 2, "yz"), ("q", 0, "yxz"), ("q", 1, "xyz"),
-    ("q", 2, "xyz"), ("u", 2, "yz"), ("q", 3, "xyz"), ("q", 4, "xyz"),
-    ("q", 5, "yxz"), ("d", 3, "yz"), ("u", 3, "yz"), ("v", 0, "xyz"),
+    ("o", 0, "xyz"), ("d", 0, "zy"), ("d", 1, "yz"), ("d", 2, "yz"),
+    ("u", 0, "yz"), ("u", 1, "zy"), ("q", 0, "xyz"), ("d", 3, "yz"),
+    ("q", 1, "xyz"), ("q", 2, "xyz"), ("q", 3, "yxz"), ("u", 2, "yz"),
+    ("q", 4, "yxz"), ("u", 3, "yz"), ("q", 5, "xyz"), ("v", 0, "xyz"),
 )
 SCATTER_STEPS = (
-    (-1, 0), (-1, 1), (-1, 2), (-1, 3), (-1, 4), (-1, 7), (-1, 8), (-1, 11),
-    (-1, 5), (0, 0), (1, 0), (-1, 12), (-1, 6), (5, 0), (-1, 9), (4, 0),
-    (-1, 10), (1, 1), (3, 0), (0, 1), (-1, 13), (5, 1), (13, 0), (-1, 14),
-    (0, 2), (4, 1), (9, 0), (14, 0), (-1, 15), (2, 0), (-1, 16), (-1, 17),
-    (1, 2), (-1, 18), (-1, 19), (-1, 20), (6, 0), (7, 0), (13, 1), (-1, 21),
-    (8, 0), (-1, 22), (-1, 23), (2, 1), (5, 2), (9, 1), (11, 0), (14, 1),
-    (-1, 24), (4, 2), (3, 1), (6, 1), (12, 0), (7, 1), (3, 2), (15, 0),
-    (4, 3), (2, 2), (13, 2), (8, 1), (10, 0), (3, 3), (9, 2), (6, 2),
-    (14, 2), (15, 1), (7, 2), (11, 1), (8, 2), (12, 1), (9, 3), (14, 3),
-    (15, 2), (2, 3), (10, 1), (11, 2), (12, 2), (6, 3), (7, 3), (10, 2),
-    (15, 3), (8, 3), (11, 3), (12, 3), (10, 3),
+    (-1, 0), (-1, 1), (-1, 2), (-1, 25), (-1, 26), (-1, 27), (-1, 3), (-1, 4),
+    (-1, 7), (-1, 8), (-1, 11), (-1, 5), (1, 0), (2, 0), (-1, 12), (-1, 6),
+    (3, 0), (7, 0), (-1, 9), (5, 0), (-1, 10), (2, 1), (4, 0), (-1, 13),
+    (-1, 14), (1, 1), (3, 1), (7, 1), (11, 0), (13, 0), (-1, 15), (0, 0),
+    (-1, 16), (-1, 17), (1, 2), (4, 1), (-1, 18), (-1, 19), (-1, 20), (2, 2),
+    (6, 0), (-1, 21), (9, 0), (10, 0), (-1, 22), (-1, 23), (0, 1), (11, 1),
+    (5, 1), (8, 0), (13, 1), (-1, 24), (15, 0), (3, 2), (10, 1), (5, 2),
+    (7, 2), (6, 1), (0, 2), (4, 2), (15, 1), (9, 1), (5, 3), (12, 0),
+    (14, 0), (6, 2), (15, 2), (4, 3), (10, 2), (11, 2), (8, 1), (13, 2),
+    (9, 2), (15, 3), (11, 3), (14, 1), (12, 1), (13, 3), (8, 2), (6, 3),
+    (10, 3), (14, 2), (0, 3), (12, 2), (9, 3), (8, 3), (14, 3), (12, 3),
 )
 WIDTHS = {"v": 128, "q": 3 * OWN, "o": OWN, "u": FF4, "d": WIDTH}
 
@@ -708,6 +708,7 @@
     kb,
     vb,
     pb,
+    bias,
     att,
     attb,
     attx,
@@ -927,55 +928,62 @@
     lane = lax.broadcasted_iota(jnp.int32, (1, 128), 1)
     block = 128
 
-    def attend(pair):
-        at = pl.ds(mul(pair, 128), 128)
+    def masks():
         for r in range(NPOS // block):
-            rows = pl.ds(r * block, block)
             count = (r + 1) * block
             q_pos = r * block + lax.broadcasted_iota(jnp.int32, (block, 1), 0)
             k_pos = lax.broadcasted_iota(jnp.int32, (1, count), 1)
             allowed = (segment(q_pos) == segment(k_pos)) & (k_pos <= q_pos)
+            bias[r * block : (r + 1) * block, 0:count] = jnp.where(allowed, 0.0, FILLER)
+
+    def attend(half, pair):
+        at = pl.ds(mul(pair, 128), 128)
+        for r in (half, half + 2):
+            rows = pl.ds(r * block, block)
+            count = (r + 1) * block
             q = qb[rows, at]
             k = kb[0:count, at]
             v = vb[0:count, at]
             outs = []
             for head in range(2):
                 mine = (lane < 64) if head == 0 else (lane >= 64)
-                scores = dot_nt(jnp.where(mine, q, jnp.zeros_like(q)), k)
-                scores = jnp.where(allowed, scores, FILLER)
+                scores = dot_nt(jnp.where(mine, q, jnp.zeros_like(q)), k) + bias[rows, 0:count]
                 top = jnp.max(scores, axis=1, keepdims=True)
-                weights = jnp.exp(ALPHA * (scores - top))
-                probs = weights * (1.0 / jnp.sum(weights, axis=1, keepdims=True))
-                probs = probs.astype(BF)
-                pb[pair * 2 + head, rows, 0:count] = probs
-                outs.append(dot_nn(probs, v))
+                weights = jnp.exp2((scores - top) * (ALPHA * math.log2(math.e)))
+                summed = dot_nn(weights.astype(BF), jnp.where(mine, v, jnp.ones_like(v)))
+                turned = pltpu.roll(summed, 64, 1)
+                inverse = 1.0 / jnp.where(mine, turned, summed)
+                wide = jnp.concatenate([inverse] * (r + 1), axis=1)
+                pb[pair * 2 + head, rows, 0:count] = (weights * wide).astype(BF)
+                outs.append(summed * inverse)
             out = jnp.where(lane < 64, outs[0], outs[1])
             att[rows, at] = out
             attb[rows, at] = out.astype(BF)
 
     other_rows = pl.ds(mul(1 - core, LEN), LEN)
     own_rows = pl.ds(mul(core, LEN), LEN)
-
-    def attend_last():
-        attend(3)
-        got["att"] = net.sibling(attb.at[other_rows, :], attx)
+    got_att = []
+
+    def half_rows(of_core, half):
+        return pl.ds(pl.multiple_of(of_core * LEN + half * block, block), block)
+
+    def attend_some(half, pair0):
+        loop(2, lambda i: attend(half, i + pair0))
+        if pair0 == 2:
+            sent = attb.at[half_rows(1 - core, half), :]
+            got_att.append(net.sibling(sent, attx.at[pl.ds(half * block, block), :]))
 
     own_group = net.x * 2 + core
     across_group = (1 - net.x) * 2 + core
 
-    def branch_tile(n):
+    def branch_tile(half, n):
         lanes = pl.ds(mul(n % 2, 256), 256)
         mine = wo[n // 2, pl.ds(2 * core, 2), :, :, :, lanes].reshape(OWN, 256)
         theirs = wo[n // 2, pl.ds(2 * (1 - core), 2), :, :, :, lanes].reshape(OWN, 256)
         at = pl.ds(mul(n, 256), 256)
-        own[:, at] = dot_nn(attb[own_rows, :], mine) + dot_nn(attx[...], theirs)
-
-    def branch_all():
-        got["att"].wait_recv()
-        loop(2, lambda i: branch_tile(core * 2 + i))
-        for part in got_wo:
-            part.wait_recv()
-        loop(2, lambda i: branch_tile((1 - core) * 2 + i))
+        here = pl.ds(half * block, block)
+        value = dot_nn(attb[half_rows(core, half), :], mine)
+        own[here, at] = value + dot_nn(attx[here, :], theirs)
 
     def ln12(i):
         here = pl.ds(mul(i, chunk), chunk)
@@ -1005,9 +1013,14 @@
             view = self.ref.at[across_group, pl.ds(half * 128, 128)]
             self.passed.append(net.sibling(view, view))
 
-        def wait(self, copies):
-            for copy in copies:
+        def wait_beside(self):
+            for copy in self.beside:
                 copy.wait_recv()
+
+        def wait_passed(self):
+            for copy in self.passed:
+                copy.wait_recv()
+            self.passed = []
 
     class Reduce:
         def __init__(self, product):
@@ -1017,14 +1030,22 @@
         def group_rows(self, group):
             return pl.ds(mul(group, LEN), LEN)
 
-        def multiply(self, n):
+        def multiply_here(self, n):
             at = pl.ds(n * 256, 256)
-            for xg in range(2):
-                value = self.product(self.group_rows(xg * 2 + 1 - core), n)
-                snd_s[xg, :, at] = value.astype(BF)
+            value = self.product(self.group_rows(net.x * 2 + 1 - core), n)
+            snd_s[net.x, :, at] = value.astype(BF)
+            own[:, at] = self.product(self.group_rows(own_group), n)
+
+        def multiply_there(self, n):
+            at = pl.ds(n * 256, 256)
+            value = self.product(self.group_rows((1 - net.x) * 2 + 1 - core), n)
+            snd_s[1 - net.x, :, at] = value.astype(BF)
             self.beside.append(net.sibling(snd_s.at[:, :, at], rcv_s.at[:, :, at]))
             own_x[:, at] = self.product(self.group_rows(across_group), n)
-            own[:, at] = self.product(self.group_rows(own_group), n)
+
+        def multiply(self, n):
+            self.multiply_here(n)
+            self.multiply_there(n)
 
         def cross(self, n):
             at = pl.ds(n * 256, 256)
@@ -1051,10 +1072,17 @@
 
     share_fin, share_gff = Share(fin), Share(gff)
 
-    def norms_12():
-        for half in range(2):
-            loop(chunks // 2, lambda i: ln12(i + half * (chunks // 2)))
-            share_fin.send(half)
+    def branch_half(half):
+        got_att[half].wait_recv()
+        if half == 0:
+            loop(2, lambda i: branch_tile(half, core * 2 + i))
+            for part in got_wo:
+                part.wait_recv()
+            loop(2, lambda i: branch_tile(half, (1 - core) * 2 + i))
+        else:
+            loop(4, functools.partial(branch_tile, half))
+        loop(chunks // 2, lambda i: ln12(i + half * (chunks // 2)))
+        share_fin.send(half)
 
     root = math.sqrt(2.0 / math.pi)
 
@@ -1073,11 +1101,11 @@
         loop(4, lambda n: up_tile(n, group))
 
     def up_beside():
-        share_fin.wait(share_fin.beside)
+        share_fin.wait_beside()
         up_group(net.x * 2 + 1 - core)
 
     def up_last():
-        share_fin.wait(share_fin.passed)
+        share_fin.wait_passed()
         up_group((1 - net.x) * 2 + 1 - core)
 
     def down_product(rows, n):
@@ -1088,16 +1116,20 @@
     def tiles_of(width, count, body):
         return [functools.partial(body, lane0, count) for lane0 in range(0, width, count)]
 
+    def attention_input_and_masks():
+        attention_input()
+        masks()
+
     steps = [
         spread_vectors,
-        attention_input,
+        attention_input_and_masks,
         projections,
-        lambda: loop(1, attend),
-        lambda: loop(1, lambda i: attend(i + 1)),
-        lambda: loop(1, lambda i: attend(i + 2)),
-        attend_last,
-        branch_all,
-        norms_12,
+        lambda: attend_some(0, 0),
+        lambda: attend_some(0, 2),
+        lambda: attend_some(1, 0),
+        lambda: attend_some(1, 2),
+        lambda: branch_half(0),
+        lambda: branch_half(1),
         lambda: share_fin.pass_on(0),
         lambda: share_fin.pass_on(1),
     ]
@@ -1235,15 +1267,29 @@
         if stage == len(scatters[piece]) - 1:
             ship(*plan[piece][:3])
 
-    def gdown_piece(lane0, count):
+    def over_rows(chip_x, left, right, out, at, count, add):
+        groups = pl.ds(chip_x * 2, 2)
+
+        def tile(z):
+            a, b = left(groups, pl.ds(mul(z, 256), 256)), right(groups, at)
+            value = dot_tn(a.reshape(NPOS, 256), b.reshape(NPOS, count)).reshape(2, 128, count)
+            if add:
+                value = value + out[z, :, :, at].astype(F32)
+            out[z, :, :, at] = value.astype(BF)
+
+        loop(NZ, tile)
+
+    def rows_of(ref):
+        return lambda groups, at: ref[pl.ds(mul(groups.start, LEN), NPOS), at]
+
+    def groups_of(ref):
+        return lambda groups, at: ref[groups, :, at]
+
+    def gdown_piece(chip_x, add, lane0, count):
         at = pl.ds(lane0, count)
-
-        def tile(z):
-            left = act[:, pl.ds(mul(z, 256), 256)]
-            grad = gff[:, :, at].reshape(4 * LEN, count)
-            gd[z, :, :, at] = dot_tn(left, grad).astype(BF).reshape(2, 128, count)
-
-        loop(NZ, tile)
+        if add:
+            share_gff.wait_passed()
+        over_rows(chip_x, rows_of(act), groups_of(gff), gd, at, count, add)
 
     def gpre_tile(group, z):
         at = pl.ds(mul(z, 256), 256)
@@ -1258,31 +1304,30 @@
         loop(NZ, functools.partial(gpre_tile, group))
 
     def gpre_beside():
-        share_gff.wait(share_gff.beside)
+        share_gff.wait_beside()
         gpre_group(net.x * 2 + 1 - core)
 
     def gpre_last():
-        share_gff.wait(share_gff.passed)
+        share_gff.wait_passed()
         gpre_group((1 - net.x) * 2 + 1 - core)
 
-    def gup_piece(lane0, count):
+    def gup_piece(chip_x, add, lane0, count):
         at = pl.ds(lane0, count)
-
-        def tile(z):
-            left = fin[:, :, pl.ds(mul(z, 256), 256)].reshape(4 * LEN, 256)
-            gu[z, :, :, at] = dot_tn(left, dge[:, at]).astype(BF).reshape(2, 128, count)
-
-        loop(NZ, tile)
+        over_rows(chip_x, groups_of(fin), rows_of(dge), gu, at, count, add)
 
     def grad_ffn_in_product(rows, n):
         return dot_nt(dge[rows, :], wu[n].reshape(256, FF4))
 
     gfi = Reduce(grad_ffn_in_product)
 
-    def grad_ffn_in():
+    def grad_ffn_in_here():
         down.free()
         for n in range(4):
-            gfi.multiply(n)
+            gfi.multiply_here(n)
+
+    def grad_ffn_in_there():
+        for n in range(4):
+            gfi.multiply_there(n)
 
     def grad_ffn_in_cross():
         for n in range(4):
@@ -1351,7 +1396,7 @@
                 delta = jnp.sum(grad.astype(F32) * att[rows, at], axis=1, keepdims=True)
                 probs = pb[pair * 2 + head, rows, 0:count].astype(F32)
                 grad_probs = dot_nt(grad, vb[0:count, at])
-                scores = (ALPHA * probs * (grad_probs - delta)).astype(BF)
+                scores = (probs * (grad_probs - delta)).astype(BF)
                 dsb[rows, 0:count] = scores
                 queries_.append(dot_nn(scores, kb[0:count, at]))
             keys_, values_ = [], []
@@ -1366,7 +1411,8 @@
         for r in range(NPOS // block):
             rows = pl.ds(r * block, block)
             merged = [
-                jnp.where(lane < 64, sums[0][i][r], sums[1][i][r]).astype(BF) for i in range(3)
+                (jnp.where(lane < 64, sums[0][i][r], sums[1][i][r]) * power).astype(BF)
+                for i, power in enumerate((float(ALPHA), float(ALPHA), 1.0))
             ]
             grad_q = merged[0] * jnp.asarray(scale, BF)
             qb[rows, at] = grad_q
@@ -1437,11 +1483,11 @@
         gpre_beside,
         lambda: share_gff.pass_on(0),
         lambda: share_gff.pass_on(1),
-        *tiles_of(WIDTH, 512, gdown_piece),
+        *tiles_of(WIDTH, 512, functools.partial(gdown_piece, 1 - net.x, True)),
         lambda: gpre_group(across_group),
         gpre_last,
-        *tiles_of(FF4, 512, gup_piece),
-        grad_ffn_in,
+        *tiles_of(FF4, 512, functools.partial(gup_piece, 1 - net.x, True)),
+        grad_ffn_in_there,
         grad_ffn_in_cross,
         grad_middle,
         grad_out,
@@ -1450,6 +1496,16 @@
     steps += [functools.partial(loop, 1, lambda i, pair=p: attend_back(i + pair)) for p in range(4)]
     steps += tiles_of(3 * OWN, 512, gqkv_piece)
     steps += [grad_attn_in, bottom]
+
+    def both(piece, width):
+        for step in tiles_of(width, 512, functools.partial(piece, net.x, False)):
+            step()
+
+    steps += [
+        lambda: both(gdown_piece, WIDTH),
+        lambda: both(gup_piece, FF4),
+        grad_ffn_in_here,
+    ]
     for piece, stage in SCATTER_STEPS:
         if piece < 0:
             steps[stage]()
@@ -1483,21 +1539,11 @@
     ]
 
 
-SPLIT = 4
-
-
 def hand_out_kernel(*refs):
     large, vec = refs[:6], refs[6]
-    outs, small, held, sems = refs[7:13], refs[13:19], refs[19:25], refs[25]
-    arrivals, copies = [], []
-    for src, mid, dst in zip(large, held, outs, strict=True):
-        rows = src.shape[0] // SPLIT
-        for part in range(SPLIT):
-            here = pl.ds(part * rows, rows)
-            at = len(arrivals)
-            arrivals.append(pltpu.make_async_copy(src.at[here], mid.at[here], sems.at[0, at]))
-            copies.append(pltpu.make_async_copy(mid.at[here], dst.at[here], sems.at[1, at]))
-            arrivals[-1].start()
+    outs, small = refs[7:13], refs[13:19]
+    for src, dst in zip(large, outs, strict=True):
+        dst[...] = src[...]
     right = lax.axis_index("dp") % 2 == 1
     values = vec[...]
     half = jnp.where(right, values[:, 64:], values[:, :64])
@@ -1507,12 +1553,6 @@
     small[3][...] = half[ROW_DOWN : ROW_DOWN + 1]
     small[4][...] = half[ROW_GAIN : ROW_GAIN + 4]
     small[5][...] = half[ROW_SHIFT : ROW_SHIFT + 4]
-    for arrival, copy in zip(arrivals, copies, strict=True):
-        arrival.wait()
-        copy.start()
-    for copy in copies:
-        copy.wait()
-
 
 def fused(
     tokens,
@@ -1549,6 +1589,7 @@
         pltpu.VMEM((NPOS, OWN), BF),
         pltpu.VMEM((NPOS, OWN), BF),
         pltpu.VMEM((8, NPOS, NPOS), BF),
+        pltpu.VMEM((NPOS, NPOS), F32),
         pltpu.VMEM((NPOS, OWN), F32),
         pltpu.VMEM((NPOS, OWN), BF),
         pltpu.VMEM((LEN, OWN), BF),
@@ -1642,10 +1683,9 @@
             jax.ShapeDtypeStruct((4, 64), F32),
             jax.ShapeDtypeStruct((4, 64), F32),
         ],
-        in_specs=[anywhere] * 6 + [vmem],
-        out_specs=[anywhere] * 6 + [vmem] * 6,
-        scratch_shapes=[pltpu.VMEM(array.shape, array.dtype) for array in large]
-        + [pltpu.SemaphoreType.DMA((2, 6 * SPLIT))],
+        in_specs=[vmem] * 7,
+        out_specs=[vmem] * 12,
+        compiler_params=pltpu.CompilerParams(vmem_limit_bytes=63 * MIB),
         name="hand_out",
     )(*large, vec)
     result, grad_inputs, grad_qkv, grad_out, grad_up, grad_down = done[:6]

time: 228 us -> 219 us (0.961)
  Pallas kernels: 227 us -> 218 us
    pallas_call x1, Pallas kernels: 221 us -> 213 us  [fused(): pl.pallas_call(layer_kernel, out_shape=[jax.ShapeDtypeStruct((LEN, WIDTH)...]
where the time goes in v4:
time: 219 us
  Pallas kernels  218 us (100%)
    pallas_call x1, Pallas kernels, fused(): pl.pallas_call(layer_kernel, out_shape=[jax.ShapeDtypeStruct((LEN, WIDTH)...  213 us
    pallas_call x1, Pallas kernels, fused(): pl.pallas_call(hand_out_kernel, out_shape=[jax.ShapeDtypeStruct(array.sha...  4.62 us

profile of v4, /device:TPU:1, one launch (start us, length us, event | category | flops | bytes accessed | tf_op | source)
XLA Modules:
  0.0 218.9 jit_solution(1715363056881071611)
XLA Ops:
  0.6 213.5 %layer.1 = (bf16[256,1024]{1,0:T(8,128)(2,1)}, f32[256,1024]{1,0:T(8,128)}, f32[64,3072]{1,0:T(8,128)}, f32[64,1024]{1,0:T(8,128)}, f32[64,4096]{1,0:T(8,128)}, /*index=5*/f32[256,1024]{1,0:T(8,128)}, f32[16,128]{1,0:T(8,128)}) custom-call(bf16[256,1024]{1,0:T(8,128)(2,1)} %bitcast.12, s32[1,8]{1,0:T(1,128)} %doc.1, bf16[256,1024]{1,0:T(8,128)(2,1)} %bitcast.13, ...), custom_call_target="tpu_custom_call" | custom-call | tf_op jit(solution)/shard_map/layer/pallas_call | solution.py:1639
  214.1 4.6 %hand_out.1 = (bf16[256,1024]{1,0:T(8,128)(2,1)}, f32[256,1024]{1,0:T(8,128)}, f32[64,3072]{1,0:T(8,128)}, f32[64,1024]{1,0:T(8,128)}, f32[64,4096]{1,0:T(8,128)...) custom-call(bf16[256,1024]{1,0:T(8,128)(2,1)} %get-tuple-element.31., ...), custom_call_target="tpu_custom_call" | custom-call | tf_op jit(solution)/shard_map/hand_out/pallas_call | solution.py:1675

commit v5 on v4

--- a/solution.py
+++ b/solution.py
@@ -357,23 +357,25 @@
     (-1, 20), (-1, 21), (-1, 22), (-1, 23),
 )
 SCATTER = (
-    ("o", 0, "xyz"), ("d", 0, "zy"), ("d", 1, "yz"), ("d", 2, "yz"),
-    ("u", 0, "yz"), ("u", 1, "zy"), ("q", 0, "xyz"), ("d", 3, "yz"),
-    ("q", 1, "xyz"), ("q", 2, "xyz"), ("q", 3, "yxz"), ("u", 2, "yz"),
-    ("q", 4, "yxz"), ("u", 3, "yz"), ("q", 5, "xyz"), ("v", 0, "xyz"),
+    ("q", 0, "xyz"), ("d", 0, "zy"), ("o", 0, "xyz"), ("d", 1, "yz"),
+    ("u", 0, "yz"), ("d", 2, "zy"), ("u", 1, "yz"), ("o", 1, "xyz"),
+    ("q", 1, "yxz"), ("q", 2, "yxz"), ("u", 2, "yz"), ("q", 3, "xyz"),
+    ("d", 3, "yz"), ("q", 4, "xyz"), ("q", 5, "xyz"), ("u", 3, "yz"),
+    ("v", 0, "xyz"),
 )
 SCATTER_STEPS = (
     (-1, 0), (-1, 1), (-1, 2), (-1, 25), (-1, 26), (-1, 27), (-1, 3), (-1, 4),
-    (-1, 7), (-1, 8), (-1, 11), (-1, 5), (1, 0), (2, 0), (-1, 12), (-1, 6),
-    (3, 0), (7, 0), (-1, 9), (5, 0), (-1, 10), (2, 1), (4, 0), (-1, 13),
-    (-1, 14), (1, 1), (3, 1), (7, 1), (11, 0), (13, 0), (-1, 15), (0, 0),
-    (-1, 16), (-1, 17), (1, 2), (4, 1), (-1, 18), (-1, 19), (-1, 20), (2, 2),
-    (6, 0), (-1, 21), (9, 0), (10, 0), (-1, 22), (-1, 23), (0, 1), (11, 1),
-    (5, 1), (8, 0), (13, 1), (-1, 24), (15, 0), (3, 2), (10, 1), (5, 2),
-    (7, 2), (6, 1), (0, 2), (4, 2), (15, 1), (9, 1), (5, 3), (12, 0),
-    (14, 0), (6, 2), (15, 2), (4, 3), (10, 2), (11, 2), (8, 1), (13, 2),
-    (9, 2), (15, 3), (11, 3), (14, 1), (12, 1), (13, 3), (8, 2), (6, 3),
-    (10, 3), (14, 2), (0, 3), (12, 2), (9, 3), (8, 3), (14, 3), (12, 3),
+    (-1, 7), (-1, 8), (-1, 11), (-1, 5), (1, 0), (3, 0), (-1, 12), (-1, 6),
+    (5, 0), (-1, 9), (4, 0), (-1, 10), (3, 1), (6, 0), (-1, 13), (4, 1),
+    (12, 0), (-1, 14), (6, 1), (10, 0), (15, 0), (-1, 15), (2, 0), (7, 0),
+    (-1, 16), (-1, 17), (-1, 18), (1, 1), (12, 1), (-1, 19), (3, 2), (-1, 20),
+    (0, 0), (-1, 21), (9, 0), (11, 0), (-1, 22), (1, 2), (2, 1), (7, 1),
+    (10, 1), (14, 0), (15, 1), (-1, 23), (4, 2), (5, 1), (8, 0), (-1, 24),
+    (6, 2), (2, 2), (4, 3), (0, 1), (7, 2), (9, 1), (5, 2), (6, 3),
+    (11, 1), (12, 2), (13, 0), (14, 1), (9, 2), (0, 2), (8, 1), (16, 0),
+    (10, 2), (2, 3), (11, 2), (7, 3), (13, 1), (14, 2), (15, 2), (16, 1),
+    (10, 3), (8, 2), (9, 3), (15, 3), (0, 3), (13, 2), (16, 2), (11, 3),
+    (14, 3), (16, 3), (8, 3), (13, 3),
 )
 WIDTHS = {"v": 128, "q": 3 * OWN, "o": OWN, "u": FF4, "d": WIDTH}
 
@@ -743,6 +745,8 @@
     gv,
     vother,
     piece_bufs,
+    res,
+    gtok,
     st_q,
     st_o,
     st_u,
@@ -1071,6 +1075,11 @@
                 copy.wait_send()
 
     share_fin, share_gff = Share(fin), Share(gff)
+    row_copies = []
+
+    def copy_out(src, dst):
+        row_copies.append(pltpu.make_async_copy(src, dst, local_sems.at[23 + len(row_copies)]))
+        row_copies[-1].start()
 
     def branch_half(half):
         got_att[half].wait_recv()
@@ -1158,7 +1167,7 @@
         here = pl.ds(mul(i, chunk), chunk)
         value = own[here, :] + rcv_x[here, :].astype(F32) + vecs[ROW_DOWN : ROW_DOWN + 1, :]
         hat, inv = normalize(value)
-        res_out[here, :] = (mid[here, :] + hat * gain(3) + shift(3)).astype(BF)
+        res[here, :] = (mid[here, :] + hat * gain(3) + shift(3)).astype(BF)
         upstream = upstream_of(i)
         grad = norm_back(hat, inv, gain(3), upstream).astype(BF)
         gff[own_group, here, :] = grad
@@ -1172,6 +1181,7 @@
         for half in range(2):
             loop(chunks // 2, lambda i: top_tile(i + half * (chunks // 2)))
             share_gff.send(half)
+        copy_out(res, res_out)
 
     steps.append(top)
     for piece, stage in GATHER_STEPS:
@@ -1184,7 +1194,7 @@
     out_copies = []
 
     def deliver(src, dst):
-        copy = pltpu.make_async_copy(src, dst, local_sems.at[23 + len(out_copies)])
+        copy = pltpu.make_async_copy(src, dst, local_sems.at[25 + len(out_copies)])
         copy.start()
         out_copies.append((copy, net.sibling(src, dst)))
 
@@ -1455,11 +1465,12 @@
         grad_in = own[here, :] + rcv[here, :]
         accumulate(ROW_GAIN, grad_in * hat)
         accumulate(ROW_SHIFT, grad_in)
-        gtok_out[here, :] = mid[here, :] + norm_back(hat, inv, gain(0), grad_in)
+        gtok[here, :] = mid[here, :] + norm_back(hat, inv, gain(0), grad_in)
 
     def bottom():
         got["gai"].wait_recv()
         loop(chunks, bottom_tile)
+        copy_out(gtok, gtok_out)
         for row in range(16):
             gvecs[row : row + 1, :] = jnp.sum(acc[row], axis=0, keepdims=True)
         row_id = lax.broadcasted_iota(jnp.int32, (16, 1), 0)
@@ -1515,6 +1526,8 @@
     got_vec.wait_send()
     got_vec.wait_recv()
     gvec_out[...] = gvec_out[...] + vother[...]
+    for copy in row_copies:
+        copy.wait()
     for copy, remote in out_copies:
         copy.wait()
         remote.wait_recv()
@@ -1627,6 +1640,8 @@
             scatter_bufs(group, count, order)
             for group, _, count, order in pieces_of(SCATTER, WIDTHS)
         ],
+        pltpu.VMEM((LEN, WIDTH), BF),
+        pltpu.VMEM((LEN, WIDTH), F32),
         pltpu.VMEM((64, 3 * OWN), F32),
         pltpu.VMEM((64, OWN), F32),
         pltpu.VMEM((2, 64, FF4), F32),
@@ -1650,7 +1665,7 @@
         in_specs=[anywhere, pl.BlockSpec(memory_space=pltpu.SMEM), anywhere]
         + [anywhere] * 4
         + [vmem] * 6,
-        out_specs=[vmem, vmem] + [anywhere] * 4 + [vmem],
+        out_specs=[anywhere] * 6 + [vmem],
         scratch_shapes=scratch,
         compiler_params=pltpu.CompilerParams(
             collective_id=0, has_side_effects=True, vmem_limit_bytes=63 * MIB

time: 219 us -> 217 us (level)
  no operation moved by 1% of the time
where the time goes in v5:
time: 217 us
  Pallas kernels  216 us (100%)
    pallas_call x1, Pallas kernels, fused(): pl.pallas_call(layer_kernel, out_shape=[jax.ShapeDtypeStruct((LEN, WIDTH)...  211 us
    pallas_call x1, Pallas kernels, fused(): pl.pallas_call(hand_out_kernel, out_shape=[jax.ShapeDtypeStruct(array.sha...  4.62 us

profile of v5, /device:TPU:1, one launch (start us, length us, event | category | flops | bytes accessed | tf_op | source)
XLA Modules:
  0.0 216.9 jit_solution(2078570863439239619)
XLA Ops:
  0.6 211.5 %layer.1 = (bf16[256,1024]{1,0:T(8,128)(2,1)}, f32[256,1024]{1,0:T(8,128)}, f32[64,3072]{1,0:T(8,128)}, f32[64,1024]{1,0:T(8,128)}, f32[64,4096]{1,0:T(8,128)}, /*index=5*/f32[256,1024]{1,0:T(8,128)}, f32[16,128]{1,0:T(8,128)}) custom-call(bf16[256,1024]{1,0:T(8,128)(2,1)} %bitcast.12, s32[1,8]{1,0:T(1,128)} %doc.1, bf16[256,1024]{1,0:T(8,128)(2,1)} %bitcast.13, ...), custom_call_target="tpu_custom_call" | custom-call | tf_op jit(solution)/shard_map/layer/pallas_call | solution.py:1654
  212.1 4.6 %hand_out.1 = (bf16[256,1024]{1,0:T(8,128)(2,1)}, f32[256,1024]{1,0:T(8,128)}, f32[64,3072]{1,0:T(8,128)}, f32[64,1024]{1,0:T(8,128)}, f32[64,4096]{1,0:T(8,128)...) custom-call(bf16[256,1024]{1,0:T(8,128)(2,1)} %get-tuple-element.31., ...), custom_call_target="tpu_custom_call" | custom-call | tf_op jit(solution)/shard_map/hand_out/pallas_call | solution.py:1690

commit v6 on v5

--- a/solution.py
+++ b/solution.py
@@ -1009,8 +1009,8 @@
         def send(self, half):
             rows = pl.ds(half * 128, 128)
             view = self.ref.at[own_group, rows]
+            self.across.append(net.send(view, view, net.sem(), net.peers("x")[0]))
             self.beside.append(net.sibling(view, view))
-            self.across.append(net.send(view, view, net.sem(), net.peers("x")[0]))
 
         def pass_on(self, half):
             self.across[half].wait_recv()
@@ -1048,8 +1048,13 @@
             own_x[:, at] = self.product(self.group_rows(across_group), n)
 
         def multiply(self, n):
-            self.multiply_here(n)
-            self.multiply_there(n)
+            at = pl.ds(n * 256, 256)
+            for xg in range(2):
+                value = self.product(self.group_rows(xg * 2 + 1 - core), n)
+                snd_s[xg, :, at] = value.astype(BF)
+            self.beside.append(net.sibling(snd_s.at[:, :, at], rcv_s.at[:, :, at]))
+            own_x[:, at] = self.product(self.group_rows(across_group), n)
+            own[:, at] = self.product(self.group_rows(own_group), n)
 
         def cross(self, n):
             at = pl.ds(n * 256, 256)
@@ -1059,12 +1064,16 @@
                 here = pl.ds(mul(i, 64), 64)
                 over = own_x[here, at] + rcv_s[1 - net.x, here, at].astype(F32)
                 snd_x[here, at] = over.astype(BF)
+
+            def keep(i):
+                here = pl.ds(mul(i, 64), 64)
                 own[here, at] += rcv_s[net.x, here, at].astype(F32)
 
             loop(4, add)
             self.across.append(
                 net.send(snd_x.at[:, at], rcv_x.at[:, at], net.sem(), net.peers("x")[0])
             )
+            loop(4, keep)
 
         def wait(self):
             for copy in self.across:

time: 217 us -> 216 us (level)
  no operation moved by 1% of the time
where the time goes in v6:
time: 216 us
  Pallas kernels  215 us (100%)
    pallas_call x1, Pallas kernels, fused(): pl.pallas_call(layer_kernel, out_shape=[jax.ShapeDtypeStruct((LEN, WIDTH)...  211 us
    pallas_call x1, Pallas kernels, fused(): pl.pallas_call(hand_out_kernel, out_shape=[jax.ShapeDtypeStruct(array.sha...  4.62 us

profile of v6, /device:TPU:1, one launch (start us, length us, event | category | flops | bytes accessed | tf_op | source)
XLA Modules:
  0.0 216.3 jit_solution(1171761632025342175)
XLA Ops:
  0.6 210.8 %layer.1 = (bf16[256,1024]{1,0:T(8,128)(2,1)}, f32[256,1024]{1,0:T(8,128)}, f32[64,3072]{1,0:T(8,128)}, f32[64,1024]{1,0:T(8,128)}, f32[64,4096]{1,0:T(8,128)}, /*index=5*/f32[256,1024]{1,0:T(8,128)}, f32[16,128]{1,0:T(8,128)}) custom-call(bf16[256,1024]{1,0:T(8,128)(2,1)} %bitcast.12, s32[1,8]{1,0:T(1,128)} %doc.1, bf16[256,1024]{1,0:T(8,128)(2,1)} %bitcast.13, ...), custom_call_target="tpu_custom_call" | custom-call | tf_op jit(solution)/shard_map/layer/pallas_call | solution.py:1663
  211.5 4.6 %hand_out.1 = (bf16[256,1024]{1,0:T(8,128)(2,1)}, f32[256,1024]{1,0:T(8,128)}, f32[64,3072]{1,0:T(8,128)}, f32[64,1024]{1,0:T(8,128)}, f32[64,4096]{1,0:T(8,128)...) custom-call(bf16[256,1024]{1,0:T(8,128)(2,1)} %get-tuple-element.31., ...), custom_call_target="tpu_custom_call" | custom-call | tf_op jit(solution)/shard_map/hand_out/pallas_call | solution.py:1699
